TPU v7x, 128 devices: a whole 4x4x4 slice. The times are simulated.
128 devices in a mesh: row: 4 (over y_lo, core), col: 32 (over z, x, y_hi).
Axes of the slice: x: 4, y: 4 (y_hi: 2, y_lo: 2; y = y_hi * 2 + y_lo), z: 4, core: 2. Of those that a mesh axis runs over, the one named last changes fastest.
Arguments:
- start_block: float32 [16384, 128], P(('row', 'col')), may hold values from -6 to 6
- tiles: bfloat16 [2048, 128, 128], P(('row', 'col')), may hold values from -0.1875 to 0.1875
- tile_rows: int32 [2048], P(('row', 'col')), may hold values from -1 to 31, as said below
- tile_cols: int32 [2048], P(('row', 'col')), may hold values from -1 to 3, as said below
- bounds: float32 [2], replicated, as said below
Outputs:
- basis: float32 [16384, 128], P(('row', 'col'))
Inputs may be any that keep to these rules, and one draw needn't show every extreme that they name: `tile_rows`: live slots of a device come first; each device has between 4 and 16 live slots and some device has 16; empty slots hold -1. `tile_cols`: -1 exactly in the empty slots of tile_rows. bounds[0] lies in [-1.5, -0.5] and bounds[1] in [0.5, 1.5].
All inputs are finite; a program needn't handle non-finite values.
Results may differ from a plain program's by a relative error of at most 0.0003.
Values sent between devices are 32-bit elements; how exact they have to be, the bound alone decides.
No kernel may reach another device: no remote copies, remote signals or barrier semaphores. Data moves between devices by JAX's collectives and lax.ppermute only.
A program may use at most 64 MiB of HBM per device.

v0:
```python
import math

import jax
import jax.numpy as jnp
from jax import lax
from jax.sharding import PartitionSpec as P

ITERS = 2


def on_device(start_block, tiles, tile_rows, tile_cols, bounds):
    centre = (bounds[0] + bounds[1]) / 2.0
    half = (bounds[1] - bounds[0]) / 2.0
    blk = tiles.shape[1]
    width = start_block.shape[1]
    own_rows = start_block.shape[0]
    own_blocks = own_rows // blk
    row_count = lax.axis_size("row")
    col_count = lax.axis_size("col")
    total_rows = own_rows * row_count * col_count
    col_index = jnp.clip(tile_cols, 0, row_count * own_blocks - 1)
    tiles_wide = tiles.astype(jnp.float32)

    def product(gathered):
        blocks = gathered.reshape(row_count * own_blocks, blk, width)
        chosen = blocks[col_index]
        prods = jnp.einsum("tij,tjk->tik", tiles_wide, chosen, precision=lax.Precision.HIGHEST)
        block_ids = jnp.arange(own_rows * lax.axis_size("col") // blk, dtype=jnp.int32)
        onehot = (tile_rows[None, :] == block_ids[:, None]).astype(jnp.float32)
        placed = jnp.einsum("bt,tik->bik", onehot, prods, precision=lax.Precision.HIGHEST)
        return lax.psum_scatter(
            placed.reshape(own_rows * lax.axis_size("col"), width),
            "col",
            scatter_dimension=0,
            tiled=True,
        )

    def collect(vec):
        return lax.all_gather(vec, "row", axis=0, tiled=True)

    current = start_block
    for step in range(ITERS):
        gathered = collect(current)
        first = (product(gathered) - centre * current) / half
        second = 2.0 * (product(collect(first)) - centre * first) / half - current
        third = 2.0 * (product(collect(second)) - centre * second) / half - first
        local_gram = jnp.dot(
            third.T, third, precision=lax.Precision.HIGHEST, preferred_element_type=jnp.float32
        )
        gram = lax.psum(local_gram, ("row", "col"))
        factor = jnp.linalg.cholesky(gram)
        current = jax.scipy.linalg.solve_triangular(factor, third.T, lower=True).T
    return current * math.sqrt(total_rows)


def solution(mesh):
    return jax.shard_map(
        on_device,
        mesh=mesh,
        in_specs=(
            P(("row", "col"), None),
            P(("row", "col"), None, None),
            P(("row", "col")),
            P(("row", "col")),
            P(),
        ),
        out_specs=P(("row", "col"), None),
        check_vma=False,
    )
```

profile of v0, /device:TPU:1, one launch (start us, length us, event | category | flops | bytes accessed | tf_op | source)
XLA Modules:
  0.0 1524.4 jit_solution(9914895551191620836)
XLA Ops:
  7.3 7.4 all_gather.18
  17.9 1.2 copy.16
  19.2 1.9 copy.17
  24.9 161.6 %reduce-scatter.7.cloned.1.call-done = f32[128,128]{0,1:T(8,128)} async-done(((f32[4096,128]{0,1:T(8,128)}), f32[128,128]{0,1:T(8,128)}) %reduce-scatter.7.cloned.1.call-update) | async-done | bytes 65552 | tf_op jit(solution)/shard_map/reduce_scatter | solution.py:31
  187.4 30.1 %all_gather.19 = f32[512,128]{0,1:T(8,128)S(1)} all-gather(f32[128,128]{0,1:T(8,128)S(1)} %subtract_divide_fusion.1), channel_id=1, replica_groups=mesh['row'=4,'col'=32] {'row'}, dimensions={0}, use_global_device_ids=true | all-gather | bytes 327680 | tf_op jit(solution)/shard_map/all_gather | solution.py:39
  219.8 1.1 fusion.9
  220.9 1.2 copy.20
  222.1 1.9 copy.21
  224.0 157.5 %reduce-scatter.9.cloned.1.call-done = f32[128,128]{0,1:T(8,128)} async-done(((f32[4096,128]{0,1:T(8,128)}), f32[128,128]{0,1:T(8,128)}) %reduce-scatter.9.cloned.1.call-update) | async-done | bytes 65552 | tf_op jit(solution)/shard_map/reduce_scatter | solution.py:31
  382.5 30.9 %all_gather.20 = f32[512,128]{0,1:T(8,128)S(1)} all-gather(f32[128,128]{0,1:T(8,128)S(1)} %divide_subtract_fusion.3), channel_id=1, replica_groups=mesh['row'=4,'col'=32] {'row'}, dimensions={0}, use_global_device_ids=true | all-gather | bytes 327680 | tf_op jit(solution)/shard_map/all_gather | solution.py:39
  415.6 1.1 fusion.7
  416.7 1.2 copy.24
  417.9 1.9 copy.25
  419.8 158.4 %reduce-scatter.11.cloned.1.call-done = f32[128,128]{0,1:T(8,128)} async-done(((f32[4096,128]{0,1:T(8,128)}), f32[128,128]{0,1:T(8,128)}) %reduce-scatter.11.cloned.1.call-update) | async-done | bytes 65552 | tf_op jit(solution)/shard_map/reduce_scatter | solution.py:31
  580.1 160.0 %all-reduce.3.cloned.1.call-done = f32[128,128]{0,1:T(8,128)} async-done(((f32[128,128]{0,1:T(8,128)}), f32[128,128]{0,1:T(8,128)}) %all-reduce.3.cloned.1.call-update) | async-done | bytes 65552 | tf_op jit(solution)/shard_map/psum | solution.py:50
  741.9 11.7 cholesky.44
  754.9 9.8 custom-call.6
  765.0 5.6 all_gather.21
  772.4 1.6 fusion.5
  774.0 3.0 copy.73
  777.0 160.2 %reduce-scatter.13.cloned.1.call-done = f32[128,128]{0,1:T(8,128)} async-done(((f32[4096,128]{0,1:T(8,128)}), f32[128,128]{0,1:T(8,128)}) %reduce-scatter.13.cloned.1.call-update) | async-done | bytes 65552 | tf_op jit(solution)/shard_map/reduce_scatter | solution.py:31
  938.1 30.8 %all_gather.22 = f32[512,128]{0,1:T(8,128)S(1)} all-gather(f32[128,128]{0,1:T(8,128)S(1)} %subtract_divide_fusion), channel_id=1, replica_groups=mesh['row'=4,'col'=32] {'row'}, dimensions={0}, use_global_device_ids=true | all-gather | bytes 327680 | tf_op jit(solution)/shard_map/all_gather | solution.py:39
  970.6 1.6 fusion.3
  972.2 3.0 copy.72
  975.3 158.1 %reduce-scatter.15.cloned.1.call-done = f32[128,128]{0,1:T(8,128)} async-done(((f32[4096,128]{0,1:T(8,128)}), f32[128,128]{0,1:T(8,128)}) %reduce-scatter.15.cloned.1.call-update) | async-done | bytes 65552 | tf_op jit(solution)/shard_map/reduce_scatter | solution.py:31
  1134.2 30.6 %all_gather.23 = f32[512,128]{0,1:T(8,128)S(1)} all-gather(f32[128,128]{0,1:T(8,128)S(1)} %divide_subtract_fusion.1), channel_id=1, replica_groups=mesh['row'=4,'col'=32] {'row'}, dimensions={0}, use_global_device_ids=true | all-gather | bytes 327680 | tf_op jit(solution)/shard_map/all_gather | solution.py:39
  1166.6 1.6 fusion.1
  1168.1 3.0 copy.71
  1171.2 157.9 %reduce-scatter.17.cloned.1.call-done = f32[128,128]{0,1:T(8,128)} async-done(((f32[4096,128]{0,1:T(8,128)}), f32[128,128]{0,1:T(8,128)}) %reduce-scatter.17.cloned.1.call-update) | async-done | bytes 65552 | tf_op jit(solution)/shard_map/reduce_scatter | solution.py:31
  1330.9 160.5 %all-reduce.5.cloned.1.call-done = f32[128,128]{0,1:T(8,128)} async-done(((f32[128,128]{0,1:T(8,128)}), f32[128,128]{0,1:T(8,128)}) %all-reduce.5.cloned.1.call-update) | async-done | bytes 65552 | tf_op jit(solution)/shard_map/psum | solution.py:50
  1493.2 11.7 cholesky.55
  1506.2 9.8 custom-call.7
  (70 shorter events, 29.9 us)
Async XLA Ops:
  6.5 8.7 copy-start
  6.5 180.1 %reduce-scatter.7.cloned.1.call-start = ((), (), s32[]{:S(2)}) async-start(), calls=%async_computation.6 | async-start | bytes 2162688 | tf_op jit(solution)/shard_map/reduce_scatter | solution.py:31
  15.3 1.5 copy-start.2
  21.0 0.7 copy-start.3
  21.0 3.8 copy-start.1
  21.0 360.6 %reduce-scatter.9.cloned.1.call-start = ((), (), s32[]{:S(2)}) async-start(), calls=%async_computation.7 | async-start | bytes 2162688 | tf_op jit(solution)/shard_map/reduce_scatter | solution.py:31
  224.0 354.3 %reduce-scatter.11.cloned.1.call-start = ((), (), s32[]{:S(2)}) async-start(), calls=%async_computation.8 | async-start | bytes 2162688 | tf_op jit(solution)/shard_map/reduce_scatter | solution.py:31
  419.8 320.3 %all-reduce.3.cloned.1.call-start = ((), (), s32[]{:S(2)}) async-start(), calls=%async_computation.9 | async-start | bytes 131072 | tf_op jit(solution)/shard_map/psum | solution.py:50
  580.0 357.2 %reduce-scatter.13.cloned.1.call-start = ((), (), s32[]{:S(2)}) async-start(), calls=%async_computation.10 | async-start | bytes 2162688 | tf_op jit(solution)/shard_map/reduce_scatter | solution.py:31
  777.0 356.3 %reduce-scatter.15.cloned.1.call-start = ((), (), s32[]{:S(2)}) async-start(), calls=%async_computation.11 | async-start | bytes 2162688 | tf_op jit(solution)/shard_map/reduce_scatter | solution.py:31
  975.2 353.9 %reduce-scatter.17.cloned.1.call-start = ((), (), s32[]{:S(2)}) async-start(), calls=%async_computation.12 | async-start | bytes 2162688 | tf_op jit(solution)/shard_map/reduce_scatter | solution.py:31
  1171.1 320.2 %all-reduce.5.cloned.1.call-start = ((), (), s32[]{:S(2)}) async-start(), calls=%async_computation.13 | async-start | bytes 131072 | tf_op jit(solution)/shard_map/psum | solution.py:50
Sparse Core Ops, SparseCore 0:
  21.2 165.3 reduce-scatter.6
  224.1 157.4 reduce-scatter.8
  419.9 158.3 reduce-scatter.10
  583.6 156.4 all-reduce.2
  777.1 160.0 reduce-scatter.12
  975.3 157.9 reduce-scatter.14
  1171.3 157.7 reduce-scatter.16
  1334.5 156.8 all-reduce.4
where the time goes:
time: 1530 us; the launch traced here: 1520 us
  waiting for transfers between devices  1270 us (83%)
  blocking collectives  135 us (9%)
  other arithmetic  53.3 us (3%)
  local copies, waits for them, and re-layouts  27.9 us (2%)
  between operations  16.8 us (1%)
  matrix products  16.4 us (1%)
    reduce_scatter x6, waiting for transfers between devices, product(): lax.psum_scatter(placed.reshape(own_rows * lax.axis_size('col'), width),...  954 us
    psum x2, waiting for transfers between devices, on_device(): gram = lax.psum(local_gram, ('row', 'col'))  321 us
    all_gather x6, blocking collectives, collect(): return lax.all_gather(vec, 'row', axis=0, tiled=True)  135 us
  transfers between devices with their start and end apart: 8, of which 8 were waited for; matrix products, arithmetic and copies ran while one was open for 0% of the time, Pallas kernels for 0%

commit v1 on v0

v1 whole, which is shorter than its diff:
```python
import functools
import math

import jax
import jax.numpy as jnp
from jax import lax
from jax.experimental import pallas as pl
from jax.experimental.pallas import tpu as pltpu
from jax.sharding import Mesh
from jax.sharding import PartitionSpec as P

ITERS = 2
HIGH = lax.Precision.HIGHEST
AXES = ("ylo", "core", "zhi", "zlo", "xhi", "xlo", "yhi")
ROW = ("ylo", "core")
COL = ("zhi", "zlo", "xhi", "xlo", "yhi")
SPLIT = ("xhi", "yhi")
SCATTER = ("zhi", "zlo", "xlo")
NS = 2 ** len(SPLIT)
NM = 2 ** len(SCATTER)


def digits(index, names):
    out = 0
    for name in names:
        shift = len(COL) - 1 - COL.index(name)
        out = out * 2 + ((index >> shift) & 1)
    return out


def swap(x, name):
    return lax.ppermute(x, name, [(0, 1), (1, 0)])


def exchange(x, names):
    if not names:
        return x
    return lax.all_to_all(x, names, 0, 0, tiled=True)


def widen_kernel(t_ref, o_ref):
    o_ref[...] = t_ref[...].astype(jnp.float32)


def widen(tiles):
    return pl.pallas_call(
        widen_kernel,
        out_shape=jax.ShapeDtypeStruct(tiles.shape, jnp.float32),
        name="widen",
    )(tiles)


def pack_kernel(own_ref, *refs):
    o_ref = refs[-1]
    slots = own_ref.shape[0]
    o_ref[0:slots] = own_ref[...]
    at = slots
    for r in refs[:-1]:
        o_ref[at : at + r.shape[0]] = r[...].astype(jnp.bfloat16)
        at += r.shape[0]


def pack(own, parts):
    slots = own.shape[0] + sum(p.shape[0] for p in parts)
    return pl.pallas_call(
        pack_kernel,
        out_shape=jax.ShapeDtypeStruct((slots,) + own.shape[1:], jnp.bfloat16),
        compiler_params=pltpu.CompilerParams(vmem_limit_bytes=32 * 2**20),
        name="pack",
    )(own, *parts)


def share_tiles(tiles, rows, cols):
    half = tiles.shape[0] // 2
    meta = jnp.stack([rows, cols])
    wide = widen(tiles)
    a, b = wide[:half], wide[half:]
    a_y, b_x = swap(a, "yhi"), swap(b, "xhi")
    a_x, b_y = swap(a, "xhi"), swap(b, "yhi")
    a_xy, b_xy = swap(a_y, "xhi"), swap(b_x, "yhi")
    m_y, m_x = swap(meta, "yhi"), swap(meta, "xhi")
    m_xy = swap(m_y, "xhi")
    packed = pack(tiles, [a_y, b_y, a_x, b_x, a_xy, b_xy])
    metas = jnp.stack([meta, m_y, m_x, m_xy])
    return packed, metas[:, 0], metas[:, 1]


def product_kernel(place_ref, source_ref, v_ref, tiles_ref, o_ref, parts):
    blocks, width, blk = v_ref.shape
    v = v_ref[...]
    high = v.astype(jnp.bfloat16)
    rest = v - high.astype(jnp.float32)
    middle = rest.astype(jnp.bfloat16)
    low = (rest - middle.astype(jnp.float32)).astype(jnp.bfloat16)
    parts[0:blocks, 0:width, :] = high
    parts[0:blocks, width : 2 * width, :] = middle
    parts[0:blocks, 2 * width : 3 * width, :] = low
    parts[blocks] = jnp.zeros(parts.shape[1:], jnp.bfloat16)
    o_ref[...] = jnp.zeros_like(o_ref)

    def step(t, _):
        p = lax.dot_general(
            parts[source_ref[t]],
            tiles_ref[t],
            (((1,), (1,)), ((), ())),
            preferred_element_type=jnp.float32,
        )
        o_ref[place_ref[t]] += p[0:width] + p[width : 2 * width] + p[2 * width :]
        return 0

    lax.fori_loop(0, tiles_ref.shape[0], step, 0, unroll=UNROLL)


UNROLL = 16


def product(place, source, v, tiles, out_blocks):
    blocks, width, blk = v.shape
    smem = pl.BlockSpec(memory_space=pltpu.SMEM)
    vmem = pl.BlockSpec(memory_space=pltpu.VMEM)
    return pl.pallas_call(
        product_kernel,
        out_shape=jax.ShapeDtypeStruct((out_blocks, width, blk), jnp.float32),
        in_specs=[smem, smem, vmem, vmem],
        out_specs=vmem,
        scratch_shapes=[pltpu.VMEM((blocks + 1, 3 * width, blk), jnp.bfloat16)],
        compiler_params=pltpu.CompilerParams(vmem_limit_bytes=32 * 2**20),
        name="product",
    )(place, source, v, tiles)


def gram_sum(local):
    k = local.shape[0]
    n = 2 ** len(AXES)
    pieces = lax.all_to_all(local.reshape(n, k * k // n), AXES, 0, 0, tiled=True)
    mine = jnp.sum(pieces, axis=0)
    full = lax.all_to_all(jnp.broadcast_to(mine[None], pieces.shape), AXES, 0, 0, tiled=True)
    return full.reshape(k, k)


def on_device(start_block, tiles, tile_rows, tile_cols, bounds):
    centre = (bounds[0] + bounds[1]) / 2.0
    half = (bounds[1] - bounds[0]) / 2.0
    blk = tiles.shape[1]
    width = start_block.shape[1]
    rows = 4
    total_rows = blk * 2 ** len(AXES)
    own = 0
    for name in SPLIT:
        own = own * 2 + lax.axis_index(name)

    packed, all_rows, all_cols = share_tiles(tiles, tile_rows, tile_cols)
    live = all_rows >= 0
    position = own ^ jnp.arange(NS, dtype=jnp.int32)[:, None]
    source = jnp.where(live, all_cols * NS + position, rows * NS).reshape(-1)
    place = jnp.where(live, digits(all_rows, SCATTER) * NS + digits(all_rows, SPLIT), 0).reshape(-1)

    def apply(v):
        wide = lax.all_gather(v, ROW, axis=0, tiled=True)
        prods = product(place, source, wide, packed, NM * NS)
        got = exchange(prods.reshape(NM, NS, *v.shape[1:]), SCATTER)
        return jnp.sum(got, axis=0)

    def to_split(x):
        return exchange(x.reshape(NS, width // NS, blk), SPLIT)

    def to_whole(x):
        return exchange(x, SPLIT).reshape(width, blk)

    def filtered(current):
        first = (apply(current) - centre * current) / half
        second = 2.0 * (apply(first) - centre * first) / half - current
        return 2.0 * (apply(second) - centre * second) / half - first

    def normal_factor(x):
        local = lax.dot_general(
            x, x, (((1,), (1,)), ((), ())), precision=HIGH, preferred_element_type=jnp.float32
        )
        return jnp.linalg.cholesky(gram_sum(local))

    def solve(factor, x):
        return jax.scipy.linalg.solve_triangular(factor, x, lower=True)

    third = filtered(to_split(start_block.T))
    factor_one = normal_factor(to_whole(third))
    third = solve(factor_one, to_whole(filtered(third)))
    basis = solve(normal_factor(third), third)
    return basis.T * math.sqrt(total_rows)


def solution(mesh):
    fine = Mesh(mesh.devices.reshape((2,) * len(AXES)), AXES)
    return jax.shard_map(
        on_device,
        mesh=fine,
        in_specs=(P(AXES, None), P(AXES, None, None), P(AXES), P(AXES), P()),
        out_specs=P(AXES, None),
        check_vma=False,
    )
```

time: 1530 us -> 294 us (0.19)
  waiting for transfers between devices: 1270 us -> 25.6 us
  starting transfers between devices: 0.29 us -> 69.7 us
  blocking collectives: 135 us -> 109 us
  Pallas kernels: 0 us -> 21.1 us
    reduce_scatter x6 -> x0, waiting for transfers between devices: 954 us -> none  [product(): lax.psum_scatter(placed.reshape(own_rows * lax.axis_size('col'), width),...]
    psum x2 -> x0, waiting for transfers between devices: 321 us -> none  [on_device(): gram = lax.psum(local_gram, ('row', 'col'))]
    all_gather x6, blocking collectives: 135 us -> 50.6 us  [apply(): wide = lax.all_gather(v, ROW, axis=0, tiled=True)]
    all_to_all x0 -> x4, blocking collectives: none -> 58.8 us  [the longest x2 24.7 us: exchange(): return lax.all_to_all(x, names, 0, 0, tiled=True)]
    all_to_all x0 -> x9, starting transfers between devices: none -> 50 us  [the longest x7 34.2 us: exchange(): return lax.all_to_all(x, names, 0, 0, tiled=True)]
    all_to_all x0 -> x9, waiting for transfers between devices: none -> 24.9 us  [the longest x7 24.9 us: exchange(): return lax.all_to_all(x, names, 0, 0, tiled=True)]
    pallas_call x0 -> x8, Pallas kernels: none -> 21.1 us  [the longest x6 17.7 us: product(): pl.pallas_call(product_kernel, out_shape=jax.ShapeDtypeStruct((out_blocks...]
    ppermute x0 -> x9, starting transfers between devices: none -> 19.7 us  [swap(): return lax.ppermute(x, name, [(0, 1), (1, 0)])]
  transfers between devices with their start and end apart: 8 -> 18, of which waited for: 8 -> 5; matrix products, arithmetic and copies ran while one was open for 0% -> 9% of each run, Pallas kernels for 0% -> 3%
where the time goes in v1:
time: 294 us; the launch traced here: 293 us
  blocking collectives  109 us (37%)
  starting transfers between devices  69.7 us (24%)
  other arithmetic  49.4 us (17%)
  waiting for transfers between devices  25.6 us (9%)
  Pallas kernels  21.1 us (7%)
  local copies, waits for them, and re-layouts  13.1 us (4%)
    all_gather x6, blocking collectives, apply(): wide = lax.all_gather(v, ROW, axis=0, tiled=True)  50.6 us
    all_to_all x7, starting transfers between devices, exchange(): return lax.all_to_all(x, names, 0, 0, tiled=True)  34.2 us
    all_to_all x7, waiting for transfers between devices, exchange(): return lax.all_to_all(x, names, 0, 0, tiled=True)  24.9 us
    another operation x6, other arithmetic, normal_factor(): return jnp.linalg.cholesky(gram_sum(local))  24.8 us
    all_to_all x2, blocking collectives, exchange(): return lax.all_to_all(x, names, 0, 0, tiled=True)  24.7 us
    another operation x4, other arithmetic, solve(): return jax.scipy.linalg.solve_triangular(factor, x, lower=True)  20.9 us
    all_to_all x1, blocking collectives, gram_sum(): lax.all_to_all(local.reshape(n, k * k // n), AXES, 0, 0, tiled=True)  20.1 us
    ppermute x9, starting transfers between devices, swap(): return lax.ppermute(x, name, [(0, 1), (1, 0)])  19.7 us
  transfers between devices with their start and end apart: 18, of which 5 were waited for; matrix products, arithmetic and copies ran while one was open for 9% of the time, Pallas kernels for 3%

profile of v1, /device:TPU:1, one launch (start us, length us, event | category | flops | bytes accessed | tf_op | source)
XLA Modules:
  0.0 292.8 jit_solution(17622407383193583924)
XLA Ops:
  4.5 3.7 %collective-permute-start.3 = (f32[8,128,128]{2,1,0:T(8,128)}, f32[8,128,128]{2,1,0:T(8,128)S(1)}, u32[]{:S(2)}, u32[]{:S(2)}) collective-permute-start(f32[8,128,128]{2,1,0:T(8,128)} %get-tuple-element.8), channel_id=1, source_target_pairs={{0,1},{1,0},{2,3},{3,2},{4,5},{5,4},{6,7},{7,6},{8,9},{9,8},{10,11... | collective-permute-start | bytes 1572872 | tf_op jit(solution)/shard_map/ppermute | solution.py:32
  11.4 2.9 collective-permute-start.4
  15.0 4.0 %all-to-all-start = ((f32[4,32,128]{2,1,0:T(8,128)}), f32[4,32,128]{2,1,0:T(8,128)S(1)}, u32[]{:S(2)}, u32[]{:S(2)}) async-start(f32[4,32,128]{2,1,0:T(8,128)} %bitcast.11), calls=%async_computation | async-start | bytes 131072 | tf_op jit(solution)/shard_map/all_to_all | solution.py:38
  31.7 15.2 %all_gather.18.v_ref = f32[16,32,128]{2,1,0:T(8,128)S(1)} all-gather(f32[4,32,128]{2,1,0:T(8,128)S(1)} %all-to-all-done), channel_id=1, replica_groups=mesh['ylo'=2,'core'=2,'zhi'=2,'zlo'=2,'xhi'=2,'xlo'=2,'yhi'=2] {'ylo','c..., dimensions={0}, use_global_device_ids=true | all-gather | bytes 327680 | tf_op jit(solution)/shard_map/all_gather | solution.py:159
  54.8 3.2 %product.6 = f32[32,32,128]{2,1,0:T(8,128)} custom-call(s32[64]{0:T(128)S(1)} %get-tuple-element.14.place_ref, s32[64]{0:T(128)S(1)} %get-tuple-element.13.source_ref, f32[16,32,128]{2,1,0:T(8,128)S(1)} %all_gather.18.v_ref, bf16[64,128,128]{2,1,0:T(8,128)(2,1)S(1)} %pack.1.tiles_ref), custom_call_target="tpu_custom_call" | custom-call | tf_op jit(solution)/shard_map/product/pallas_call | solution.py:121
  58.0 6.0 %all-to-all-start.1 = ((f32[8,4,32,128]{3,2,1,0:T(8,128)}), f32[8,4,32,128]{3,2,1,0:T(8,128)S(1)}, u32[]{:S(2)}, u32[]{:S(2)}) async-start(f32[8,4,32,128]{3,2,1,0:T(8,128)} %bitcast.12), calls=%async_computation.1 | async-start | bytes 1048576 | tf_op jit(solution)/shard_map/all_to_all | solution.py:38
  67.2 5.5 %all-to-all-done.1 = f32[8,4,32,128]{3,2,1,0:T(8,128)S(1)} async-done(((f32[8,4,32,128]{3,2,1,0:T(8,128)}), f32[8,4,32,128]{3,2,1,0:T(8,128)S(1)}, u32[]{:S(2)}, u32[]{:S(2)}) %all-to-all-start.1) | async-done | bytes 524320 | tf_op jit(solution)/shard_map/all_to_all | solution.py:38
  72.8 8.0 %all_gather.19.v_ref = f32[16,32,128]{2,1,0:T(8,128)S(1)} all-gather(f32[4,32,128]{2,1,0:T(8,128)S(1)} %subtract_divide_fusion.1), channel_id=1, replica_groups=mesh['ylo'=2,'core'=2,'zhi'=2,'zlo'=2,'xhi'=2,'xlo'=2,'yhi'=2] {'ylo','c..., dimensions={0}, use_global_device_ids=true | all-gather | bytes 327680 | tf_op jit(solution)/shard_map/all_gather | solution.py:159
  83.1 12.4 %all_to_all.81 = f32[8,4,32,128]{3,2,1,0:T(8,128)S(1)} all-to-all(f32[8,4,32,128]{3,2,1,0:T(8,128)S(1)} %bitcast.74), channel_id=1, replica_groups=mesh['ylo'=2,'core'=2,'zhi'=2,'zlo'=2,'xhi'=2,'xlo'=2,'yhi'=2] {'zhi','z..., dimensions={0} | all-to-all | bytes 1048576 | tf_op jit(solution)/shard_map/all_to_all | solution.py:38
  95.6 6.7 %all_gather.20.v_ref = f32[16,32,128]{2,1,0:T(8,128)S(1)} all-gather(f32[4,32,128]{2,1,0:T(8,128)S(1)} %divide_subtract_fusion.3), channel_id=1, replica_groups=mesh['ylo'=2,'core'=2,'zhi'=2,'zlo'=2,'xhi'=2,'xlo'=2,'yhi'=2] {'ylo','c..., dimensions={0}, use_global_device_ids=true | all-gather | bytes 327680 | tf_op jit(solution)/shard_map/all_gather | solution.py:159
  104.7 12.4 %all_to_all.82 = f32[8,4,32,128]{3,2,1,0:T(8,128)S(1)} all-to-all(f32[8,4,32,128]{3,2,1,0:T(8,128)S(1)} %bitcast.75), channel_id=1, replica_groups=mesh['ylo'=2,'core'=2,'zhi'=2,'zlo'=2,'xhi'=2,'xlo'=2,'yhi'=2] {'zhi','z..., dimensions={0} | all-to-all | bytes 1048576 | tf_op jit(solution)/shard_map/all_to_all | solution.py:38
  117.7 5.0 %all-to-all-start.4 = ((f32[4,32,128]{2,1,0:T(8,128)}), f32[4,32,128]{2,1,0:T(8,128)S(1)}, u32[]{:S(2)}, u32[]{:S(2)}) async-start(f32[4,32,128]{2,1,0:T(8,128)} %divide_subtract_fusion.2), calls=%async_computation.4 | async-start | bytes 131072 | tf_op jit(solution)/shard_map/all_to_all | solution.py:38
  122.7 7.4 %all_gather.21.v_ref = f32[16,32,128]{2,1,0:T(8,128)S(1)} all-gather(f32[4,32,128]{2,1,0:T(8,128)} %divide_subtract_fusion.2), channel_id=1, replica_groups=mesh['ylo'=2,'core'=2,'zhi'=2,'zlo'=2,'xhi'=2,'xlo'=2,'yhi'=2] {'ylo','c..., dimensions={0}, use_global_device_ids=true | all-gather | bytes 327680 | tf_op jit(solution)/shard_map/all_gather | solution.py:159
  130.1 3.2 %product.9 = f32[32,32,128]{2,1,0:T(8,128)} custom-call(s32[64]{0:T(128)S(1)} %get-tuple-element.14.place_ref, s32[64]{0:T(128)S(1)} %get-tuple-element.13.source_ref, f32[16,32,128]{2,1,0:T(8,128)S(1)} %all_gather.21.v_ref, bf16[64,128,128]{2,1,0:T(8,128)(2,1)S(1)} %pack.1.tiles_ref), custom_call_target="tpu_custom_call" | custom-call | tf_op jit(solution)/shard_map/product/pallas_call | solution.py:121
  133.3 3.5 %all-to-all-start.7 = ((f32[8,4,32,128]{3,2,1,0:T(8,128)}), f32[8,4,32,128]{3,2,1,0:T(8,128)S(1)}, u32[]{:S(2)}, u32[]{:S(2)}) async-start(f32[8,4,32,128]{3,2,1,0:T(8,128)} %bitcast.25), calls=%async_computation.7 | async-start | bytes 1048576 | tf_op jit(solution)/shard_map/all_to_all | solution.py:38
  137.7 9.2 %all-to-all-done.7 = f32[8,4,32,128]{3,2,1,0:T(8,128)S(1)} async-done(((f32[8,4,32,128]{3,2,1,0:T(8,128)}), f32[8,4,32,128]{3,2,1,0:T(8,128)S(1)}, u32[]{:S(2)}, u32[]{:S(2)}) %all-to-all-start.7) | async-done | bytes 524320 | tf_op jit(solution)/shard_map/all_to_all | solution.py:38
  146.9 7.8 %all-to-all-start.5 = ((f32[128,1,128]{2,1,0:T(1,128)}), f32[128,1,128]{2,1,0:T(1,128)S(1)}, u32[]{:S(2)}, u32[]{:S(2)}) async-start(f32[128,1,128]{2,1,0:T(1,128)} %bitcast.19), calls=%async_computation.5 | async-start | bytes 131072 | tf_op jit(solution)/shard_map/all_to_all | solution.py:135
  155.6 6.7 %all_gather.22.v_ref = f32[16,32,128]{2,1,0:T(8,128)S(1)} all-gather(f32[4,32,128]{2,1,0:T(8,128)S(1)} %subtract_divide_fusion), channel_id=1, replica_groups=mesh['ylo'=2,'core'=2,'zhi'=2,'zlo'=2,'xhi'=2,'xlo'=2,'yhi'=2] {'ylo','c..., dimensions={0}, use_global_device_ids=true | all-gather | bytes 327680 | tf_op jit(solution)/shard_map/all_gather | solution.py:159
  162.3 3.2 %product.10 = f32[32,32,128]{2,1,0:T(8,128)} custom-call(s32[64]{0:T(128)S(1)} %get-tuple-element.14.place_ref, s32[64]{0:T(128)S(1)} %get-tuple-element.13.source_ref, f32[16,32,128]{2,1,0:T(8,128)S(1)} %all_gather.22.v_ref, bf16[64,128,128]{2,1,0:T(8,128)(2,1)S(1)} %pack.1.tiles_ref), custom_call_target="tpu_custom_call" | custom-call | tf_op jit(solution)/shard_map/product/pallas_call | solution.py:121
  165.6 4.8 %all-to-all-start.8 = ((f32[8,4,32,128]{3,2,1,0:T(8,128)}), f32[8,4,32,128]{3,2,1,0:T(8,128)S(1)}, u32[]{:S(2)}, u32[]{:S(2)}) async-start(f32[8,4,32,128]{3,2,1,0:T(8,128)} %bitcast.26), calls=%async_computation.8 | async-start | bytes 1048576 | tf_op jit(solution)/shard_map/all_to_all | solution.py:38
  170.5 9.3 %all-to-all-done.8 = f32[8,4,32,128]{3,2,1,0:T(8,128)S(1)} async-done(((f32[8,4,32,128]{3,2,1,0:T(8,128)}), f32[8,4,32,128]{3,2,1,0:T(8,128)S(1)}, u32[]{:S(2)}, u32[]{:S(2)}) %all-to-all-start.8) | async-done | bytes 524320 | tf_op jit(solution)/shard_map/all_to_all | solution.py:38
  180.5 7.9 %all-to-all-start.6 = ((f32[128,1,128]{2,1,0:T(1,128)}), f32[128,1,128]{2,1,0:T(1,128)S(1)}, u32[]{:S(2)}, u32[]{:S(2)}) async-start(f32[128,1,128]{2,1,0:T(1,128)} %broadcast_in_dim.11), calls=%async_computation.6 | async-start | bytes 131072 | tf_op jit(solution)/shard_map/all_to_all | solution.py:137
  189.3 6.7 %all_gather.23.v_ref = f32[16,32,128]{2,1,0:T(8,128)S(1)} all-gather(f32[4,32,128]{2,1,0:T(8,128)S(1)} %divide_subtract_fusion.1), channel_id=1, replica_groups=mesh['ylo'=2,'core'=2,'zhi'=2,'zlo'=2,'xhi'=2,'xlo'=2,'yhi'=2] {'ylo','c..., dimensions={0}, use_global_device_ids=true | all-gather | bytes 327680 | tf_op jit(solution)/shard_map/all_gather | solution.py:159
  196.0 3.2 %product.11 = f32[32,32,128]{2,1,0:T(8,128)} custom-call(s32[64]{0:T(128)S(1)} %get-tuple-element.14.place_ref, s32[64]{0:T(128)S(1)} %get-tuple-element.13.source_ref, f32[16,32,128]{2,1,0:T(8,128)S(1)} %all_gather.23.v_ref, bf16[64,128,128]{2,1,0:T(8,128)(2,1)S(1)} %pack.1.tiles_ref), custom_call_target="tpu_custom_call" | custom-call | tf_op jit(solution)/shard_map/product/pallas_call | solution.py:121
  199.2 4.8 %all-to-all-start.9 = ((f32[8,4,32,128]{3,2,1,0:T(8,128)}), f32[8,4,32,128]{3,2,1,0:T(8,128)S(1)}, u32[]{:S(2)}, u32[]{:S(2)}) async-start(f32[8,4,32,128]{3,2,1,0:T(8,128)} %bitcast.27), calls=%async_computation.9 | async-start | bytes 1048576 | tf_op jit(solution)/shard_map/all_to_all | solution.py:38
  204.1 11.7 %cholesky.44 = f32[128,128]{1,0:T(8,128)S(1)} custom-call(f32[128,128]{1,0:T(8,128)S(1)} %fusion.4), custom_call_target="Cholesky" | custom-call | tf_op jit(solution)/shard_map/jit(cholesky)/cholesky | solution.py:179
  217.3 6.2 %all-to-all-start.10 = ((f32[4,32,128]{2,1,0:T(8,128)}), f32[4,32,128]{2,1,0:T(8,128)S(1)}, u32[]{:S(2)}, u32[]{:S(2)}) async-start(f32[4,32,128]{2,1,0:T(8,128)} %divide_subtract_fusion), calls=%async_computation.10 | async-start | bytes 131072 | tf_op jit(solution)/shard_map/all_to_all | solution.py:38
  224.1 9.8 %custom-call.6 = f32[1,128,128]{1,2,0:T(8,128)S(1)} custom-call(f32[1,128,128]{2,1,0:T(8,128)S(1)} %fusion.1), custom_call_target="InvertDiagBlocksLowerTriangular" | custom-call | tf_op jit(solution)/shard_map/jit(_solve_triangular)/triangular_solve | solution.py:182
  234.5 20.1 %all_to_all.83 = f32[128,1,128]{2,1,0:T(1,128)S(1)} all-to-all(f32[128,1,128]{2,1,0:T(1,128)S(1)} %bitcast.80), channel_id=1, replica_groups=mesh['ylo'=2,'core'=2,'zhi'=2,'zlo'=2,'xhi'=2,'xlo'=2,'yhi'=2] {'ylo','c..., dimensions={0} | all-to-all | bytes 131072 | tf_op jit(solution)/shard_map/all_to_all | solution.py:135
  254.8 14.0 %all_to_all.84 = f32[128,1,128]{2,1,0:T(1,128)S(1)} all-to-all(f32[128,1,128]{2,1,0:T(1,128)S(1)} %broadcast_in_dim.12), channel_id=1, replica_groups=mesh['ylo'=2,'core'=2,'zhi'=2,'zlo'=2,'xhi'=2,'xlo'=2,'yhi'=2] {'ylo','c..., dimensions={0} | all-to-all | bytes 131072 | tf_op jit(solution)/shard_map/all_to_all | solution.py:137
  268.9 11.7 %cholesky.55 = f32[128,128]{1,0:T(8,128)S(1)} custom-call(f32[128,128]{1,0:T(8,128)S(1)} %fusion.3), custom_call_target="Cholesky" | custom-call | tf_op jit(solution)/shard_map/jit(cholesky)/cholesky | solution.py:179
  281.9 9.8 %custom-call.7 = f32[1,128,128]{1,2,0:T(8,128)S(1)} custom-call(f32[1,128,128]{2,1,0:T(8,128)S(1)} %fusion.2), custom_call_target="InvertDiagBlocksLowerTriangular" | custom-call | tf_op jit(solution)/shard_map/jit(_solve_triangular)/triangular_solve | solution.py:182
  (97 shorter events, 44.0 us)
Async XLA Ops:
  0.0 49.4 %copy-start = (bf16[16,128,128]{2,1,0:T(8,128)(2,1)S(1)}, bf16[16,128,128]{2,1,0:T(8,128)(2,1)}, u32[]{:S(2)}) copy-start(bf16[16,128,128]{2,1,0:T(8,128)(2,1)} %own_ref.1) | copy-start | bytes 1572868
  0.0 10.9 %copy-start.12 = (s32[16]{0:T(128)S(1)}, s32[16]{0:T(128)}, u32[]{:S(2)}) copy-start(s32[16]{0:T(128)} %param.10) | copy-start | bytes 196
  0.0 10.9 %copy-start.11 = (s32[16]{0:T(128)S(1)}, s32[16]{0:T(128)}, u32[]{:S(2)}) copy-start(s32[16]{0:T(128)} %param.11) | copy-start | bytes 196
  0.0 14.2 %copy-start.9 = (f32[128,128]{1,0:T(8,128)S(1)}, f32[128,128]{1,0:T(8,128)}, u32[]{:S(2)}) copy-start(f32[128,128]{1,0:T(8,128)} %param.8) | copy-start | bytes 196612
  4.5 20.9 %collective-permute-start.3 = (f32[8,128,128]{2,1,0:T(8,128)}, f32[8,128,128]{2,1,0:T(8,128)S(1)}, u32[]{:S(2)}, u32[]{:S(2)}) collective-permute-start(f32[8,128,128]{2,1,0:T(8,128)} %get-tuple-element.8), channel_id=1, source_target_pairs={{0,1},{1,0},{2,3},{3,2},{4,5},{5,4},{6,7},{7,6},{8,9},{9,8},{10,11... | collective-permute-start | bytes 1572872 | tf_op jit(solution)/shard_map/ppermute | solution.py:32
  8.2 18.9 %collective-permute-start.6 = (f32[8,128,128]{2,1,0:T(8,128)}, f32[8,128,128]{2,1,0:T(8,128)S(1)}, u32[]{:S(2)}, u32[]{:S(2)}) collective-permute-start(f32[8,128,128]{2,1,0:T(8,128)} %get-tuple-element.6), channel_id=1, source_target_pairs={{0,4},{4,0},{1,5},{5,1},{2,6},{6,2},{3,7},{7,3},{8,12},{12,8},{9,1... | collective-permute-start | bytes 1572872 | tf_op jit(solution)/shard_map/ppermute | solution.py:32
  11.0 8.8 %collective-permute-start = (s32[2,16]{1,0:T(2,128)S(1)}, s32[2,16]{1,0:T(2,128)S(1)}, u32[]{:S(2)}, u32[]{:S(2)}) collective-permute-start(s32[2,16]{1,0:T(2,128)S(1)} %pad_add_fusion.1), channel_id=1, source_target_pairs={{0,1},{1,0},{2,3},{3,2},{4,5},{5,4},{6,7},{7,6},{8,9},{9,8},{10,11... | collective-permute-start | bytes 392 | tf_op jit(solution)/shard_map/ppermute | solution.py:32
  11.1 11.5 %collective-permute-start.1 = (s32[2,16]{1,0:T(2,128)S(1)}, s32[2,16]{1,0:T(2,128)S(1)}, u32[]{:S(2)}, u32[]{:S(2)}) collective-permute-start(s32[2,16]{1,0:T(2,128)S(1)} %pad_add_fusion.1), channel_id=1, source_target_pairs={{0,4},{4,0},{1,5},{5,1},{2,6},{6,2},{3,7},{7,3},{8,12},{12,8},{9,1... | collective-permute-start | bytes 392 | tf_op jit(solution)/shard_map/ppermute | solution.py:32
  11.4 35.6 %collective-permute-start.4 = (f32[8,128,128]{2,1,0:T(8,128)}, f32[8,128,128]{2,1,0:T(8,128)S(1)}, u32[]{:S(2)}, u32[]{:S(2)}) collective-permute-start(f32[8,128,128]{2,1,0:T(8,128)} %get-tuple-element.6), channel_id=1, source_target_pairs={{0,1},{1,0},{2,3},{3,2},{4,5},{5,4},{6,7},{7,6},{8,9},{9,8},{10,11... | collective-permute-start | bytes 1572872 | tf_op jit(solution)/shard_map/ppermute | solution.py:32
  15.0 16.8 %all-to-all-start = ((f32[4,32,128]{2,1,0:T(8,128)}), f32[4,32,128]{2,1,0:T(8,128)S(1)}, u32[]{:S(2)}, u32[]{:S(2)}) async-start(f32[4,32,128]{2,1,0:T(8,128)} %bitcast.11), calls=%async_computation | async-start | bytes 131072 | tf_op jit(solution)/shard_map/all_to_all | solution.py:38
  19.8 5.4 %collective-permute-start.2 = (s32[2,16]{1,0:T(2,128)S(1)}, s32[2,16]{1,0:T(2,128)S(1)}, u32[]{:S(2)}, u32[]{:S(2)}) collective-permute-start(s32[2,16]{1,0:T(2,128)S(1)} %collective-permute-done), channel_id=1, source_target_pairs={{0,4},{4,0},{1,5},{5,1},{2,6},{6,2},{3,7},{7,3},{8,12},{12,8},{9,1... | collective-permute-start | bytes 392 | tf_op jit(solution)/shard_map/ppermute | solution.py:32
  22.6 25.2 %collective-permute-start.5 = (f32[8,128,128]{2,1,0:T(8,128)}, f32[8,128,128]{2,1,0:T(8,128)S(1)}, u32[]{:S(2)}, u32[]{:S(2)}) collective-permute-start(f32[8,128,128]{2,1,0:T(8,128)} %get-tuple-element.8), channel_id=1, source_target_pairs={{0,4},{4,0},{1,5},{5,1},{2,6},{6,2},{3,7},{7,3},{8,12},{12,8},{9,1... | collective-permute-start | bytes 1572872 | tf_op jit(solution)/shard_map/ppermute | solution.py:32
  25.4 23.2 %collective-permute-start.7 = (f32[8,128,128]{2,1,0:T(8,128)S(1)}, f32[8,128,128]{2,1,0:T(8,128)S(1)}, u32[]{:S(2)}, u32[]{:S(2)}) collective-permute-start(f32[8,128,128]{2,1,0:T(8,128)S(1)} %collective-permute-done.3.refs_0_), channel_id=1, source_target_pairs={{0,4},{4,0},{1,5},{5,1},{2,6},{6,2},{3,7},{7,3},{8,12},{12,8},{9,1... | collective-permute-start | bytes 1572872 | tf_op jit(solution)/shard_map/ppermute | solution.py:32
  27.1 22.3 %collective-permute-start.8 = (f32[8,128,128]{2,1,0:T(8,128)S(1)}, f32[8,128,128]{2,1,0:T(8,128)}, u32[]{:S(2)}, u32[]{:S(2)}) collective-permute-start(f32[8,128,128]{2,1,0:T(8,128)S(1)} %collective-permute-done.6.refs_3_), channel_id=1, source_target_pairs={{0,1},{1,0},{2,3},{3,2},{4,5},{5,4},{6,7},{7,6},{8,9},{9,8},{10,11... | collective-permute-start | bytes 1572872 | tf_op jit(solution)/shard_map/ppermute | solution.py:32
  29.9 0.8 copy-start.1
  47.0 0.8 copy-start.3
  47.8 0.8 copy-start.5
  48.6 0.8 copy-start.7
  49.4 1.0 copy-start.2
  50.4 1.0 copy-start.4
  51.5 1.0 copy-start.6
  52.5 1.0 copy-start.8
  54.8 9.2 %copy-start.10 = (f32[2]{0:T(128)S(1)}, f32[2]{0:T(128)}, u32[]{:S(2)}) copy-start(f32[2]{0:T(128)} %param.12) | copy-start | bytes 28
  58.0 14.7 %all-to-all-start.1 = ((f32[8,4,32,128]{3,2,1,0:T(8,128)}), f32[8,4,32,128]{3,2,1,0:T(8,128)S(1)}, u32[]{:S(2)}, u32[]{:S(2)}) async-start(f32[8,4,32,128]{3,2,1,0:T(8,128)} %bitcast.12), calls=%async_computation.1 | async-start | bytes 1048576 | tf_op jit(solution)/shard_map/all_to_all | solution.py:38
  117.7 15.6 %all-to-all-start.4 = ((f32[4,32,128]{2,1,0:T(8,128)}), f32[4,32,128]{2,1,0:T(8,128)S(1)}, u32[]{:S(2)}, u32[]{:S(2)}) async-start(f32[4,32,128]{2,1,0:T(8,128)} %divide_subtract_fusion.2), calls=%async_computation.4 | async-start | bytes 131072 | tf_op jit(solution)/shard_map/all_to_all | solution.py:38
  133.3 13.6 %all-to-all-start.7 = ((f32[8,4,32,128]{3,2,1,0:T(8,128)}), f32[8,4,32,128]{3,2,1,0:T(8,128)S(1)}, u32[]{:S(2)}, u32[]{:S(2)}) async-start(f32[8,4,32,128]{3,2,1,0:T(8,128)} %bitcast.25), calls=%async_computation.7 | async-start | bytes 1048576 | tf_op jit(solution)/shard_map/all_to_all | solution.py:38
  146.9 18.7 %all-to-all-start.5 = ((f32[128,1,128]{2,1,0:T(1,128)}), f32[128,1,128]{2,1,0:T(1,128)S(1)}, u32[]{:S(2)}, u32[]{:S(2)}) async-start(f32[128,1,128]{2,1,0:T(1,128)} %bitcast.19), calls=%async_computation.5 | async-start | bytes 131072 | tf_op jit(solution)/shard_map/all_to_all | solution.py:135
  165.6 14.2 %all-to-all-start.8 = ((f32[8,4,32,128]{3,2,1,0:T(8,128)}), f32[8,4,32,128]{3,2,1,0:T(8,128)S(1)}, u32[]{:S(2)}, u32[]{:S(2)}) async-start(f32[8,4,32,128]{3,2,1,0:T(8,128)} %bitcast.26), calls=%async_computation.8 | async-start | bytes 1048576 | tf_op jit(solution)/shard_map/all_to_all | solution.py:38
  180.5 18.8 %all-to-all-start.6 = ((f32[128,1,128]{2,1,0:T(1,128)}), f32[128,1,128]{2,1,0:T(1,128)S(1)}, u32[]{:S(2)}, u32[]{:S(2)}) async-start(f32[128,1,128]{2,1,0:T(1,128)} %broadcast_in_dim.11), calls=%async_computation.6 | async-start | bytes 131072 | tf_op jit(solution)/shard_map/all_to_all | solution.py:137
  199.2 17.3 %all-to-all-start.9 = ((f32[8,4,32,128]{3,2,1,0:T(8,128)}), f32[8,4,32,128]{3,2,1,0:T(8,128)S(1)}, u32[]{:S(2)}, u32[]{:S(2)}) async-start(f32[8,4,32,128]{3,2,1,0:T(8,128)} %bitcast.27), calls=%async_computation.9 | async-start | bytes 1048576 | tf_op jit(solution)/shard_map/all_to_all | solution.py:38
  217.3 16.7 %all-to-all-start.10 = ((f32[4,32,128]{2,1,0:T(8,128)}), f32[4,32,128]{2,1,0:T(8,128)S(1)}, u32[]{:S(2)}, u32[]{:S(2)}) async-start(f32[4,32,128]{2,1,0:T(8,128)} %divide_subtract_fusion), calls=%async_computation.10 | async-start | bytes 131072 | tf_op jit(solution)/shard_map/all_to_all | solution.py:38

commit v2 on v1

v2 whole, which is shorter than its diff:
```python
import functools
import math

import jax
import jax.numpy as jnp
from jax import lax
from jax.experimental import pallas as pl
from jax.experimental.pallas import tpu as pltpu
from jax.sharding import Mesh
from jax.sharding import PartitionSpec as P

ITERS = 2
HIGH = lax.Precision.HIGHEST
AXES = ("ylo", "core", "zhi", "zlo", "xhi", "xlo", "yhi")
ROW = ("ylo", "core")
COL = ("zhi", "zlo", "xhi", "xlo", "yhi")
SPLIT = ("xhi", "yhi")
SCATTER = ("zhi", "zlo", "xlo")
NS = 2 ** len(SPLIT)
NM = 2 ** len(SCATTER)


def digits(index, names):
    out = 0
    for name in names:
        shift = len(COL) - 1 - COL.index(name)
        out = out * 2 + ((index >> shift) & 1)
    return out


def swap(x, name):
    return lax.ppermute(x, name, [(0, 1), (1, 0)])


def exchange(x, names):
    if not names:
        return x
    return lax.all_to_all(x, names, 0, 0, tiled=True)


def widen_kernel(a_ref, b_ref, wide_a_ref, wide_b_ref):
    wide_a_ref[...] = a_ref[...].astype(jnp.float32)
    wide_b_ref[...] = b_ref[...].astype(jnp.float32)


def widen(tiles):
    slots, blk, _ = tiles.shape
    step = 2
    steps = slots // 2 // step
    block = (step, blk, blk)
    first = pl.BlockSpec(block, lambda i: (i, 0, 0))
    second = pl.BlockSpec(block, lambda i: (i + steps, 0, 0))
    wide = jax.ShapeDtypeStruct((slots // 2, blk, blk), jnp.float32)
    return pl.pallas_call(
        widen_kernel,
        grid=(steps,),
        out_shape=(wide, wide),
        in_specs=[first, second],
        out_specs=(first, first),
        compiler_params=pltpu.CompilerParams(vmem_limit_bytes=48 * 2**20),
        name="widen",
    )(tiles, tiles)


def pack_kernel(*refs):
    o_ref = refs[-1]
    for i, r in enumerate(refs[:-1]):
        o_ref[i] = r[...].astype(jnp.bfloat16)


def pack(parts):
    slots, blk, _ = parts[0].shape
    step = 2
    spec = pl.BlockSpec((step, blk, blk), lambda i: (i, 0, 0))
    return pl.pallas_call(
        pack_kernel,
        grid=(slots // step,),
        out_shape=jax.ShapeDtypeStruct((len(parts), slots, blk, blk), jnp.bfloat16),
        in_specs=[spec] * len(parts),
        out_specs=pl.BlockSpec((len(parts), step, blk, blk), lambda i: (0, i, 0, 0)),
        compiler_params=pltpu.CompilerParams(vmem_limit_bytes=48 * 2**20),
        name="pack",
    )(*parts).reshape(-1, blk, blk)


def share_tiles(tiles, rows, cols):
    meta = jnp.stack([rows, cols])
    a, b = widen(tiles)
    a_y, b_x = swap(a, "yhi"), swap(b, "xhi")
    a_x, b_y = swap(a, "xhi"), swap(b, "yhi")
    a_xy, b_xy = swap(a_y, "xhi"), swap(b_x, "yhi")
    m_y, m_x = swap(meta, "yhi"), swap(meta, "xhi")
    m_xy = swap(m_y, "xhi")
    early = pack([a_y, b_y, a_x, b_x])
    late = pack([a_xy, b_xy])
    metas = jnp.stack([meta, m_y, m_x, m_xy])
    return (tiles, early, late), metas[:, 0], metas[:, 1]


def product_kernel(count, place_ref, source_ref, *refs):
    v_refs, tile_refs, o_ref, parts = refs[:count], refs[count:-2], refs[-2], refs[-1]
    blocks, width, blk = v_refs[0].shape
    for i, v_ref in enumerate(v_refs):
        v = v_ref[...]
        high = v.astype(jnp.bfloat16)
        rest = v - high.astype(jnp.float32)
        middle = rest.astype(jnp.bfloat16)
        low = (rest - middle.astype(jnp.float32)).astype(jnp.bfloat16)
        at = slice(i * blocks, (i + 1) * blocks)
        parts[at, 0:width, :] = high
        parts[at, width : 2 * width, :] = middle
        parts[at, 2 * width : 3 * width, :] = low
    parts[count * blocks] = jnp.zeros(parts.shape[1:], jnp.bfloat16)
    o_ref[...] = jnp.zeros_like(o_ref)
    base = 0
    for tiles_ref in tile_refs:
        slots = tiles_ref.shape[0]

        def step(t, _):
            p = lax.dot_general(
                parts[source_ref[base + t]],
                tiles_ref[t],
                (((1,), (1,)), ((), ())),
                preferred_element_type=jnp.float32,
            )
            o_ref[place_ref[base + t]] += p[0:width] + p[width : 2 * width] + p[2 * width :]
            return 0

        lax.fori_loop(0, slots, step, 0, unroll=16)
        base += slots


def product(place, source, vs, tiles, out_blocks):
    blocks, width, blk = vs[0].shape
    smem = pl.BlockSpec(memory_space=pltpu.SMEM)
    vmem = pl.BlockSpec(memory_space=pltpu.VMEM)
    return pl.pallas_call(
        functools.partial(product_kernel, len(vs)),
        out_shape=jax.ShapeDtypeStruct((out_blocks, width, blk), jnp.float32),
        in_specs=[smem, smem] + [vmem] * (len(vs) + len(tiles)),
        out_specs=vmem,
        scratch_shapes=[pltpu.VMEM((len(vs) * blocks + 1, 3 * width, blk), jnp.bfloat16)],
        compiler_params=pltpu.CompilerParams(vmem_limit_bytes=32 * 2**20),
        name="product",
    )(place, source, *vs, *tiles)


def factor_inverse(gram):
    size = gram.shape[0]
    count = size // 8

    def spread(x):
        return jnp.broadcast_to(x, (8, size))

    lane = lax.broadcasted_iota(jnp.int32, (8, size), 1)
    sub = lax.broadcasted_iota(jnp.int32, (8, size), 0)
    left = [gram[8 * r : 8 * r + 8, :] for r in range(count)]
    right = [jnp.where(lane == sub + 8 * r, 1.0, 0.0) for r in range(count)]
    out = []
    for p in range(count):
        steps, rows = [], []
        for r in range(p, count):
            columns = [spread(left[r][:, 8 * p + m : 8 * p + m + 1]) for m in range(8)]
            for j in range(8):
                if r == p:
                    scale = lax.rsqrt(spread(columns[j][j : j + 1, :]))
                    others = [spread(columns[m][j : j + 1, :]) * scale for m in range(j + 1, 8)]
                    steps.append((scale, others, spread(left[r][j : j + 1, :]) * scale, spread(right[r][j : j + 1, :]) * scale))
                    rows.append(steps[j][3][0:1])
                scale, others, up, row = steps[j]
                entry = columns[j] * scale
                for m in range(j + 1, 8):
                    columns[m] = columns[m] - entry * others[m - j - 1]
                left[r] = left[r] - entry * up
                right[r] = right[r] - entry * row
        out.append(jnp.concatenate(rows, axis=0))
    return out


def factor_kernel(gram_ref, o_ref):
    for i, rows in enumerate(factor_inverse(gram_ref[...])):
        o_ref[8 * i : 8 * i + 8, :] = rows


def factor(gram):
    return pl.pallas_call(factor_kernel, out_shape=jax.ShapeDtypeStruct(gram.shape, jnp.float32), name="factor")(gram)


def finish_kernel(scale, gram_ref, x_ref, o_ref, inverse):
    factor_kernel(gram_ref, inverse)
    x = jnp.dot(inverse[...], x_ref[...], precision=HIGH, preferred_element_type=jnp.float32)
    o_ref[...] = x.T * scale


def finish(gram, x, scale):
    return pl.pallas_call(
        functools.partial(finish_kernel, scale),
        out_shape=jax.ShapeDtypeStruct(x.shape[::-1], jnp.float32),
        scratch_shapes=[pltpu.VMEM(gram.shape, jnp.float32)],
        name="finish",
    )(gram, x)


def whole_blocks(refs):
    pieces = [r[i] for r in refs for i in range(r.shape[0])]
    return jnp.concatenate([jnp.concatenate(pieces[b::NS], axis=0) for b in range(NS)], axis=1)


def inner(x):
    return lax.dot_general(x, x, (((1,), (1,)), ((), ())), precision=HIGH, preferred_element_type=jnp.float32)


def gram_kernel(*refs):
    refs[-1][...] = inner(whole_blocks(refs[:-1]))


def gram(slices):
    width = slices[0].shape[1] * NS
    return pl.pallas_call(
        gram_kernel, out_shape=jax.ShapeDtypeStruct((width, width), jnp.float32), name="gram"
    )(*slices)


def normal_kernel(own_ref, inverse_ref, *refs):
    o_ref, gram_ref, all_ref = refs[-3:]
    x = whole_blocks(refs[:-3])
    y = jnp.dot(inverse_ref[...], x, precision=HIGH, preferred_element_type=jnp.float32)
    gram_ref[...] = inner(y)
    blk = o_ref.shape[1]
    for i in range(NS):
        all_ref[i] = y[:, i * blk : (i + 1) * blk]
    o_ref[...] = all_ref[own_ref[0]]


def normal(own, inverse, slices):
    width, blk = inverse.shape[0], slices[0].shape[2]
    vmem = pl.BlockSpec(memory_space=pltpu.VMEM)
    return pl.pallas_call(
        normal_kernel,
        out_shape=(
            jax.ShapeDtypeStruct((width, blk), jnp.float32),
            jax.ShapeDtypeStruct((width, width), jnp.float32),
        ),
        in_specs=[pl.BlockSpec(memory_space=pltpu.SMEM)] + [vmem] * (1 + len(slices)),
        scratch_shapes=[pltpu.VMEM((NS, width, blk), jnp.float32)],
        name="normal",
    )(own.reshape(1), inverse, *slices)


def on_device(start_block, tiles, tile_rows, tile_cols, bounds):
    centre = (bounds[0] + bounds[1]) / 2.0
    half = (bounds[1] - bounds[0]) / 2.0
    blk = tiles.shape[1]
    width = start_block.shape[1]
    total_rows = blk * 2 ** len(AXES)
    own = 0
    for name in SPLIT:
        own = own * 2 + lax.axis_index(name)
    own_row = 2 * lax.axis_index("ylo") + lax.axis_index("core")

    tile_sets, all_rows, all_cols = share_tiles(tiles, tile_rows, tile_cols)
    live = all_rows >= 0
    position = own ^ jnp.arange(NS, dtype=jnp.int32)[:, None]
    source = jnp.where(live, (all_cols ^ own_row) * NS + position, 4 * NS)
    place = jnp.where(live, digits(all_rows, SCATTER) * NS + digits(all_rows, SPLIT), 0)
    source, place = source.reshape(-1), place.reshape(-1)

    def four(v):
        return [swap(v, "core"), swap(v, "ylo"), lax.ppermute(v, ROW, [(i, i ^ 3) for i in range(4)])]

    def multiply(v, others):
        prods = product(place, source, [v, *others], tile_sets, NM * NS)
        got = exchange(prods.reshape(NM, NS, *v.shape[1:]), SCATTER)
        return jnp.sum(got, axis=0)

    def apply(v):
        return multiply(v, four(v))

    def join(x, other, name):
        low = lax.axis_index(name) == 0
        return [jnp.where(low, x, other), jnp.where(low, other, x)]

    tie = lax.optimization_barrier
    current = exchange(start_block.T.reshape(NS, width // NS, blk), SPLIT)
    first = (apply(current) - centre * current) / half
    second = 2.0 * (apply(first) - centre * first) / half - current
    third = 2.0 * (apply(second) - centre * second) / half - first

    current = third
    (others, other) = tie((four(current), swap(current, "yhi")))
    pair = jnp.concatenate(join(current, other, "yhi"), axis=0)
    first = (multiply(current, others) - centre * current) / half
    first, other = tie((first, swap(pair, "xhi")))
    others, local = tie((four(first), gram(join(pair, other, "xhi"))))
    second = 2.0 * (multiply(first, others) - centre * first) / half - current
    second, sums = tie((second, four(local)))
    local = (local + sums[0]) + (sums[1] + sums[2])
    others, other = tie((four(second), swap(local, "zlo")))
    local = local + other
    third = 2.0 * (multiply(second, others) - centre * second) / half - first
    local = local + swap(local, "zhi")
    local = local + swap(local, "xlo")
    inverse = factor(local)

    pair = jnp.concatenate(join(third, swap(third, "yhi"), "yhi"), axis=0)
    block, local = normal(own, inverse, join(pair, swap(pair, "xhi"), "xhi"))
    sums = four(local)
    local = (local + sums[0]) + (sums[1] + sums[2])
    for name in SCATTER[::-1]:
        local = local + swap(local, name)
    return finish(local, block, math.sqrt(total_rows))


def solution(mesh):
    fine = Mesh(mesh.devices.reshape((2,) * len(AXES)), AXES)
    return jax.shard_map(
        on_device,
        mesh=fine,
        in_specs=(P(AXES, None), P(AXES, None, None), P(AXES), P(AXES), P()),
        out_specs=P(AXES, None),
        check_vma=False,
    )
```

time: 294 us -> 235 us (0.80)
  blocking collectives: 109 us -> 37.4 us
  other arithmetic: 49.4 us -> 4.03 us
  waiting for transfers between devices: 25.6 us -> 61.3 us
  starting transfers between devices: 69.7 us -> 84.7 us
  Pallas kernels: 21.1 us -> 34.9 us
  local copies, waits for them, and re-layouts: 13.1 us -> 6.13 us
    all_gather x6 -> x0, blocking collectives: 50.6 us -> none  [apply(): wide = lax.all_gather(v, ROW, axis=0, tiled=True)]
    another operation x10 -> x0, other arithmetic: 45.7 us -> none  [the longest x6 24.8 us: normal_factor(): return jnp.linalg.cholesky(gram_sum(local))]
    all_to_all x2 -> x0, blocking collectives: 34.1 us -> none  [the longest x1 20.1 us: gram_sum(): lax.all_to_all(local.reshape(n, k * k // n), AXES, 0, 0, tiled=True)]
    ppermute x9 -> x35, starting transfers between devices: 19.7 us -> 51.9 us  [swap(): return lax.ppermute(x, name, [(0, 1), (1, 0)])]
    ppermute x9 -> x35, waiting for transfers between devices: 0.67 us -> 31.1 us  [swap(): return lax.ppermute(x, name, [(0, 1), (1, 0)])]
    all_to_all x7 -> x4, starting transfers between devices: 34.2 us -> 16.4 us  [exchange(): return lax.all_to_all(x, names, 0, 0, tiled=True)]
    ppermute x0 -> x8, starting transfers between devices: none -> 16.4 us  [four(): lax.ppermute(v, ROW, [(i, i ^ 3) for i in range(4)])]
    all_to_all x2 -> x0, starting transfers between devices: 15.8 us -> none  [the longest x1 7.94 us: gram_sum(): lax.all_to_all(jnp.broadcast_to(mine[None], pieces.shape), AXES, 0, 0, ti...]
  transfers between devices with their start and end apart: 18 -> 47, of which waited for: 5 -> 21; matrix products, arithmetic and copies ran while one was open for 9% -> 1% of each run, Pallas kernels for 3% -> 4%
where the time goes in v2:
time: 235 us; the launch traced here: 231 us
  starting transfers between devices  84.7 us (36%)
  waiting for transfers between devices  61.3 us (26%)
  blocking collectives  37.4 us (16%)
  Pallas kernels  34.9 us (15%)
  local copies, waits for them, and re-layouts  6.13 us (3%)
  other arithmetic  4.03 us (2%)
  between operations  2.88 us (1%)
    ppermute x35, starting transfers between devices, swap(): return lax.ppermute(x, name, [(0, 1), (1, 0)])  51.9 us
    all_to_all x3, blocking collectives, exchange(): return lax.all_to_all(x, names, 0, 0, tiled=True)  37.4 us
    ppermute x35, waiting for transfers between devices, swap(): return lax.ppermute(x, name, [(0, 1), (1, 0)])  31.1 us
    all_to_all x4, waiting for transfers between devices, exchange(): return lax.all_to_all(x, names, 0, 0, tiled=True)  22.4 us
    ppermute x8, starting transfers between devices, four(): lax.ppermute(v, ROW, [(i, i ^ 3) for i in range(4)])  16.4 us
    all_to_all x4, starting transfers between devices, exchange(): return lax.all_to_all(x, names, 0, 0, tiled=True)  16.4 us
    pallas_call x6, Pallas kernels, product(): pl.pallas_call(functools.partial(product_kernel, len(vs)), out_shape=jax....  15.9 us
    ppermute x8, waiting for transfers between devices, four(): lax.ppermute(v, ROW, [(i, i ^ 3) for i in range(4)])  7.81 us
  transfers between devices with their start and end apart: 47, of which 21 were waited for; matrix products, arithmetic and copies ran while one was open for 1% of the time, Pallas kernels for 4%

profile of v2, /device:TPU:1, one launch (start us, length us, event | category | flops | bytes accessed | tf_op | source)
XLA Modules:
  0.0 231.3 jit_solution(17706573747209039380)
XLA Ops:
  2.5 3.7 %collective-permute-start.6 = (f32[8,128,128]{2,1,0:T(8,128)S(1)}, f32[8,128,128]{2,1,0:T(8,128)S(1)}, u32[]{:S(2)}, u32[]{:S(2)}) collective-permute-start(f32[8,128,128]{2,1,0:T(8,128)S(1)} %get-tuple-element.27), channel_id=1, source_target_pairs={{0,1},{1,0},{2,3},{3,2},{4,5},{5,4},{6,7},{7,6},{8,9},{9,8},{10,11... | collective-permute-start | bytes 1572872 | tf_op jit(solution)/shard_map/ppermute | solution.py:32
  6.2 2.7 %collective-permute-start.9 = (f32[8,128,128]{2,1,0:T(8,128)}, f32[8,128,128]{2,1,0:T(8,128)}, u32[]{:S(2)}, u32[]{:S(2)}) collective-permute-start(f32[8,128,128]{2,1,0:T(8,128)} %get-tuple-element.28), channel_id=1, source_target_pairs={{0,4},{4,0},{1,5},{5,1},{2,6},{6,2},{3,7},{7,3},{8,12},{12,8},{9,1... | collective-permute-start | bytes 1572872 | tf_op jit(solution)/shard_map/ppermute | solution.py:32
  10.0 2.9 %collective-permute-start.7 = (f32[8,128,128]{2,1,0:T(8,128)}, f32[8,128,128]{2,1,0:T(8,128)S(1)}, u32[]{:S(2)}, u32[]{:S(2)}) collective-permute-start(f32[8,128,128]{2,1,0:T(8,128)} %get-tuple-element.28), channel_id=1, source_target_pairs={{0,1},{1,0},{2,3},{3,2},{4,5},{5,4},{6,7},{7,6},{8,9},{9,8},{10,11... | collective-permute-start | bytes 1572872 | tf_op jit(solution)/shard_map/ppermute | solution.py:32
  13.6 4.0 %all-to-all-start = ((f32[4,32,128]{2,1,0:T(8,128)}), f32[4,32,128]{2,1,0:T(8,128)S(1)}, u32[]{:S(2)}, u32[]{:S(2)}) async-start(f32[4,32,128]{2,1,0:T(8,128)} %bitcast.12), calls=%async_computation | async-start | bytes 131072 | tf_op jit(solution)/shard_map/all_to_all | solution.py:38
  17.8 3.0 %collective-permute-start.2 = (s32[2,16]{1,0:T(2,128)S(1)}, s32[2,16]{1,0:T(2,128)S(1)}, u32[]{:S(2)}, u32[]{:S(2)}) collective-permute-start(s32[2,16]{1,0:T(2,128)S(1)} %collective-permute-done), channel_id=1, source_target_pairs={{0,4},{4,0},{1,5},{5,1},{2,6},{6,2},{3,7},{7,3},{8,12},{12,8},{9,1... | collective-permute-start | bytes 392 | tf_op jit(solution)/shard_map/ppermute | solution.py:32
  25.2 2.6 %collective-permute-start.11 = (f32[8,128,128]{2,1,0:T(8,128)}, f32[8,128,128]{2,1,0:T(8,128)S(1)}, u32[]{:S(2)}, u32[]{:S(2)}) collective-permute-start(f32[8,128,128]{2,1,0:T(8,128)} %collective-permute-done.9.refs_3_), channel_id=1, source_target_pairs={{0,1},{1,0},{2,3},{3,2},{4,5},{5,4},{6,7},{7,6},{8,9},{9,8},{10,11... | collective-permute-start | bytes 1572872 | tf_op jit(solution)/shard_map/ppermute | solution.py:32
  29.5 2.7 %collective-permute-start.3 = (f32[4,32,128]{2,1,0:T(8,128)S(1)}, f32[4,32,128]{2,1,0:T(8,128)S(1)}, u32[]{:S(2)}, u32[]{:S(2)}) collective-permute-start(f32[4,32,128]{2,1,0:T(8,128)S(1)} %all-to-all-done.refs_0_), channel_id=1, source_target_pairs={{0,32},{32,0},{1,33},{33,1},{2,34},{34,2},{3,35},{35,3},{4,36},{36... | collective-permute-start | bytes 196616 | tf_op jit(solution)/shard_map/ppermute | solution.py:32
  34.4 7.5 %collective-permute-start.5 = (f32[4,32,128]{2,1,0:T(8,128)S(1)}, f32[4,32,128]{2,1,0:T(8,128)S(1)}, u32[]{:S(2)}, u32[]{:S(2)}) collective-permute-start(f32[4,32,128]{2,1,0:T(8,128)S(1)} %all-to-all-done.refs_0_), channel_id=1, source_target_pairs={{0,96},{32,64},{64,32},{96,0},{1,97},{33,65},{65,33},{97,1},{2,98}... | collective-permute-start | bytes 196616 | tf_op jit(solution)/shard_map/ppermute | solution.py:269
  45.9 3.1 %product.6 = f32[32,32,128]{2,1,0:T(8,128)} custom-call(s32[64]{0:T(128)S(1)} %get-tuple-element.63.place_ref, s32[64]{0:T(128)S(1)} %get-tuple-element.62.source_ref, f32[4,32,128]{2,1,0:T(8,128)S(1)} %all-to-all-done.refs_0_, f32[4,32,128]{2,1,0:T(8,128)S(1)} %collective-permute-done.3.refs_1_, f32[4,32,128]{2,1,0:T(8,128)S(1)} %collective-permute-done.4.refs_2_, ...), custom_call_target="tpu_custom_call" | custom-call | tf_op jit(solution)/shard_map/product/pallas_call | solution.py:137
  49.0 5.2 %all-to-all-start.1 = ((f32[8,4,32,128]{3,2,1,0:T(8,128)}), f32[8,4,32,128]{3,2,1,0:T(8,128)S(1)}, u32[]{:S(2)}, u32[]{:S(2)}) async-start(f32[8,4,32,128]{3,2,1,0:T(8,128)} %bitcast.15), calls=%async_computation.1 | async-start | bytes 1048576 | tf_op jit(solution)/shard_map/all_to_all | solution.py:38
  57.4 4.4 %all-to-all-done.1 = f32[8,4,32,128]{3,2,1,0:T(8,128)S(1)} async-done(((f32[8,4,32,128]{3,2,1,0:T(8,128)}), f32[8,4,32,128]{3,2,1,0:T(8,128)S(1)}, u32[]{:S(2)}, u32[]{:S(2)}) %all-to-all-start.1) | async-done | bytes 524320 | tf_op jit(solution)/shard_map/all_to_all | solution.py:38
  61.9 4.2 %collective-permute-start.12 = (f32[4,32,128]{2,1,0:T(8,128)S(1)}, f32[4,32,128]{2,1,0:T(8,128)S(1)}, u32[]{:S(2)}, u32[]{:S(2)}) collective-permute-start(f32[4,32,128]{2,1,0:T(8,128)S(1)} %subtract_divide_fusion.1.refs_0_), channel_id=1, source_target_pairs={{0,32},{32,0},{1,33},{33,1},{2,34},{34,2},{3,35},{35,3},{4,36},{36... | collective-permute-start | bytes 196616 | tf_op jit(solution)/shard_map/ppermute | solution.py:32
  73.6 12.2 %all_to_all.35 = f32[8,4,32,128]{3,2,1,0:T(8,128)S(1)} all-to-all(f32[8,4,32,128]{3,2,1,0:T(8,128)S(1)} %bitcast.46), channel_id=1, replica_groups=mesh['ylo'=2,'core'=2,'zhi'=2,'zlo'=2,'xhi'=2,'xlo'=2,'yhi'=2] {'zhi','z..., dimensions={0} | all-to-all | bytes 1048576 | tf_op jit(solution)/shard_map/all_to_all | solution.py:38
  94.6 12.2 %all_to_all.36 = f32[8,4,32,128]{3,2,1,0:T(8,128)S(1)} all-to-all(f32[8,4,32,128]{3,2,1,0:T(8,128)S(1)} %bitcast.47), channel_id=1, replica_groups=mesh['ylo'=2,'core'=2,'zhi'=2,'zlo'=2,'xhi'=2,'xlo'=2,'yhi'=2] {'zhi','z..., dimensions={0} | all-to-all | bytes 1048576 | tf_op jit(solution)/shard_map/all_to_all | solution.py:38
  110.0 2.8 %collective-permute-start.21 = (f32[4,32,128]{2,1,0:T(8,128)S(1)}, f32[4,32,128]{2,1,0:T(8,128)S(1)}, u32[]{:S(2)}, u32[]{:S(2)}) collective-permute-start(f32[4,32,128]{2,1,0:T(8,128)S(1)} %divide_subtract_fusion.2.refs_0_), channel_id=1, source_target_pairs={{0,1},{1,0},{2,3},{3,2},{4,5},{5,4},{6,7},{7,6},{8,9},{9,8},{10,11... | collective-permute-start | bytes 196616 | tf_op jit(solution)/shard_map/ppermute | solution.py:32
  113.5 3.8 %collective-permute-done.21 = f32[4,32,128]{2,1,0:T(8,128)S(1)} collective-permute-done((f32[4,32,128]{2,1,0:T(8,128)S(1)}, f32[4,32,128]{2,1,0:T(8,128)S(1)}, u32[]{:S(2)}, u32[]{:S(2)}) %collective-permute-start.21) | collective-permute-done | bytes 65568 | tf_op jit(solution)/shard_map/ppermute | solution.py:32
  117.3 3.1 %product.9 = f32[32,32,128]{2,1,0:T(8,128)} custom-call(s32[64]{0:T(128)S(1)} %get-tuple-element.63.place_ref, s32[64]{0:T(128)S(1)} %get-tuple-element.62.source_ref, f32[4,32,128]{2,1,0:T(8,128)S(1)} %divide_subtract_fusion.2.refs_0_, f32[4,32,128]{2,1,0:T(8,128)S(1)} %collective-permute-done.18.refs_1_, ...), custom_call_target="tpu_custom_call" | custom-call | tf_op jit(solution)/shard_map/product/pallas_call | solution.py:137
  120.3 3.5 %all-to-all-start.4 = ((f32[8,4,32,128]{3,2,1,0:T(8,128)}), f32[8,4,32,128]{3,2,1,0:T(8,128)S(1)}, u32[]{:S(2)}, u32[]{:S(2)}) async-start(f32[8,4,32,128]{3,2,1,0:T(8,128)} %bitcast.20), calls=%async_computation.4 | async-start | bytes 1048576 | tf_op jit(solution)/shard_map/all_to_all | solution.py:38
  123.8 9.2 %all-to-all-done.4 = f32[8,4,32,128]{3,2,1,0:T(8,128)S(1)} async-done(((f32[8,4,32,128]{3,2,1,0:T(8,128)}), f32[8,4,32,128]{3,2,1,0:T(8,128)S(1)}, u32[]{:S(2)}, u32[]{:S(2)}) %all-to-all-start.4) | async-done | bytes 524320 | tf_op jit(solution)/shard_map/all_to_all | solution.py:38
  134.0 4.5 %collective-permute-done.22 = f32[8,32,128]{2,1,0:T(8,128)S(1)} collective-permute-done((f32[8,32,128]{2,1,0:T(8,128)S(1)}, f32[8,32,128]{2,1,0:T(8,128)S(1)}, u32[]{:S(2)}, u32[]{:S(2)}) %collective-permute-start.22) | collective-permute-done | bytes 131104 | tf_op jit(solution)/shard_map/ppermute | solution.py:32
  138.5 2.9 %collective-permute-start.23 = (f32[4,32,128]{2,1,0:T(8,128)S(1)}, f32[4,32,128]{2,1,0:T(8,128)S(1)}, u32[]{:S(2)}, u32[]{:S(2)}) collective-permute-start(f32[4,32,128]{2,1,0:T(8,128)S(1)} %get-tuple-element.33.refs_0_), channel_id=1, source_target_pairs={{0,32},{32,0},{1,33},{33,1},{2,34},{34,2},{3,35},{35,3},{4,36},{36... | collective-permute-start | bytes 196616 | tf_op jit(solution)/shard_map/ppermute | solution.py:32
  146.7 3.1 %product.10 = f32[32,32,128]{2,1,0:T(8,128)} custom-call(s32[64]{0:T(128)S(1)} %get-tuple-element.63.place_ref, s32[64]{0:T(128)S(1)} %get-tuple-element.62.source_ref, f32[4,32,128]{2,1,0:T(8,128)S(1)} %get-tuple-element.33.refs_0_, f32[4,32,128]{2,1,0:T(8,128)S(1)} %collective-permute-done.23.refs_1_, f32[4,32,128]{2,1,0:T(8,128)S(1)} %collective-permute-done.24.refs_2_, ...), custom_call_target="tpu_custom_call" | custom-call | tf_op jit(solution)/shard_map/product/pallas_call | solution.py:137
  149.7 3.6 %all-to-all-start.5 = ((f32[8,4,32,128]{3,2,1,0:T(8,128)}), f32[8,4,32,128]{3,2,1,0:T(8,128)S(1)}, u32[]{:S(2)}, u32[]{:S(2)}) async-start(f32[8,4,32,128]{3,2,1,0:T(8,128)} %bitcast.21), calls=%async_computation.5 | async-start | bytes 1048576 | tf_op jit(solution)/shard_map/all_to_all | solution.py:38
  155.6 7.3 %all-to-all-done.5 = f32[8,4,32,128]{3,2,1,0:T(8,128)S(1)} async-done(((f32[8,4,32,128]{3,2,1,0:T(8,128)}), f32[8,4,32,128]{3,2,1,0:T(8,128)S(1)}, u32[]{:S(2)}, u32[]{:S(2)}) %all-to-all-start.5) | async-done | bytes 524320 | tf_op jit(solution)/shard_map/all_to_all | solution.py:38
  172.1 12.9 %all_to_all.37 = f32[8,4,32,128]{3,2,1,0:T(8,128)S(1)} all-to-all(f32[8,4,32,128]{3,2,1,0:T(8,128)S(1)} %bitcast.45), channel_id=1, replica_groups=mesh['ylo'=2,'core'=2,'zhi'=2,'zlo'=2,'xhi'=2,'xlo'=2,'yhi'=2] {'zhi','z..., dimensions={0} | all-to-all | bytes 1048576 | tf_op jit(solution)/shard_map/all_to_all | solution.py:38
  186.7 3.1 %collective-permute-done.35 = f32[4,32,128]{2,1,0:T(8,128)S(1)} collective-permute-done((f32[4,32,128]{2,1,0:T(8,128)S(1)}, f32[4,32,128]{2,1,0:T(8,128)S(1)}, u32[]{:S(2)}, u32[]{:S(2)}) %collective-permute-start.35) | collective-permute-done | bytes 65568 | tf_op jit(solution)/shard_map/ppermute | solution.py:32
  191.4 2.6 %collective-permute-done.34 = f32[128,128]{1,0:T(8,128)S(1)} collective-permute-done((f32[128,128]{1,0:T(8,128)S(1)}, f32[128,128]{1,0:T(8,128)S(1)}, u32[]{:S(2)}, u32[]{:S(2)}) %collective-permute-start.34) | collective-permute-done | bytes 65568 | tf_op jit(solution)/shard_map/ppermute | solution.py:32
  194.6 5.3 %factor.1.inverse_ref = f32[128,128]{1,0:T(8,128)} custom-call(f32[128,128]{1,0:T(8,128)} %add.96.gram_ref), custom_call_target="tpu_custom_call" | custom-call | tf_op jit(solution)/shard_map/factor/pallas_call | solution.py:186
  203.1 4.3 %collective-permute-start.37 = (f32[128,128]{1,0:T(8,128)}, f32[128,128]{1,0:T(8,128)S(1)}, u32[]{:S(2)}, u32[]{:S(2)}) collective-permute-start(f32[128,128]{1,0:T(8,128)} %get-tuple-element.47), channel_id=1, source_target_pairs={{0,32},{32,0},{1,33},{33,1},{2,34},{34,2},{3,35},{35,3},{4,36},{36... | collective-permute-start | bytes 196616 | tf_op jit(solution)/shard_map/ppermute | solution.py:32
  217.0 3.1 %collective-permute-done.41 = f32[128,128]{1,0:T(8,128)S(1)} collective-permute-done((f32[128,128]{1,0:T(8,128)S(1)}, f32[128,128]{1,0:T(8,128)S(1)}, u32[]{:S(2)}, u32[]{:S(2)}) %collective-permute-start.41) | collective-permute-done | bytes 65568 | tf_op jit(solution)/shard_map/ppermute | solution.py:32
  221.3 3.8 %collective-permute-done.42 = f32[128,128]{1,0:T(8,128)S(1)} collective-permute-done((f32[128,128]{1,0:T(8,128)S(1)}, f32[128,128]{1,0:T(8,128)S(1)}, u32[]{:S(2)}, u32[]{:S(2)}) %collective-permute-start.42) | collective-permute-done | bytes 65568 | tf_op jit(solution)/shard_map/ppermute | solution.py:32
  225.7 5.6 %finish.1 = f32[128,128]{1,0:T(8,128)} custom-call(f32[128,128]{1,0:T(8,128)} %add.102.gram_ref, f32[128,128]{1,0:T(8,128)} %get-tuple-element.48.x_ref), custom_call_target="tpu_custom_call" | custom-call | tf_op jit(solution)/shard_map/finish/pallas_call | solution.py:196
  (134 shorter events, 73.3 us)
Async XLA Ops:
  2.5 20.8 %collective-permute-start.6 = (f32[8,128,128]{2,1,0:T(8,128)S(1)}, f32[8,128,128]{2,1,0:T(8,128)S(1)}, u32[]{:S(2)}, u32[]{:S(2)}) collective-permute-start(f32[8,128,128]{2,1,0:T(8,128)S(1)} %get-tuple-element.27), channel_id=1, source_target_pairs={{0,1},{1,0},{2,3},{3,2},{4,5},{5,4},{6,7},{7,6},{8,9},{9,8},{10,11... | collective-permute-start | bytes 1572872 | tf_op jit(solution)/shard_map/ppermute | solution.py:32
  6.2 19.0 %collective-permute-start.9 = (f32[8,128,128]{2,1,0:T(8,128)}, f32[8,128,128]{2,1,0:T(8,128)}, u32[]{:S(2)}, u32[]{:S(2)}) collective-permute-start(f32[8,128,128]{2,1,0:T(8,128)} %get-tuple-element.28), channel_id=1, source_target_pairs={{0,4},{4,0},{1,5},{5,1},{2,6},{6,2},{3,7},{7,3},{8,12},{12,8},{9,1... | collective-permute-start | bytes 1572872 | tf_op jit(solution)/shard_map/ppermute | solution.py:32
  9.6 8.2 %collective-permute-start = (s32[2,16]{1,0:T(2,128)S(1)}, s32[2,16]{1,0:T(2,128)S(1)}, u32[]{:S(2)}, u32[]{:S(2)}) collective-permute-start(s32[2,16]{1,0:T(2,128)S(1)} %pad_add_fusion.1), channel_id=1, source_target_pairs={{0,1},{1,0},{2,3},{3,2},{4,5},{5,4},{6,7},{7,6},{8,9},{9,8},{10,11... | collective-permute-start | bytes 392 | tf_op jit(solution)/shard_map/ppermute | solution.py:32
  9.8 11.0 %collective-permute-start.1 = (s32[2,16]{1,0:T(2,128)S(1)}, s32[2,16]{1,0:T(2,128)S(1)}, u32[]{:S(2)}, u32[]{:S(2)}) collective-permute-start(s32[2,16]{1,0:T(2,128)S(1)} %pad_add_fusion.1), channel_id=1, source_target_pairs={{0,4},{4,0},{1,5},{5,1},{2,6},{6,2},{3,7},{7,3},{8,12},{12,8},{9,1... | collective-permute-start | bytes 392 | tf_op jit(solution)/shard_map/ppermute | solution.py:32
  10.0 22.2 %collective-permute-start.7 = (f32[8,128,128]{2,1,0:T(8,128)}, f32[8,128,128]{2,1,0:T(8,128)S(1)}, u32[]{:S(2)}, u32[]{:S(2)}) collective-permute-start(f32[8,128,128]{2,1,0:T(8,128)} %get-tuple-element.28), channel_id=1, source_target_pairs={{0,1},{1,0},{2,3},{3,2},{4,5},{5,4},{6,7},{7,6},{8,9},{9,8},{10,11... | collective-permute-start | bytes 1572872 | tf_op jit(solution)/shard_map/ppermute | solution.py:32
  13.6 15.9 %all-to-all-start = ((f32[4,32,128]{2,1,0:T(8,128)}), f32[4,32,128]{2,1,0:T(8,128)S(1)}, u32[]{:S(2)}, u32[]{:S(2)}) async-start(f32[4,32,128]{2,1,0:T(8,128)} %bitcast.12), calls=%async_computation | async-start | bytes 131072 | tf_op jit(solution)/shard_map/all_to_all | solution.py:38
  17.8 5.5 %collective-permute-start.2 = (s32[2,16]{1,0:T(2,128)S(1)}, s32[2,16]{1,0:T(2,128)S(1)}, u32[]{:S(2)}, u32[]{:S(2)}) collective-permute-start(s32[2,16]{1,0:T(2,128)S(1)} %collective-permute-done), channel_id=1, source_target_pairs={{0,4},{4,0},{1,5},{5,1},{2,6},{6,2},{3,7},{7,3},{8,12},{12,8},{9,1... | collective-permute-start | bytes 392 | tf_op jit(solution)/shard_map/ppermute | solution.py:32
  20.8 12.8 %collective-permute-start.8 = (f32[8,128,128]{2,1,0:T(8,128)S(1)}, f32[8,128,128]{2,1,0:T(8,128)S(1)}, u32[]{:S(2)}, u32[]{:S(2)}) collective-permute-start(f32[8,128,128]{2,1,0:T(8,128)S(1)} %get-tuple-element.27), channel_id=1, source_target_pairs={{0,4},{4,0},{1,5},{5,1},{2,6},{6,2},{3,7},{7,3},{8,12},{12,8},{9,1... | collective-permute-start | bytes 1572872 | tf_op jit(solution)/shard_map/ppermute | solution.py:32
  23.3 21.6 %collective-permute-start.10 = (f32[8,128,128]{2,1,0:T(8,128)S(1)}, f32[8,128,128]{2,1,0:T(8,128)S(1)}, u32[]{:S(2)}, u32[]{:S(2)}) collective-permute-start(f32[8,128,128]{2,1,0:T(8,128)S(1)} %collective-permute-done.6.refs_0_), channel_id=1, source_target_pairs={{0,4},{4,0},{1,5},{5,1},{2,6},{6,2},{3,7},{7,3},{8,12},{12,8},{9,1... | collective-permute-start | bytes 1572872 | tf_op jit(solution)/shard_map/ppermute | solution.py:32
  25.2 19.7 %collective-permute-start.11 = (f32[8,128,128]{2,1,0:T(8,128)}, f32[8,128,128]{2,1,0:T(8,128)S(1)}, u32[]{:S(2)}, u32[]{:S(2)}) collective-permute-start(f32[8,128,128]{2,1,0:T(8,128)} %collective-permute-done.9.refs_3_), channel_id=1, source_target_pairs={{0,1},{1,0},{2,3},{3,2},{4,5},{5,4},{6,7},{7,6},{8,9},{9,8},{10,11... | collective-permute-start | bytes 1572872 | tf_op jit(solution)/shard_map/ppermute | solution.py:32
  29.5 15.6 %collective-permute-start.3 = (f32[4,32,128]{2,1,0:T(8,128)S(1)}, f32[4,32,128]{2,1,0:T(8,128)S(1)}, u32[]{:S(2)}, u32[]{:S(2)}) collective-permute-start(f32[4,32,128]{2,1,0:T(8,128)S(1)} %all-to-all-done.refs_0_), channel_id=1, source_target_pairs={{0,32},{32,0},{1,33},{33,1},{2,34},{34,2},{3,35},{35,3},{4,36},{36... | collective-permute-start | bytes 196616 | tf_op jit(solution)/shard_map/ppermute | solution.py:32
  32.2 12.9 %collective-permute-start.4 = (f32[4,32,128]{2,1,0:T(8,128)S(1)}, f32[4,32,128]{2,1,0:T(8,128)S(1)}, u32[]{:S(2)}, u32[]{:S(2)}) collective-permute-start(f32[4,32,128]{2,1,0:T(8,128)S(1)} %all-to-all-done.refs_0_), channel_id=1, source_target_pairs={{0,64},{64,0},{1,65},{65,1},{2,66},{66,2},{3,67},{67,3},{4,68},{68... | collective-permute-start | bytes 196616 | tf_op jit(solution)/shard_map/ppermute | solution.py:32
  34.4 10.8 %collective-permute-start.5 = (f32[4,32,128]{2,1,0:T(8,128)S(1)}, f32[4,32,128]{2,1,0:T(8,128)S(1)}, u32[]{:S(2)}, u32[]{:S(2)}) collective-permute-start(f32[4,32,128]{2,1,0:T(8,128)S(1)} %all-to-all-done.refs_0_), channel_id=1, source_target_pairs={{0,96},{32,64},{64,32},{96,0},{1,97},{33,65},{65,33},{97,1},{2,98}... | collective-permute-start | bytes 196616 | tf_op jit(solution)/shard_map/ppermute | solution.py:269
  49.0 12.8 %all-to-all-start.1 = ((f32[8,4,32,128]{3,2,1,0:T(8,128)}), f32[8,4,32,128]{3,2,1,0:T(8,128)S(1)}, u32[]{:S(2)}, u32[]{:S(2)}) async-start(f32[8,4,32,128]{3,2,1,0:T(8,128)} %bitcast.15), calls=%async_computation.1 | async-start | bytes 1048576 | tf_op jit(solution)/shard_map/all_to_all | solution.py:38
  61.9 5.9 %collective-permute-start.12 = (f32[4,32,128]{2,1,0:T(8,128)S(1)}, f32[4,32,128]{2,1,0:T(8,128)S(1)}, u32[]{:S(2)}, u32[]{:S(2)}) collective-permute-start(f32[4,32,128]{2,1,0:T(8,128)S(1)} %subtract_divide_fusion.1.refs_0_), channel_id=1, source_target_pairs={{0,32},{32,0},{1,33},{33,1},{2,34},{34,2},{3,35},{35,3},{4,36},{36... | collective-permute-start | bytes 196616 | tf_op jit(solution)/shard_map/ppermute | solution.py:32
  106.9 5.9 %collective-permute-start.18 = (f32[4,32,128]{2,1,0:T(8,128)S(1)}, f32[4,32,128]{2,1,0:T(8,128)S(1)}, u32[]{:S(2)}, u32[]{:S(2)}) collective-permute-start(f32[4,32,128]{2,1,0:T(8,128)S(1)} %divide_subtract_fusion.2.refs_0_), channel_id=1, source_target_pairs={{0,32},{32,0},{1,33},{33,1},{2,34},{34,2},{3,35},{35,3},{4,36},{36... | collective-permute-start | bytes 196616 | tf_op jit(solution)/shard_map/ppermute | solution.py:32
  110.0 7.3 %collective-permute-start.21 = (f32[4,32,128]{2,1,0:T(8,128)S(1)}, f32[4,32,128]{2,1,0:T(8,128)S(1)}, u32[]{:S(2)}, u32[]{:S(2)}) collective-permute-start(f32[4,32,128]{2,1,0:T(8,128)S(1)} %divide_subtract_fusion.2.refs_0_), channel_id=1, source_target_pairs={{0,1},{1,0},{2,3},{3,2},{4,5},{5,4},{6,7},{7,6},{8,9},{9,8},{10,11... | collective-permute-start | bytes 196616 | tf_op jit(solution)/shard_map/ppermute | solution.py:32
  120.3 12.7 %all-to-all-start.4 = ((f32[8,4,32,128]{3,2,1,0:T(8,128)}), f32[8,4,32,128]{3,2,1,0:T(8,128)S(1)}, u32[]{:S(2)}, u32[]{:S(2)}) async-start(f32[8,4,32,128]{3,2,1,0:T(8,128)} %bitcast.20), calls=%async_computation.4 | async-start | bytes 1048576 | tf_op jit(solution)/shard_map/all_to_all | solution.py:38
  133.1 5.4 %collective-permute-start.22 = (f32[8,32,128]{2,1,0:T(8,128)S(1)}, f32[8,32,128]{2,1,0:T(8,128)S(1)}, u32[]{:S(2)}, u32[]{:S(2)}) collective-permute-start(f32[8,32,128]{2,1,0:T(8,128)S(1)} %pad_maximum_fusion), channel_id=1, source_target_pairs={{0,4},{4,0},{1,5},{5,1},{2,6},{6,2},{3,7},{7,3},{8,12},{12,8},{9,1... | collective-permute-start | bytes 393224 | tf_op jit(solution)/shard_map/ppermute | solution.py:32
  138.5 7.3 %collective-permute-start.23 = (f32[4,32,128]{2,1,0:T(8,128)S(1)}, f32[4,32,128]{2,1,0:T(8,128)S(1)}, u32[]{:S(2)}, u32[]{:S(2)}) collective-permute-start(f32[4,32,128]{2,1,0:T(8,128)S(1)} %get-tuple-element.33.refs_0_), channel_id=1, source_target_pairs={{0,32},{32,0},{1,33},{33,1},{2,34},{34,2},{3,35},{35,3},{4,36},{36... | collective-permute-start | bytes 196616 | tf_op jit(solution)/shard_map/ppermute | solution.py:32
  141.4 5.2 %collective-permute-start.25 = (f32[4,32,128]{2,1,0:T(8,128)S(1)}, f32[4,32,128]{2,1,0:T(8,128)S(1)}, u32[]{:S(2)}, u32[]{:S(2)}) collective-permute-start(f32[4,32,128]{2,1,0:T(8,128)S(1)} %get-tuple-element.33.refs_0_), channel_id=1, source_target_pairs={{0,96},{32,64},{64,32},{96,0},{1,97},{33,65},{65,33},{97,1},{2,98}... | collective-permute-start | bytes 196616 | tf_op jit(solution)/shard_map/ppermute | solution.py:269
  149.7 13.2 %all-to-all-start.5 = ((f32[8,4,32,128]{3,2,1,0:T(8,128)}), f32[8,4,32,128]{3,2,1,0:T(8,128)S(1)}, u32[]{:S(2)}, u32[]{:S(2)}) async-start(f32[8,4,32,128]{3,2,1,0:T(8,128)} %bitcast.21), calls=%async_computation.5 | async-start | bytes 1048576 | tf_op jit(solution)/shard_map/all_to_all | solution.py:38
  153.4 9.6 %collective-permute-start.26 = (f32[128,128]{1,0:T(8,128)S(1)}, f32[128,128]{1,0:T(8,128)S(1)}, u32[]{:S(2)}, u32[]{:S(2)}) collective-permute-start(f32[128,128]{1,0:T(8,128)S(1)} %copy-done.4), channel_id=1, source_target_pairs={{0,32},{32,0},{1,33},{33,1},{2,34},{34,2},{3,35},{35,3},{4,36},{36... | collective-permute-start | bytes 196616 | tf_op jit(solution)/shard_map/ppermute | solution.py:32
  153.8 9.3 %collective-permute-start.27 = (f32[128,128]{1,0:T(8,128)S(1)}, f32[128,128]{1,0:T(8,128)S(1)}, u32[]{:S(2)}, u32[]{:S(2)}) collective-permute-start(f32[128,128]{1,0:T(8,128)S(1)} %copy-done.4), channel_id=1, source_target_pairs={{0,64},{64,0},{1,65},{65,1},{2,66},{66,2},{3,67},{67,3},{4,68},{68... | collective-permute-start | bytes 196616 | tf_op jit(solution)/shard_map/ppermute | solution.py:32
  154.1 9.0 %collective-permute-start.28 = (f32[128,128]{1,0:T(8,128)S(1)}, f32[128,128]{1,0:T(8,128)S(1)}, u32[]{:S(2)}, u32[]{:S(2)}) collective-permute-start(f32[128,128]{1,0:T(8,128)S(1)} %copy-done.4), channel_id=1, source_target_pairs={{0,96},{32,64},{64,32},{96,0},{1,97},{33,65},{65,33},{97,1},{2,98}... | collective-permute-start | bytes 196616 | tf_op jit(solution)/shard_map/ppermute | solution.py:269
  164.9 5.0 %collective-permute-start.31 = (f32[4,32,128]{2,1,0:T(8,128)S(1)}, f32[4,32,128]{2,1,0:T(8,128)S(1)}, u32[]{:S(2)}, u32[]{:S(2)}) collective-permute-start(f32[4,32,128]{2,1,0:T(8,128)S(1)} %divide_subtract_fusion.1.refs_0_), channel_id=1, source_target_pairs={{0,96},{32,64},{64,32},{96,0},{1,97},{33,65},{65,33},{97,1},{2,98}... | collective-permute-start | bytes 196616 | tf_op jit(solution)/shard_map/ppermute | solution.py:269
  185.1 4.7 %collective-permute-start.35 = (f32[4,32,128]{2,1,0:T(8,128)S(1)}, f32[4,32,128]{2,1,0:T(8,128)S(1)}, u32[]{:S(2)}, u32[]{:S(2)}) collective-permute-start(f32[4,32,128]{2,1,0:T(8,128)S(1)} %divide_subtract_fusion), channel_id=1, source_target_pairs={{0,1},{1,0},{2,3},{3,2},{4,5},{5,4},{6,7},{7,6},{8,9},{9,8},{10,11... | collective-permute-start | bytes 196616 | tf_op jit(solution)/shard_map/ppermute | solution.py:32
  185.7 5.0 %collective-permute-start.33 = (f32[128,128]{1,0:T(8,128)S(1)}, f32[128,128]{1,0:T(8,128)S(1)}, u32[]{:S(2)}, u32[]{:S(2)}) collective-permute-start(f32[128,128]{1,0:T(8,128)S(1)} %add.94), channel_id=1, source_target_pairs={{0,16},{16,0},{1,17},{17,1},{2,18},{18,2},{3,19},{19,3},{4,20},{20... | collective-permute-start | bytes 196616 | tf_op jit(solution)/shard_map/ppermute | solution.py:32
  189.9 10.1 %collective-permute-start.36 = (f32[8,32,128]{2,1,0:T(8,128)S(1)}, f32[8,32,128]{2,1,0:T(8,128)S(1)}, u32[]{:S(2)}, u32[]{:S(2)}) collective-permute-start(f32[8,32,128]{2,1,0:T(8,128)S(1)} %pad_maximum_fusion.1), channel_id=1, source_target_pairs={{0,4},{4,0},{1,5},{5,1},{2,6},{6,2},{3,7},{7,3},{8,12},{12,8},{9,1... | collective-permute-start | bytes 393224 | tf_op jit(solution)/shard_map/ppermute | solution.py:32
  203.1 6.0 %collective-permute-start.37 = (f32[128,128]{1,0:T(8,128)}, f32[128,128]{1,0:T(8,128)S(1)}, u32[]{:S(2)}, u32[]{:S(2)}) collective-permute-start(f32[128,128]{1,0:T(8,128)} %get-tuple-element.47), channel_id=1, source_target_pairs={{0,32},{32,0},{1,33},{33,1},{2,34},{34,2},{3,35},{35,3},{4,36},{36... | collective-permute-start | bytes 196616 | tf_op jit(solution)/shard_map/ppermute | solution.py:32
  207.7 5.2 %collective-permute-start.39 = (f32[128,128]{1,0:T(8,128)}, f32[128,128]{1,0:T(8,128)S(1)}, u32[]{:S(2)}, u32[]{:S(2)}) collective-permute-start(f32[128,128]{1,0:T(8,128)} %get-tuple-element.47), channel_id=1, source_target_pairs={{0,96},{32,64},{64,32},{96,0},{1,97},{33,65},{65,33},{97,1},{2,98}... | collective-permute-start | bytes 196616 | tf_op jit(solution)/shard_map/ppermute | solution.py:269
  220.2 4.9 %collective-permute-start.42 = (f32[128,128]{1,0:T(8,128)S(1)}, f32[128,128]{1,0:T(8,128)S(1)}, u32[]{:S(2)}, u32[]{:S(2)}) collective-permute-start(f32[128,128]{1,0:T(8,128)S(1)} %add.101), channel_id=1, source_target_pairs={{0,16},{16,0},{1,17},{17,1},{2,18},{18,2},{3,19},{19,3},{4,20},{20... | collective-permute-start | bytes 196616 | tf_op jit(solution)/shard_map/ppermute | solution.py:32
  (24 other events, 82.4 us)

commit v3 on v2

v3 whole, which is shorter than its diff:
```python
import functools
import math

import jax
import jax.numpy as jnp
from jax import lax
from jax.experimental import pallas as pl
from jax.experimental.pallas import tpu as pltpu
from jax.sharding import Mesh
from jax.sharding import PartitionSpec as P

ITERS = 2
HIGH = lax.Precision.HIGHEST
AXES = ("ylo", "core", "zhi", "zlo", "xhi", "xlo", "yhi")
ROW = ("ylo", "core")
COL = ("zhi", "zlo", "xhi", "xlo", "yhi")
SPLIT = ("xhi", "yhi")
SCATTER = ("xlo", "zlo", "zhi")
NS = 2 ** len(SPLIT)
NM = 2 ** len(SCATTER)


def digits(index, names):
    out = 0
    for name in names:
        shift = len(COL) - 1 - COL.index(name)
        out = out * 2 + ((index >> shift) & 1)
    return out


def swap(x, name):
    return lax.ppermute(x, name, [(0, 1), (1, 0)])


def three(x, names):
    return [swap(x, names[1]), swap(x, names[0]), lax.ppermute(x, names, [(i, i ^ 3) for i in range(4)])]


def exchange(x, names):
    if not names:
        return x
    return lax.all_to_all(x, names, 0, 0, tiled=True)


def turn(tile):
    size = tile.shape[0]
    row = lax.broadcasted_iota(jnp.int32, (size, size), 0)
    column = lax.broadcasted_iota(jnp.int32, (size, size), 1)
    identity = jnp.where(row == column, 1.0, 0.0).astype(tile.dtype)
    return lax.dot_general(identity, tile, (((1,), (1,)), ((), ())), preferred_element_type=jnp.float32)


def widen_kernel(tiles_ref, a_ref, b_ref):
    slots, blk, _ = tiles_ref.shape
    half = slots // 2
    for i in range(half):
        a_ref[i * blk : (i + 1) * blk, :] = turn(tiles_ref[i])
        b_ref[i * blk : (i + 1) * blk, :] = turn(tiles_ref[half + i])


def widen(tiles):
    slots, blk, _ = tiles.shape
    wide = jax.ShapeDtypeStruct((slots // 2 * blk, blk), jnp.float32)
    return pl.pallas_call(
        widen_kernel,
        out_shape=(wide, wide),
        compiler_params=pltpu.CompilerParams(vmem_limit_bytes=32 * 2**20),
        name="widen",
    )(tiles)


def turn_kernel(tiles_ref, o_ref):
    for i in range(tiles_ref.shape[0]):
        o_ref[i] = turn(tiles_ref[i]).astype(o_ref.dtype)


def turn_all(tiles):
    return pl.pallas_call(
        turn_kernel, out_shape=jax.ShapeDtypeStruct(tiles.shape, tiles.dtype), name="turn"
    )(tiles)


def pack_kernel(*refs):
    o_ref = refs[-1]
    _, step, blk, _ = o_ref.shape
    for i, r in enumerate(refs[:-1]):
        for k in range(step):
            o_ref[i, k] = r[k * blk : (k + 1) * blk, :].astype(o_ref.dtype)


def pack(parts, slots):
    blk = parts[0].shape[1]
    step = 4
    spec = pl.BlockSpec((step * blk, blk), lambda i: (i, 0))
    return pl.pallas_call(
        pack_kernel,
        grid=(slots // step,),
        out_shape=jax.ShapeDtypeStruct((len(parts), slots, blk, blk), jnp.bfloat16),
        in_specs=[spec] * len(parts),
        out_specs=pl.BlockSpec((len(parts), step, blk, blk), lambda i: (0, i, 0, 0)),
        compiler_params=pltpu.CompilerParams(vmem_limit_bytes=32 * 2**20),
        name="pack",
    )(*parts).reshape(-1, blk, blk)


def share_tiles(tiles, small):
    half = tiles.shape[0] // 2
    a, b = widen(tiles)
    a_y, b_x = swap(a, "yhi"), swap(b, "xhi")
    a_x, b_y = swap(a, "xhi"), swap(b, "yhi")
    a_y, b_x, small = lax.optimization_barrier((a_y, b_x, small))
    a_xy, b_xy = swap(a_y, "xhi"), swap(b_x, "yhi")
    _, tiles = lax.optimization_barrier((a_x, tiles))
    return (turn_all(tiles), pack([a_y, b_y, a_x, b_x], half), pack([a_xy, b_xy], half)), small


def product_kernel(count, begun, start, own_ref, place_ref, source_ref, *refs):
    v_refs, tile_refs, o_ref, parts = refs[:count], refs[count : -2 - begun], refs[-2], refs[-1]
    blocks, width, blk = v_refs[0].shape
    for i, v_ref in enumerate(v_refs):
        v = v_ref[...]
        high = v.astype(jnp.bfloat16)
        rest = v - high.astype(jnp.float32)
        middle = rest.astype(jnp.bfloat16)
        low = (rest - middle.astype(jnp.float32)).astype(jnp.bfloat16)
        at = slice(i * blocks, (i + 1) * blocks)
        parts[at, 0:width, :] = high
        parts[at, width : 2 * width, :] = middle
        parts[at, 2 * width : 3 * width, :] = low
    parts[count * blocks] = jnp.zeros(parts.shape[1:], jnp.bfloat16)
    o_ref[...] = refs[-3][...] if begun else jnp.zeros_like(o_ref)
    slots = place_ref.shape[0] // NS
    at = start
    for tiles_ref in tile_refs:
        for t in range(tiles_ref.shape[0]):
            slot = (own_ref[0] ^ (at // slots)) * slots + at % slots
            at += 1
            p = lax.dot_general(
                parts[source_ref[slot]],
                tiles_ref[t],
                (((1,), (0,)), ((), ())),
                preferred_element_type=jnp.float32,
            )
            o_ref[place_ref[slot]] += p[0:width] + p[width : 2 * width] + p[2 * width :]


def product(own, place, source, vs, tiles, out_blocks, start=0, begun=None):
    blocks, width, blk = vs[0].shape
    smem = pl.BlockSpec(memory_space=pltpu.SMEM)
    vmem = pl.BlockSpec(memory_space=pltpu.VMEM)
    return pl.pallas_call(
        functools.partial(product_kernel, len(vs), begun is not None, start),
        out_shape=jax.ShapeDtypeStruct((out_blocks, width, blk), jnp.float32),
        in_specs=[smem] * 3 + [vmem] * (len(vs) + len(tiles) + (begun is not None)),
        out_specs=vmem,
        scratch_shapes=[pltpu.VMEM((len(vs) * blocks + 1, 3 * width, blk), jnp.bfloat16)],
        compiler_params=pltpu.CompilerParams(vmem_limit_bytes=32 * 2**20),
        name="product",
    )(own.reshape(1), place, source, *vs, *tiles, *([] if begun is None else [begun]))


def factor_solve(gram, right):
    size = gram.shape[0]
    count = size // 8

    def spread(x):
        return jnp.broadcast_to(x, (8, size))

    left = [gram[8 * r : 8 * r + 8, :] for r in range(count)]
    right = list(right)
    out = []
    for p in range(count):
        steps, rows = [], []
        for r in range(p, count):
            columns = [spread(left[r][:, 8 * p + m : 8 * p + m + 1]) for m in range(8)]
            for j in range(8):
                if r == p:
                    scale = lax.rsqrt(spread(columns[j][j : j + 1, :]))
                    others = [spread(columns[m][j : j + 1, :]) * scale for m in range(j + 1, 8)]
                    steps.append((scale, others, spread(left[r][j : j + 1, :]) * scale, spread(right[r][j : j + 1, :]) * scale))
                    rows.append(steps[j][3][0:1])
                scale, others, up, row = steps[j]
                entry = columns[j] * scale
                for m in range(j + 1, 8):
                    columns[m] = columns[m] - entry * others[m - j - 1]
                left[r] = left[r] - entry * up
                right[r] = right[r] - entry * row
        out.append(jnp.concatenate(rows, axis=0))
    return out


def factor_kernel(gram_ref, o_ref):
    size = gram_ref.shape[0]
    lane = lax.broadcasted_iota(jnp.int32, (8, size), 1)
    sub = lax.broadcasted_iota(jnp.int32, (8, size), 0)
    identity = [jnp.where(lane == sub + 8 * r, 1.0, 0.0) for r in range(size // 8)]
    for i, rows in enumerate(factor_solve(gram_ref[...], identity)):
        o_ref[8 * i : 8 * i + 8, :] = rows


def factor(gram):
    return pl.pallas_call(factor_kernel, out_shape=jax.ShapeDtypeStruct(gram.shape, jnp.float32), name="factor")(gram)


def finish_kernel(scale, gram_ref, other_ref, x_ref, o_ref):
    x = [x_ref[8 * r : 8 * r + 8, :] for r in range(x_ref.shape[0] // 8)]
    x = factor_solve(gram_ref[...] + other_ref[...], x)
    o_ref[...] = jnp.concatenate(x, axis=0).T * scale


def finish(gram, other, x, scale):
    return pl.pallas_call(
        functools.partial(finish_kernel, scale),
        out_shape=jax.ShapeDtypeStruct(x.shape[::-1], jnp.float32),
        compiler_params=pltpu.CompilerParams(vmem_limit_bytes=56 * 2**20),
        name="finish",
    )(gram, other, x)


def join(own, refs, x_ref):
    for i, r in enumerate(refs):
        blocks, width, blk = r.shape
        rows = pl.ds(pl.multiple_of((own ^ i) * width, width), width)
        for b in range(blocks):
            x_ref[rows, b * blk : (b + 1) * blk] = r[b]


def inner(x):
    return lax.dot_general(x, x, (((1,), (1,)), ((), ())), precision=HIGH, preferred_element_type=jnp.float32)


def gram_kernel(own_ref, *refs):
    o_ref, x_ref = refs[-2:]
    join(own_ref[0], refs[:-2], x_ref)
    o_ref[...] = inner(x_ref[...])


def gram(own, slices):
    blocks, width, blk = slices[0].shape
    width *= len(slices)
    vmem = pl.BlockSpec(memory_space=pltpu.VMEM)
    return pl.pallas_call(
        gram_kernel,
        out_shape=jax.ShapeDtypeStruct((width, width), jnp.float32),
        in_specs=[pl.BlockSpec(memory_space=pltpu.SMEM)] + [vmem] * len(slices),
        scratch_shapes=[pltpu.VMEM((width, blocks * blk), jnp.float32)],
        name="gram",
    )(own.reshape(1), *slices)


def normal_kernel(own_ref, inverse_ref, *refs):
    o_ref, gram_ref, x_ref, all_ref = refs[-4:]
    join(own_ref[0], refs[:-4], x_ref)
    y = jnp.dot(inverse_ref[...], x_ref[...], precision=HIGH, preferred_element_type=jnp.float32)
    gram_ref[...] = inner(y)
    blk = o_ref.shape[1]
    for i in range(all_ref.shape[0]):
        all_ref[i] = y[:, i * blk : (i + 1) * blk]
    o_ref[...] = all_ref[own_ref[0]]


def normal(own, inverse, slices):
    blocks, width, blk = slices[0].shape
    width *= len(slices)
    vmem = pl.BlockSpec(memory_space=pltpu.VMEM)
    return pl.pallas_call(
        normal_kernel,
        out_shape=(
            jax.ShapeDtypeStruct((width, blk), jnp.float32),
            jax.ShapeDtypeStruct((width, width), jnp.float32),
        ),
        in_specs=[pl.BlockSpec(memory_space=pltpu.SMEM)] + [vmem] * (1 + len(slices)),
        scratch_shapes=[
            pltpu.VMEM((width, blocks * blk), jnp.float32),
            pltpu.VMEM((blocks, width, blk), jnp.float32),
        ],
        compiler_params=pltpu.CompilerParams(vmem_limit_bytes=56 * 2**20),
        name="normal",
    )(own.reshape(1), inverse, *slices)


def ends_kernel(bounds_ref, centre_ref, half_ref):
    centre_ref[...] = jnp.full(centre_ref.shape, (bounds_ref[0] + bounds_ref[1]) / 2.0)
    half_ref[...] = jnp.full(half_ref.shape, (bounds_ref[1] - bounds_ref[0]) / 2.0)


def ends(bounds, width):
    row = jax.ShapeDtypeStruct((1, width), jnp.float32)
    return pl.pallas_call(
        ends_kernel, out_shape=(row, row), in_specs=[pl.BlockSpec(memory_space=pltpu.SMEM)], name="ends"
    )(bounds)


def on_device(start_block, tiles, tile_rows, tile_cols, bounds):
    blk = tiles.shape[1]
    centre, half = ends(bounds, blk)
    width = start_block.shape[1]
    total_rows = blk * 2 ** len(AXES)
    own = 0
    for name in SPLIT:
        own = own * 2 + lax.axis_index(name)
    own_row = 2 * lax.axis_index("ylo") + lax.axis_index("core")
    tie = lax.optimization_barrier

    start_block, centre, half = tie((start_block, centre, half))
    slots = tile_rows.shape[0]
    notes = jnp.pad(jnp.stack([tile_rows, tile_cols]).astype(jnp.float32), ((0, 6), (0, blk - slots)))
    slices = start_block.T.reshape(NS, width // NS, blk)
    slices = jnp.concatenate([slices, jnp.broadcast_to(notes, (NS, *notes.shape))], axis=1)
    got = exchange(jnp.broadcast_to(slices, (4, *slices.shape)).reshape(4 * NS, *slices.shape[1:]), ROW + SPLIT)
    tile_sets, got = share_tiles(tiles, got)
    begun = got[:, : width // NS]
    got = lax.dynamic_index_in_dim(got.reshape(4, NS, *got.shape[1:]), own_row, 0, keepdims=False)
    current = got[:, : width // NS]
    all_rows, all_cols = (got[:, width // NS + i, :slots].astype(jnp.int32) for i in range(2))
    live = all_rows >= 0
    member = jnp.arange(NS, dtype=jnp.int32)[:, None]
    source = jnp.where(live, (all_cols ^ own_row) * NS + member, 4 * NS).reshape(-1)
    source_begun = jnp.where(live, all_cols * NS + member, 4 * NS).reshape(-1)
    place = jnp.where(live, digits(all_rows, SCATTER) * NS + digits(all_rows, SPLIT), 0).reshape(-1)
    early = sum(t.shape[0] for t in tile_sets[:-1])

    def add_up(prods):
        return jnp.sum(exchange(prods.reshape(NM, NS, width // NS, blk), SCATTER), axis=0)

    def multiply(v, others):
        return add_up(product(own, place, source, [v, *others], tile_sets, NM * NS))

    def multiply_first(v):
        prods = product(own, place, source_begun, [v], tile_sets[:-1], NM * NS)
        return add_up(product(own, place, source_begun, [v], tile_sets[-1:], NM * NS, early, prods))

    def apply(v):
        return multiply(v, three(v, ROW))

    def add_three(x, others):
        return (x + others[0]) + (others[1] + others[2])

    first = (multiply_first(begun) - centre * current) / half
    second = 2.0 * (apply(first) - centre * first) / half - current
    third = 2.0 * (apply(second) - centre * second) / half - first

    current = third
    first = (apply(current) - centre * current) / half
    first, slices = tie((first, three(current, SPLIT)))
    others, local = tie((three(first, ROW), gram(own, [current, *slices])))
    second = 2.0 * (multiply(first, others) - centre * first) / half - current
    second, sums = tie((second, three(local, ROW)))
    local = add_three(local, sums)
    others, other = tie((three(second, ROW), swap(local, "zhi")))
    local = local + other
    third = 2.0 * (multiply(second, others) - centre * second) / half - first
    third, sums = tie((third, three(local, ("zlo", "xlo"))))
    inverse = factor(add_three(local, sums))

    block, local = normal(own, inverse, [third, *three(third, SPLIT)])
    local = add_three(local, three(local, ROW))
    local = add_three(local, three(local, ("zlo", "xlo")))
    return finish(local, swap(local, "zhi"), block, math.sqrt(total_rows))


def solution(mesh):
    fine = Mesh(mesh.devices.reshape((2,) * len(AXES)), AXES)
    return jax.shard_map(
        on_device,
        mesh=fine,
        in_specs=(P(AXES, None), P(AXES, None, None), P(AXES), P(AXES), P()),
        out_specs=P(AXES, None),
        check_vma=False,
    )
```

time: 235 us -> 220 us (0.936)
  starting transfers between devices: 84.7 us -> 75.8 us
  local copies, waits for them, and re-layouts: 6.13 us -> 10.2 us
  between operations: 2.88 us -> 0.37 us
    ppermute x35 -> x30, starting transfers between devices: 51.9 us -> 30.8 us  [swap(): return lax.ppermute(x, name, [(0, 1), (1, 0)])]
    ppermute x8 -> x11, starting transfers between devices: 16.4 us -> 26.8 us  [three(): lax.ppermute(x, names, [(i, i ^ 3) for i in range(4)])]
    ppermute x35 -> x30, waiting for transfers between devices: 31.1 us -> 24.4 us  [swap(): return lax.ppermute(x, name, [(0, 1), (1, 0)])]
    unnamed x18 -> x48, local copies, waits for them, and re-layouts: 4.38 us -> 7.96 us
    ppermute x8 -> x11, waiting for transfers between devices: 7.81 us -> 11.2 us  [three(): lax.ppermute(x, names, [(i, i ^ 3) for i in range(4)])]
    all_to_all x4, waiting for transfers between devices: 22.4 us -> 25.8 us  [exchange(): return lax.all_to_all(x, names, 0, 0, tiled=True)]
    pallas_call x7 -> x10, Pallas kernels: 17.4 us -> 16.3 us  [the longest x7 11.2 us: product(): pl.pallas_call(functools.partial(product_kernel, len(vs), begun is not No...]
  transfers between devices with their start and end apart: 47 -> 45, of which waited for: 21 -> 24; matrix products, arithmetic and copies ran while one was open for 1% -> 1% of each run, Pallas kernels for 4% -> 6%
where the time goes in v3:
time: 220 us; the launch traced here: 218 us
  starting transfers between devices  75.8 us (34%)
  waiting for transfers between devices  61.5 us (28%)
  blocking collectives  35.6 us (16%)
  Pallas kernels  32.7 us (15%)
  local copies, waits for them, and re-layouts  10.2 us (5%)
    all_to_all x3, blocking collectives, exchange(): return lax.all_to_all(x, names, 0, 0, tiled=True)  35.6 us
    ppermute x30, starting transfers between devices, swap(): return lax.ppermute(x, name, [(0, 1), (1, 0)])  30.8 us
    ppermute x11, starting transfers between devices, three(): lax.ppermute(x, names, [(i, i ^ 3) for i in range(4)])  26.8 us
    all_to_all x4, waiting for transfers between devices, exchange(): return lax.all_to_all(x, names, 0, 0, tiled=True)  25.8 us
    ppermute x30, waiting for transfers between devices, swap(): return lax.ppermute(x, name, [(0, 1), (1, 0)])  24.4 us
    all_to_all x4, starting transfers between devices, exchange(): return lax.all_to_all(x, names, 0, 0, tiled=True)  18.2 us
    ppermute x11, waiting for transfers between devices, three(): lax.ppermute(x, names, [(i, i ^ 3) for i in range(4)])  11.2 us
    pallas_call x7, Pallas kernels, product(): pl.pallas_call(functools.partial(product_kernel, len(vs), begun is not No...  11.2 us
  transfers between devices with their start and end apart: 45, of which 24 were waited for; matrix products, arithmetic and copies ran while one was open for 1% of the time, Pallas kernels for 6%

profile of v3, /device:TPU:1, one launch (start us, length us, event | category | flops | bytes accessed | tf_op | source)
XLA Modules:
  0.0 218.1 jit_solution(2742580585650621975)
XLA Ops:
  2.3 3.6 %collective-permute-start.4 = (f32[1024,128]{1,0:T(8,128)S(1)}, f32[1024,128]{1,0:T(8,128)S(1)}, u32[]{:S(2)}, u32[]{:S(2)}) collective-permute-start(f32[1024,128]{1,0:T(8,128)S(1)} %get-tuple-element.38), channel_id=1, source_target_pairs={{0,4},{4,0},{1,5},{5,1},{2,6},{6,2},{3,7},{7,3},{8,12},{12,8},{9,1... | collective-permute-start | bytes 1572872 | tf_op jit(solution)/shard_map/ppermute | solution.py:32
  5.9 2.9 %collective-permute-start = (f32[1024,128]{1,0:T(8,128)S(1)}, f32[1024,128]{1,0:T(8,128)S(1)}, u32[]{:S(2)}, u32[]{:S(2)}) collective-permute-start(f32[1024,128]{1,0:T(8,128)S(1)} %get-tuple-element.38), channel_id=1, source_target_pairs={{0,1},{1,0},{2,3},{3,2},{4,5},{5,4},{6,7},{7,6},{8,9},{9,8},{10,11... | collective-permute-start | bytes 1572872 | tf_op jit(solution)/shard_map/ppermute | solution.py:32
  11.9 6.3 %all-to-all-start = ((f32[16,40,128]{2,1,0:T(8,128)}), f32[16,40,128]{2,1,0:T(8,128)S(1)}, u32[]{:S(2)}, u32[]{:S(2)}) async-start(f32[16,40,128]{2,1,0:T(8,128)} %bitcast.5), calls=%async_computation | async-start | bytes 655360 | tf_op jit(solution)/shard_map/all_to_all | solution.py:42
  18.2 2.9 %collective-permute-start.5 = (f32[1024,128]{1,0:T(8,128)}, f32[1024,128]{1,0:T(8,128)S(1)}, u32[]{:S(2)}, u32[]{:S(2)}) collective-permute-start(f32[1024,128]{1,0:T(8,128)} %get-tuple-element.39), channel_id=1, source_target_pairs={{0,1},{1,0},{2,3},{3,2},{4,5},{5,4},{6,7},{7,6},{8,9},{9,8},{10,11... | collective-permute-start | bytes 1572872 | tf_op jit(solution)/shard_map/ppermute | solution.py:32
  21.2 2.5 %turn.1.refs_1_.refs_4_ = bf16[16,128,128]{2,1,0:T(8,128)(2,1)} custom-call(bf16[16,128,128]{2,1,0:T(8,128)(2,1)} %tiles_ref.2), custom_call_target="tpu_custom_call" | custom-call | tf_op jit(solution)/shard_map/turn/pallas_call | solution.py:78
  23.8 11.8 %all-to-all-done = f32[16,40,128]{2,1,0:T(8,128)S(1)} async-done(((f32[16,40,128]{2,1,0:T(8,128)}), f32[16,40,128]{2,1,0:T(8,128)S(1)}, u32[]{:S(2)}, u32[]{:S(2)}) %all-to-all-start) | async-done | bytes 327712 | tf_op jit(solution)/shard_map/all_to_all | solution.py:42
  36.3 3.1 %collective-permute-start.2 = (f32[1024,128]{1,0:T(8,128)S(1)}, f32[1024,128]{1,0:T(8,128)S(1)}, u32[]{:S(2)}, u32[]{:S(2)}) collective-permute-start(f32[1024,128]{1,0:T(8,128)S(1)} %collective-permute-done.refs_0_), channel_id=1, source_target_pairs={{0,4},{4,0},{1,5},{5,1},{2,6},{6,2},{3,7},{7,3},{8,12},{12,8},{9,1... | collective-permute-start | bytes 1572872 | tf_op jit(solution)/shard_map/ppermute | solution.py:32
  46.3 4.1 %collective-permute-done.2.refs_0_ = f32[1024,128]{1,0:T(8,128)S(1)} collective-permute-done((f32[1024,128]{1,0:T(8,128)S(1)}, f32[1024,128]{1,0:T(8,128)S(1)}, u32[]{:S(2)}, u32[]{:S(2)}) %collective-permute-start.2) | collective-permute-done | bytes 524320 | tf_op jit(solution)/shard_map/ppermute | solution.py:32
  50.4 3.6 %collective-permute-done.3.refs_1_ = f32[1024,128]{1,0:T(8,128)S(1)} collective-permute-done((f32[1024,128]{1,0:T(8,128)}, f32[1024,128]{1,0:T(8,128)S(1)}, u32[]{:S(2)}, u32[]{:S(2)}) %collective-permute-start.3) | collective-permute-done | bytes 524320 | tf_op jit(solution)/shard_map/ppermute | solution.py:32
  55.1 12.6 %all_to_all.35 = f32[8,4,32,128]{3,2,1,0:T(8,128)S(1)} all-to-all(f32[8,4,32,128]{3,2,1,0:T(8,128)S(1)} %bitcast.32), channel_id=1, replica_groups=mesh['ylo'=2,'core'=2,'zhi'=2,'zlo'=2,'xhi'=2,'xlo'=2,'yhi'=2] {'xlo','z..., dimensions={0} | all-to-all | bytes 1048576 | tf_op jit(solution)/shard_map/all_to_all | solution.py:42
  68.4 2.6 %collective-permute-start.8 = (f32[4,32,128]{2,1,0:T(8,128)S(1)}, f32[4,32,128]{2,1,0:T(8,128)S(1)}, u32[]{:S(2)}, u32[]{:S(2)}) collective-permute-start(f32[4,32,128]{2,1,0:T(8,128)S(1)} %subtract_divide_fusion.1.refs_0_), channel_id=1, source_target_pairs={{0,96},{32,64},{64,32},{96,0},{1,97},{33,65},{65,33},{97,1},{2,98}... | collective-permute-start | bytes 196616 | tf_op jit(solution)/shard_map/ppermute | solution.py:36
  73.0 3.1 %collective-permute-done.7.refs_2_ = f32[4,32,128]{2,1,0:T(8,128)S(1)} collective-permute-done((f32[4,32,128]{2,1,0:T(8,128)S(1)}, f32[4,32,128]{2,1,0:T(8,128)S(1)}, u32[]{:S(2)}, u32[]{:S(2)}) %collective-permute-start.7) | collective-permute-done | bytes 65568 | tf_op jit(solution)/shard_map/ppermute | solution.py:32
  77.4 11.4 %all_to_all.36 = f32[8,4,32,128]{3,2,1,0:T(8,128)S(1)} all-to-all(f32[8,4,32,128]{3,2,1,0:T(8,128)S(1)} %bitcast.33), channel_id=1, replica_groups=mesh['ylo'=2,'core'=2,'zhi'=2,'zlo'=2,'xhi'=2,'xlo'=2,'yhi'=2] {'xlo','z..., dimensions={0} | all-to-all | bytes 1048576 | tf_op jit(solution)/shard_map/all_to_all | solution.py:42
  92.9 2.6 %collective-permute-done.10.refs_2_ = f32[4,32,128]{2,1,0:T(8,128)S(1)} collective-permute-done((f32[4,32,128]{2,1,0:T(8,128)S(1)}, f32[4,32,128]{2,1,0:T(8,128)S(1)}, u32[]{:S(2)}, u32[]{:S(2)}) %collective-permute-start.10) | collective-permute-done | bytes 65568 | tf_op jit(solution)/shard_map/ppermute | solution.py:32
  96.8 11.6 %all_to_all.37 = f32[8,4,32,128]{3,2,1,0:T(8,128)S(1)} all-to-all(f32[8,4,32,128]{3,2,1,0:T(8,128)S(1)} %bitcast.34), channel_id=1, replica_groups=mesh['ylo'=2,'core'=2,'zhi'=2,'zlo'=2,'xhi'=2,'xlo'=2,'yhi'=2] {'xlo','z..., dimensions={0} | all-to-all | bytes 1048576 | tf_op jit(solution)/shard_map/all_to_all | solution.py:42
  108.5 2.6 %collective-permute-start.14 = (f32[4,32,128]{2,1,0:T(8,128)S(1)}, f32[4,32,128]{2,1,0:T(8,128)S(1)}, u32[]{:S(2)}, u32[]{:S(2)}) collective-permute-start(f32[4,32,128]{2,1,0:T(8,128)S(1)} %divide_subtract_fusion.2.refs_0_), channel_id=1, source_target_pairs={{0,96},{32,64},{64,32},{96,0},{1,97},{33,65},{65,33},{97,1},{2,98}... | collective-permute-start | bytes 196616 | tf_op jit(solution)/shard_map/ppermute | solution.py:36
  117.2 3.5 %all-to-all-start.4 = ((f32[8,4,32,128]{3,2,1,0:T(8,128)}), f32[8,4,32,128]{3,2,1,0:T(8,128)S(1)}, u32[]{:S(2)}, u32[]{:S(2)}) async-start(f32[8,4,32,128]{3,2,1,0:T(8,128)} %bitcast.15), calls=%async_computation.4 | async-start | bytes 1048576 | tf_op jit(solution)/shard_map/all_to_all | solution.py:42
  123.9 2.6 %collective-permute-start.15 = (f32[4,32,128]{2,1,0:T(8,128)S(1)}, f32[4,32,128]{2,1,0:T(8,128)S(1)}, u32[]{:S(2)}, u32[]{:S(2)}) collective-permute-start(f32[4,32,128]{2,1,0:T(8,128)S(1)} %divide_subtract_fusion.2.refs_0_), channel_id=1, source_target_pairs={{0,1},{1,0},{2,3},{3,2},{4,5},{5,4},{6,7},{7,6},{8,9},{9,8},{10,11... | collective-permute-start | bytes 196616 | tf_op jit(solution)/shard_map/ppermute | solution.py:32
  126.5 2.7 %all-to-all-done.4 = f32[8,4,32,128]{3,2,1,0:T(8,128)S(1)} async-done(((f32[8,4,32,128]{3,2,1,0:T(8,128)}), f32[8,4,32,128]{3,2,1,0:T(8,128)S(1)}, u32[]{:S(2)}, u32[]{:S(2)}) %all-to-all-start.4) | async-done | bytes 524320 | tf_op jit(solution)/shard_map/all_to_all | solution.py:42
  139.1 4.7 %all-to-all-start.5 = ((f32[8,4,32,128]{3,2,1,0:T(8,128)}), f32[8,4,32,128]{3,2,1,0:T(8,128)S(1)}, u32[]{:S(2)}, u32[]{:S(2)}) async-start(f32[8,4,32,128]{3,2,1,0:T(8,128)} %bitcast.16), calls=%async_computation.5 | async-start | bytes 1048576 | tf_op jit(solution)/shard_map/all_to_all | solution.py:42
  146.1 5.9 %all-to-all-done.5 = f32[8,4,32,128]{3,2,1,0:T(8,128)S(1)} async-done(((f32[8,4,32,128]{3,2,1,0:T(8,128)}), f32[8,4,32,128]{3,2,1,0:T(8,128)S(1)}, u32[]{:S(2)}, u32[]{:S(2)}) %all-to-all-start.5) | async-done | bytes 524320 | tf_op jit(solution)/shard_map/all_to_all | solution.py:42
  154.2 2.7 %collective-permute-start.26 = (f32[4,32,128]{2,1,0:T(8,128)S(1)}, f32[4,32,128]{2,1,0:T(8,128)S(1)}, u32[]{:S(2)}, u32[]{:S(2)}) collective-permute-start(f32[4,32,128]{2,1,0:T(8,128)S(1)} %divide_subtract_fusion.1.refs_0_), channel_id=1, source_target_pairs={{0,96},{32,64},{64,32},{96,0},{1,97},{33,65},{65,33},{97,1},{2,98}... | collective-permute-start | bytes 196616 | tf_op jit(solution)/shard_map/ppermute | solution.py:36
  157.4 2.4 %collective-permute-done.26.refs_3_ = f32[4,32,128]{2,1,0:T(8,128)S(1)} collective-permute-done((f32[4,32,128]{2,1,0:T(8,128)S(1)}, f32[4,32,128]{2,1,0:T(8,128)S(1)}, u32[]{:S(2)}, u32[]{:S(2)}) %collective-permute-start.26) | collective-permute-done | bytes 65568 | tf_op jit(solution)/shard_map/ppermute | solution.py:36
  163.4 3.6 %all-to-all-start.6 = ((f32[8,4,32,128]{3,2,1,0:T(8,128)}), f32[8,4,32,128]{3,2,1,0:T(8,128)S(1)}, u32[]{:S(2)}, u32[]{:S(2)}) async-start(f32[8,4,32,128]{3,2,1,0:T(8,128)} %bitcast.17), calls=%async_computation.6 | async-start | bytes 1048576 | tf_op jit(solution)/shard_map/all_to_all | solution.py:42
  167.0 2.4 %collective-permute-start.30 = (f32[128,128]{1,0:T(8,128)S(1)}, f32[128,128]{1,0:T(8,128)S(1)}, u32[]{:S(2)}, u32[]{:S(2)}) collective-permute-start(f32[128,128]{1,0:T(8,128)S(1)} %add.103), channel_id=1, source_target_pairs={{0,10},{2,8},{8,2},{10,0},{1,11},{3,9},{9,3},{11,1},{4,14},{6,12},... | collective-permute-start | bytes 196616 | tf_op jit(solution)/shard_map/ppermute | solution.py:36
  169.8 5.3 %all-to-all-done.6 = f32[8,4,32,128]{3,2,1,0:T(8,128)S(1)} async-done(((f32[8,4,32,128]{3,2,1,0:T(8,128)}), f32[8,4,32,128]{3,2,1,0:T(8,128)S(1)}, u32[]{:S(2)}, u32[]{:S(2)}) %all-to-all-start.6) | async-done | bytes 524320 | tf_op jit(solution)/shard_map/all_to_all | solution.py:42
  177.2 4.9 %collective-permute-start.33 = (f32[4,32,128]{2,1,0:T(8,128)S(1)}, f32[4,32,128]{2,1,0:T(8,128)S(1)}, u32[]{:S(2)}, u32[]{:S(2)}) collective-permute-start(f32[4,32,128]{2,1,0:T(8,128)S(1)} %divide_subtract_fusion.refs_0_), channel_id=1, source_target_pairs={{0,5},{1,4},{4,1},{5,0},{2,7},{3,6},{6,3},{7,2},{8,13},{9,12},{12,... | collective-permute-start | bytes 196616 | tf_op jit(solution)/shard_map/ppermute | solution.py:36
  183.5 5.3 %factor.1.inverse_ref = f32[128,128]{1,0:T(8,128)} custom-call(f32[128,128]{1,0:T(8,128)} %add_add_fusion.2.gram_ref), custom_call_target="tpu_custom_call" | custom-call | tf_op jit(solution)/shard_map/factor/pallas_call | solution.py:202
  190.1 2.5 %normal.1 = (f32[128,128]{1,0:T(8,128)}, f32[128,128]{1,0:T(8,128)}) custom-call(s32[1]{0:T(128)} %bitcast.own_ref, f32[128,128]{1,0:T(8,128)} %factor.1.inverse_ref, f32[4,32,128]{2,1,0:T(8,128)} %copy-done.10, f32[4,32,128]{2,1,0:T(8,128)} %copy-done.17, f32[4,32,128]{2,1,0:T(8,128)} %copy-done.16, f32[4,32,128]{2,1,0:T(8,128)} %copy-done.15), custom_call_target="tpu_custom_call" | custom-call | tf_op jit(solution)/shard_map/normal/pallas_call | solution.py:266
  192.5 3.1 %collective-permute-start.36 = (f32[128,128]{1,0:T(8,128)}, f32[128,128]{1,0:T(8,128)S(1)}, u32[]{:S(2)}, u32[]{:S(2)}) collective-permute-start(f32[128,128]{1,0:T(8,128)} %get-tuple-element.69), channel_id=1, source_target_pairs={{0,96},{32,64},{64,32},{96,0},{1,97},{33,65},{65,33},{97,1},{2,98}... | collective-permute-start | bytes 196616 | tf_op jit(solution)/shard_map/ppermute | solution.py:36
  207.1 2.8 %collective-permute-start.40 = (f32[128,128]{1,0:T(8,128)S(1)}, f32[128,128]{1,0:T(8,128)S(1)}, u32[]{:S(2)}, u32[]{:S(2)}) collective-permute-start(f32[128,128]{1,0:T(8,128)S(1)} %add_add_fusion.gram_ref), channel_id=1, source_target_pairs={{0,16},{16,0},{1,17},{17,1},{2,18},{18,2},{3,19},{19,3},{4,20},{20... | collective-permute-start | bytes 196616 | tf_op jit(solution)/shard_map/ppermute | solution.py:32
  212.7 5.4 %finish.1 = f32[128,128]{1,0:T(8,128)} custom-call(f32[128,128]{1,0:T(8,128)} %copy-done.11, f32[128,128]{1,0:T(8,128)} %copy-done.19, f32[128,128]{1,0:T(8,128)} %get-tuple-element.70.x_ref), custom_call_target="tpu_custom_call" | custom-call | tf_op jit(solution)/shard_map/finish/pallas_call | solution.py:212
  (159 shorter events, 70.5 us)
Async XLA Ops:
  2.3 18.9 %collective-permute-start.4 = (f32[1024,128]{1,0:T(8,128)S(1)}, f32[1024,128]{1,0:T(8,128)S(1)}, u32[]{:S(2)}, u32[]{:S(2)}) collective-permute-start(f32[1024,128]{1,0:T(8,128)S(1)} %get-tuple-element.38), channel_id=1, source_target_pairs={{0,4},{4,0},{1,5},{5,1},{2,6},{6,2},{3,7},{7,3},{8,12},{12,8},{9,1... | collective-permute-start | bytes 1572872 | tf_op jit(solution)/shard_map/ppermute | solution.py:32
  5.9 29.6 %collective-permute-start = (f32[1024,128]{1,0:T(8,128)S(1)}, f32[1024,128]{1,0:T(8,128)S(1)}, u32[]{:S(2)}, u32[]{:S(2)}) collective-permute-start(f32[1024,128]{1,0:T(8,128)S(1)} %get-tuple-element.38), channel_id=1, source_target_pairs={{0,1},{1,0},{2,3},{3,2},{4,5},{5,4},{6,7},{7,6},{8,9},{9,8},{10,11... | collective-permute-start | bytes 1572872 | tf_op jit(solution)/shard_map/ppermute | solution.py:32
  8.8 26.7 %collective-permute-start.1 = (f32[1024,128]{1,0:T(8,128)}, f32[1024,128]{1,0:T(8,128)}, u32[]{:S(2)}, u32[]{:S(2)}) collective-permute-start(f32[1024,128]{1,0:T(8,128)} %get-tuple-element.39), channel_id=1, source_target_pairs={{0,4},{4,0},{1,5},{5,1},{2,6},{6,2},{3,7},{7,3},{8,12},{12,8},{9,1... | collective-permute-start | bytes 1572872 | tf_op jit(solution)/shard_map/ppermute | solution.py:32
  11.9 23.6 %all-to-all-start = ((f32[16,40,128]{2,1,0:T(8,128)}), f32[16,40,128]{2,1,0:T(8,128)S(1)}, u32[]{:S(2)}, u32[]{:S(2)}) async-start(f32[16,40,128]{2,1,0:T(8,128)} %bitcast.5), calls=%async_computation | async-start | bytes 655360 | tf_op jit(solution)/shard_map/all_to_all | solution.py:42
  18.2 22.8 %collective-permute-start.5 = (f32[1024,128]{1,0:T(8,128)}, f32[1024,128]{1,0:T(8,128)S(1)}, u32[]{:S(2)}, u32[]{:S(2)}) collective-permute-start(f32[1024,128]{1,0:T(8,128)} %get-tuple-element.39), channel_id=1, source_target_pairs={{0,1},{1,0},{2,3},{3,2},{4,5},{5,4},{6,7},{7,6},{8,9},{9,8},{10,11... | collective-permute-start | bytes 1572872 | tf_op jit(solution)/shard_map/ppermute | solution.py:32
  36.3 14.1 %collective-permute-start.2 = (f32[1024,128]{1,0:T(8,128)S(1)}, f32[1024,128]{1,0:T(8,128)S(1)}, u32[]{:S(2)}, u32[]{:S(2)}) collective-permute-start(f32[1024,128]{1,0:T(8,128)S(1)} %collective-permute-done.refs_0_), channel_id=1, source_target_pairs={{0,4},{4,0},{1,5},{5,1},{2,6},{6,2},{3,7},{7,3},{8,12},{12,8},{9,1... | collective-permute-start | bytes 1572872 | tf_op jit(solution)/shard_map/ppermute | solution.py:32
  39.4 14.7 %collective-permute-start.3 = (f32[1024,128]{1,0:T(8,128)}, f32[1024,128]{1,0:T(8,128)S(1)}, u32[]{:S(2)}, u32[]{:S(2)}) collective-permute-start(f32[1024,128]{1,0:T(8,128)} %collective-permute-done.1.refs_3_), channel_id=1, source_target_pairs={{0,1},{1,0},{2,3},{3,2},{4,5},{5,4},{6,7},{7,6},{8,9},{9,8},{10,11... | collective-permute-start | bytes 1572872 | tf_op jit(solution)/shard_map/ppermute | solution.py:32
  68.4 4.6 %collective-permute-start.8 = (f32[4,32,128]{2,1,0:T(8,128)S(1)}, f32[4,32,128]{2,1,0:T(8,128)S(1)}, u32[]{:S(2)}, u32[]{:S(2)}) collective-permute-start(f32[4,32,128]{2,1,0:T(8,128)S(1)} %subtract_divide_fusion.1.refs_0_), channel_id=1, source_target_pairs={{0,96},{32,64},{64,32},{96,0},{1,97},{33,65},{65,33},{97,1},{2,98}... | collective-permute-start | bytes 196616 | tf_op jit(solution)/shard_map/ppermute | solution.py:36
  71.0 5.0 %collective-permute-start.7 = (f32[4,32,128]{2,1,0:T(8,128)S(1)}, f32[4,32,128]{2,1,0:T(8,128)S(1)}, u32[]{:S(2)}, u32[]{:S(2)}) collective-permute-start(f32[4,32,128]{2,1,0:T(8,128)S(1)} %subtract_divide_fusion.1.refs_0_), channel_id=1, source_target_pairs={{0,64},{64,0},{1,65},{65,1},{2,66},{66,2},{3,67},{67,3},{4,68},{68... | collective-permute-start | bytes 196616 | tf_op jit(solution)/shard_map/ppermute | solution.py:32
  90.9 4.5 %collective-permute-start.10 = (f32[4,32,128]{2,1,0:T(8,128)S(1)}, f32[4,32,128]{2,1,0:T(8,128)S(1)}, u32[]{:S(2)}, u32[]{:S(2)}) collective-permute-start(f32[4,32,128]{2,1,0:T(8,128)S(1)} %divide_subtract_fusion.3.refs_0_), channel_id=1, source_target_pairs={{0,64},{64,0},{1,65},{65,1},{2,66},{66,2},{3,67},{67,3},{4,68},{68... | collective-permute-start | bytes 196616 | tf_op jit(solution)/shard_map/ppermute | solution.py:32
  108.5 5.2 %collective-permute-start.14 = (f32[4,32,128]{2,1,0:T(8,128)S(1)}, f32[4,32,128]{2,1,0:T(8,128)S(1)}, u32[]{:S(2)}, u32[]{:S(2)}) collective-permute-start(f32[4,32,128]{2,1,0:T(8,128)S(1)} %divide_subtract_fusion.2.refs_0_), channel_id=1, source_target_pairs={{0,96},{32,64},{64,32},{96,0},{1,97},{33,65},{65,33},{97,1},{2,98}... | collective-permute-start | bytes 196616 | tf_op jit(solution)/shard_map/ppermute | solution.py:36
  117.2 12.0 %all-to-all-start.4 = ((f32[8,4,32,128]{3,2,1,0:T(8,128)}), f32[8,4,32,128]{3,2,1,0:T(8,128)S(1)}, u32[]{:S(2)}, u32[]{:S(2)}) async-start(f32[8,4,32,128]{3,2,1,0:T(8,128)} %bitcast.15), calls=%async_computation.4 | async-start | bytes 1048576 | tf_op jit(solution)/shard_map/all_to_all | solution.py:42
  120.7 10.0 %collective-permute-start.17 = (f32[4,32,128]{2,1,0:T(8,128)S(1)}, f32[4,32,128]{2,1,0:T(8,128)S(1)}, u32[]{:S(2)}, u32[]{:S(2)}) collective-permute-start(f32[4,32,128]{2,1,0:T(8,128)S(1)} %divide_subtract_fusion.2.refs_0_), channel_id=1, source_target_pairs={{0,5},{1,4},{4,1},{5,0},{2,7},{3,6},{6,3},{7,2},{8,13},{9,12},{12,... | collective-permute-start | bytes 196616 | tf_op jit(solution)/shard_map/ppermute | solution.py:36
  122.9 8.2 %collective-permute-start.16 = (f32[4,32,128]{2,1,0:T(8,128)S(1)}, f32[4,32,128]{2,1,0:T(8,128)S(1)}, u32[]{:S(2)}, u32[]{:S(2)}) collective-permute-start(f32[4,32,128]{2,1,0:T(8,128)S(1)} %divide_subtract_fusion.2.refs_0_), channel_id=1, source_target_pairs={{0,4},{4,0},{1,5},{5,1},{2,6},{6,2},{3,7},{7,3},{8,12},{12,8},{9,1... | collective-permute-start | bytes 196616 | tf_op jit(solution)/shard_map/ppermute | solution.py:32
  123.9 7.2 %collective-permute-start.15 = (f32[4,32,128]{2,1,0:T(8,128)S(1)}, f32[4,32,128]{2,1,0:T(8,128)S(1)}, u32[]{:S(2)}, u32[]{:S(2)}) collective-permute-start(f32[4,32,128]{2,1,0:T(8,128)S(1)} %divide_subtract_fusion.2.refs_0_), channel_id=1, source_target_pairs={{0,1},{1,0},{2,3},{3,2},{4,5},{5,4},{6,7},{7,6},{8,9},{9,8},{10,11... | collective-permute-start | bytes 196616 | tf_op jit(solution)/shard_map/ppermute | solution.py:32
  131.1 4.4 %collective-permute-start.20 = (f32[4,32,128]{2,1,0:T(8,128)S(1)}, f32[4,32,128]{2,1,0:T(8,128)S(1)}, u32[]{:S(2)}, u32[]{:S(2)}) collective-permute-start(f32[4,32,128]{2,1,0:T(8,128)S(1)} %subtract_divide_fusion.refs_0_), channel_id=1, source_target_pairs={{0,96},{32,64},{64,32},{96,0},{1,97},{33,65},{65,33},{97,1},{2,98}... | collective-permute-start | bytes 196616 | tf_op jit(solution)/shard_map/ppermute | solution.py:36
  139.1 12.9 %all-to-all-start.5 = ((f32[8,4,32,128]{3,2,1,0:T(8,128)}), f32[8,4,32,128]{3,2,1,0:T(8,128)S(1)}, u32[]{:S(2)}, u32[]{:S(2)}) async-start(f32[8,4,32,128]{3,2,1,0:T(8,128)} %bitcast.16), calls=%async_computation.5 | async-start | bytes 1048576 | tf_op jit(solution)/shard_map/all_to_all | solution.py:42
  143.9 8.2 %collective-permute-start.23 = (f32[128,128]{1,0:T(8,128)S(1)}, f32[128,128]{1,0:T(8,128)S(1)}, u32[]{:S(2)}, u32[]{:S(2)}) collective-permute-start(f32[128,128]{1,0:T(8,128)S(1)} %copy-done.9), channel_id=1, source_target_pairs={{0,96},{32,64},{64,32},{96,0},{1,97},{33,65},{65,33},{97,1},{2,98}... | collective-permute-start | bytes 196616 | tf_op jit(solution)/shard_map/ppermute | solution.py:36
  145.6 6.5 %collective-permute-start.22 = (f32[128,128]{1,0:T(8,128)S(1)}, f32[128,128]{1,0:T(8,128)S(1)}, u32[]{:S(2)}, u32[]{:S(2)}) collective-permute-start(f32[128,128]{1,0:T(8,128)S(1)} %copy-done.9), channel_id=1, source_target_pairs={{0,64},{64,0},{1,65},{65,1},{2,66},{66,2},{3,67},{67,3},{4,68},{68... | collective-permute-start | bytes 196616 | tf_op jit(solution)/shard_map/ppermute | solution.py:32
  146.0 6.2 %collective-permute-start.21 = (f32[128,128]{1,0:T(8,128)S(1)}, f32[128,128]{1,0:T(8,128)S(1)}, u32[]{:S(2)}, u32[]{:S(2)}) collective-permute-start(f32[128,128]{1,0:T(8,128)S(1)} %copy-done.9), channel_id=1, source_target_pairs={{0,32},{32,0},{1,33},{33,1},{2,34},{34,2},{3,35},{35,3},{4,36},{36... | collective-permute-start | bytes 196616 | tf_op jit(solution)/shard_map/ppermute | solution.py:32
  152.2 5.2 %collective-permute-start.27 = (f32[128,128]{1,0:T(8,128)S(1)}, f32[128,128]{1,0:T(8,128)S(1)}, u32[]{:S(2)}, u32[]{:S(2)}) collective-permute-start(f32[128,128]{1,0:T(8,128)S(1)} %add_add_fusion.3), channel_id=1, source_target_pairs={{0,16},{16,0},{1,17},{17,1},{2,18},{18,2},{3,19},{19,3},{4,20},{20... | collective-permute-start | bytes 196616 | tf_op jit(solution)/shard_map/ppermute | solution.py:32
  154.2 5.6 %collective-permute-start.26 = (f32[4,32,128]{2,1,0:T(8,128)S(1)}, f32[4,32,128]{2,1,0:T(8,128)S(1)}, u32[]{:S(2)}, u32[]{:S(2)}) collective-permute-start(f32[4,32,128]{2,1,0:T(8,128)S(1)} %divide_subtract_fusion.1.refs_0_), channel_id=1, source_target_pairs={{0,96},{32,64},{64,32},{96,0},{1,97},{33,65},{65,33},{97,1},{2,98}... | collective-permute-start | bytes 196616 | tf_op jit(solution)/shard_map/ppermute | solution.py:36
  163.4 11.8 %all-to-all-start.6 = ((f32[8,4,32,128]{3,2,1,0:T(8,128)}), f32[8,4,32,128]{3,2,1,0:T(8,128)S(1)}, u32[]{:S(2)}, u32[]{:S(2)}) async-start(f32[8,4,32,128]{3,2,1,0:T(8,128)} %bitcast.17), calls=%async_computation.6 | async-start | bytes 1048576 | tf_op jit(solution)/shard_map/all_to_all | solution.py:42
  167.0 9.7 %collective-permute-start.30 = (f32[128,128]{1,0:T(8,128)S(1)}, f32[128,128]{1,0:T(8,128)S(1)}, u32[]{:S(2)}, u32[]{:S(2)}) collective-permute-start(f32[128,128]{1,0:T(8,128)S(1)} %add.103), channel_id=1, source_target_pairs={{0,10},{2,8},{8,2},{10,0},{1,11},{3,9},{9,3},{11,1},{4,14},{6,12},... | collective-permute-start | bytes 196616 | tf_op jit(solution)/shard_map/ppermute | solution.py:36
  169.5 7.2 %collective-permute-start.29 = (f32[128,128]{1,0:T(8,128)S(1)}, f32[128,128]{1,0:T(8,128)S(1)}, u32[]{:S(2)}, u32[]{:S(2)}) collective-permute-start(f32[128,128]{1,0:T(8,128)S(1)} %add.103), channel_id=1, source_target_pairs={{0,8},{8,0},{1,9},{9,1},{2,10},{10,2},{3,11},{11,3},{4,12},{12,4},... | collective-permute-start | bytes 196616 | tf_op jit(solution)/shard_map/ppermute | solution.py:32
  169.7 7.4 %collective-permute-start.28 = (f32[128,128]{1,0:T(8,128)S(1)}, f32[128,128]{1,0:T(8,128)S(1)}, u32[]{:S(2)}, u32[]{:S(2)}) collective-permute-start(f32[128,128]{1,0:T(8,128)S(1)} %add.103), channel_id=1, source_target_pairs={{0,2},{2,0},{1,3},{3,1},{4,6},{6,4},{5,7},{7,5},{8,10},{10,8},{9,1... | collective-permute-start | bytes 196616 | tf_op jit(solution)/shard_map/ppermute | solution.py:32
  177.2 11.6 %collective-permute-start.33 = (f32[4,32,128]{2,1,0:T(8,128)S(1)}, f32[4,32,128]{2,1,0:T(8,128)S(1)}, u32[]{:S(2)}, u32[]{:S(2)}) collective-permute-start(f32[4,32,128]{2,1,0:T(8,128)S(1)} %divide_subtract_fusion.refs_0_), channel_id=1, source_target_pairs={{0,5},{1,4},{4,1},{5,0},{2,7},{3,6},{6,3},{7,2},{8,13},{9,12},{12,... | collective-permute-start | bytes 196616 | tf_op jit(solution)/shard_map/ppermute | solution.py:36
  182.1 6.7 %collective-permute-start.32 = (f32[4,32,128]{2,1,0:T(8,128)S(1)}, f32[4,32,128]{2,1,0:T(8,128)S(1)}, u32[]{:S(2)}, u32[]{:S(2)}) collective-permute-start(f32[4,32,128]{2,1,0:T(8,128)S(1)} %divide_subtract_fusion.refs_0_), channel_id=1, source_target_pairs={{0,4},{4,0},{1,5},{5,1},{2,6},{6,2},{3,7},{7,3},{8,12},{12,8},{9,1... | collective-permute-start | bytes 196616 | tf_op jit(solution)/shard_map/ppermute | solution.py:32
  182.1 6.7 %collective-permute-start.31 = (f32[4,32,128]{2,1,0:T(8,128)S(1)}, f32[4,32,128]{2,1,0:T(8,128)S(1)}, u32[]{:S(2)}, u32[]{:S(2)}) collective-permute-start(f32[4,32,128]{2,1,0:T(8,128)S(1)} %divide_subtract_fusion.refs_0_), channel_id=1, source_target_pairs={{0,1},{1,0},{2,3},{3,2},{4,5},{5,4},{6,7},{7,6},{8,9},{9,8},{10,11... | collective-permute-start | bytes 196616 | tf_op jit(solution)/shard_map/ppermute | solution.py:32
  192.5 5.7 %collective-permute-start.36 = (f32[128,128]{1,0:T(8,128)}, f32[128,128]{1,0:T(8,128)S(1)}, u32[]{:S(2)}, u32[]{:S(2)}) collective-permute-start(f32[128,128]{1,0:T(8,128)} %get-tuple-element.69), channel_id=1, source_target_pairs={{0,96},{32,64},{64,32},{96,0},{1,97},{33,65},{65,33},{97,1},{2,98}... | collective-permute-start | bytes 196616 | tf_op jit(solution)/shard_map/ppermute | solution.py:36
  201.8 5.2 %collective-permute-start.38 = (f32[128,128]{1,0:T(8,128)S(1)}, f32[128,128]{1,0:T(8,128)S(1)}, u32[]{:S(2)}, u32[]{:S(2)}) collective-permute-start(f32[128,128]{1,0:T(8,128)S(1)} %add_add_fusion.1), channel_id=1, source_target_pairs={{0,8},{8,0},{1,9},{9,1},{2,10},{10,2},{3,11},{11,3},{4,12},{12,4},... | collective-permute-start | bytes 196616 | tf_op jit(solution)/shard_map/ppermute | solution.py:32
  207.1 4.9 %collective-permute-start.40 = (f32[128,128]{1,0:T(8,128)S(1)}, f32[128,128]{1,0:T(8,128)S(1)}, u32[]{:S(2)}, u32[]{:S(2)}) collective-permute-start(f32[128,128]{1,0:T(8,128)S(1)} %add_add_fusion.gram_ref), channel_id=1, source_target_pairs={{0,16},{16,0},{1,17},{17,1},{2,18},{18,2},{3,19},{19,3},{4,20},{20... | collective-permute-start | bytes 196616 | tf_op jit(solution)/shard_map/ppermute | solution.py:32
  (37 other events, 142.8 us)

commit v4 on v3

--- a/solution.py
+++ b/solution.py
@@ -108,7 +108,6 @@
     a, b = widen(tiles)
     a_y, b_x = swap(a, "yhi"), swap(b, "xhi")
     a_x, b_y = swap(a, "xhi"), swap(b, "yhi")
-    a_y, b_x, small = lax.optimization_barrier((a_y, b_x, small))
     a_xy, b_xy = swap(a_y, "xhi"), swap(b_x, "yhi")
     _, tiles = lax.optimization_barrier((a_x, tiles))
     return (turn_all(tiles), pack([a_y, b_y, a_x, b_x], half), pack([a_xy, b_xy], half)), small
@@ -202,19 +201,47 @@
     return pl.pallas_call(factor_kernel, out_shape=jax.ShapeDtypeStruct(gram.shape, jnp.float32), name="factor")(gram)
 
 
-def finish_kernel(scale, gram_ref, other_ref, x_ref, o_ref):
+def fold(gram):
+    half = gram.shape[0] // 2
+    row = lax.broadcasted_iota(jnp.int32, (half, 2 * half), 0)
+    column = lax.broadcasted_iota(jnp.int32, (half, 2 * half), 1) - half
+    top, low = gram[:half], gram[half:]
+    body = jnp.where((column < 0) | (row < column), low, pltpu.roll(top, half, 1))
+    diagonal = jnp.sum(jnp.where(row == column, low, 0.0), axis=0, keepdims=True)
+    return jnp.concatenate([body, jnp.broadcast_to(diagonal, (8, 2 * half))], axis=0)
+
+
+def unfold(folded):
+    half = folded.shape[1] // 2
+    row = lax.broadcasted_iota(jnp.int32, (half, 2 * half), 0)
+    column = lax.broadcasted_iota(jnp.int32, (half, 2 * half), 1)
+    body, diagonal = folded[:half], folded[half : half + 1]
+    turned = jnp.concatenate([body, jnp.zeros_like(body)], axis=0).T
+    beside, below = turned[:half], turned[half:]
+    first = jnp.where(row >= column, pltpu.roll(body, half, 1), below)
+    top = jnp.where(column < half, first, pltpu.roll(beside, half, 1))
+    column = column - half
+    last = jnp.where(row == column, diagonal, pltpu.roll(below, half, 1))
+    low = jnp.where((column < 0) | (row < column), body, last)
+    return jnp.concatenate([top, low], axis=0)
+
+
+def finish_kernel(scale, folded_ref, x_ref, o_ref):
+    folded = folded_ref[0]
+    for i in range(1, folded_ref.shape[0]):
+        folded = folded + folded_ref[i]
     x = [x_ref[8 * r : 8 * r + 8, :] for r in range(x_ref.shape[0] // 8)]
-    x = factor_solve(gram_ref[...] + other_ref[...], x)
+    x = factor_solve(unfold(folded), x)
     o_ref[...] = jnp.concatenate(x, axis=0).T * scale
 
 
-def finish(gram, other, x, scale):
+def finish(folded, x, scale):
     return pl.pallas_call(
         functools.partial(finish_kernel, scale),
         out_shape=jax.ShapeDtypeStruct(x.shape[::-1], jnp.float32),
-        compiler_params=pltpu.CompilerParams(vmem_limit_bytes=56 * 2**20),
+        compiler_params=pltpu.CompilerParams(vmem_limit_bytes=32 * 2**20),
         name="finish",
-    )(gram, other, x)
+    )(folded, x)
 
 
 def join(own, refs, x_ref):
@@ -252,7 +279,7 @@
     o_ref, gram_ref, x_ref, all_ref = refs[-4:]
     join(own_ref[0], refs[:-4], x_ref)
     y = jnp.dot(inverse_ref[...], x_ref[...], precision=HIGH, preferred_element_type=jnp.float32)
-    gram_ref[...] = inner(y)
+    gram_ref[...] = fold(inner(y))
     blk = o_ref.shape[1]
     for i in range(all_ref.shape[0]):
         all_ref[i] = y[:, i * blk : (i + 1) * blk]
@@ -267,7 +294,7 @@
         normal_kernel,
         out_shape=(
             jax.ShapeDtypeStruct((width, blk), jnp.float32),
-            jax.ShapeDtypeStruct((width, width), jnp.float32),
+            jax.ShapeDtypeStruct((width // 2 + 8, width), jnp.float32),
         ),
         in_specs=[pl.BlockSpec(memory_space=pltpu.SMEM)] + [vmem] * (1 + len(slices)),
         scratch_shapes=[
@@ -342,9 +369,11 @@
 
     current = third
     first = (apply(current) - centre * current) / half
-    first, slices = tie((first, three(current, SPLIT)))
-    others, local = tie((three(first, ROW), gram(own, [current, *slices])))
+    slices = three(current, SPLIT)
+    first, *slices[:2] = tie((first, *slices[:2]))
+    others, slices[2] = tie((three(first, ROW), slices[2]))
     second = 2.0 * (multiply(first, others) - centre * first) / half - current
+    local = gram(own, [current, *slices])
     second, sums = tie((second, three(local, ROW)))
     local = add_three(local, sums)
     others, other = tie((three(second, ROW), swap(local, "zhi")))
@@ -355,8 +384,8 @@
 
     block, local = normal(own, inverse, [third, *three(third, SPLIT)])
     local = add_three(local, three(local, ROW))
-    local = add_three(local, three(local, ("zlo", "xlo")))
-    return finish(local, swap(local, "zhi"), block, math.sqrt(total_rows))
+    folded = exchange(jnp.broadcast_to(local, (NM, *local.shape)), SCATTER)
+    return finish(folded, block, math.sqrt(total_rows))
 
 
 def solution(mesh):

time: 220 us -> 215 us (0.977)
  blocking collectives: 35.6 us -> 46.2 us
  waiting for transfers between devices: 61.5 us -> 51.9 us
  starting transfers between devices: 75.8 us -> 70.6 us
    ppermute x11 -> x10, starting transfers between devices: 26.8 us -> 11.7 us  [three(): lax.ppermute(x, names, [(i, i ^ 3) for i in range(4)])]
    ppermute x30 -> x27, starting transfers between devices: 30.8 us -> 41.7 us  [swap(): return lax.ppermute(x, name, [(0, 1), (1, 0)])]
    all_to_all x3 -> x4, blocking collectives: 35.6 us -> 46.2 us  [exchange(): return lax.all_to_all(x, names, 0, 0, tiled=True)]
    all_to_all x4, waiting for transfers between devices: 25.8 us -> 15.8 us  [exchange(): return lax.all_to_all(x, names, 0, 0, tiled=True)]
    ppermute x11 -> x10, waiting for transfers between devices: 11.2 us -> 13 us  [three(): lax.ppermute(x, names, [(i, i ^ 3) for i in range(4)])]
    ppermute x30 -> x27, waiting for transfers between devices: 24.4 us -> 23.2 us  [swap(): return lax.ppermute(x, name, [(0, 1), (1, 0)])]
    unnamed x48 -> x44, local copies, waits for them, and re-layouts: 7.96 us -> 7.32 us
  transfers between devices with their start and end apart: 45 -> 41, of which waited for: 24 -> 21; matrix products, arithmetic and copies ran while one was open for 1% -> 2% of each run, Pallas kernels for 6% -> 6%
where the time goes in v4:
time: 215 us; the launch traced here: 213 us
  starting transfers between devices  70.6 us (33%)
  waiting for transfers between devices  51.9 us (24%)
  blocking collectives  46.2 us (21%)
  Pallas kernels  31.8 us (15%)
  local copies, waits for them, and re-layouts  10.5 us (5%)
    all_to_all x4, blocking collectives, exchange(): return lax.all_to_all(x, names, 0, 0, tiled=True)  46.2 us
    ppermute x27, starting transfers between devices, swap(): return lax.ppermute(x, name, [(0, 1), (1, 0)])  41.7 us
    ppermute x27, waiting for transfers between devices, swap(): return lax.ppermute(x, name, [(0, 1), (1, 0)])  23.2 us
    all_to_all x4, starting transfers between devices, exchange(): return lax.all_to_all(x, names, 0, 0, tiled=True)  17.2 us
    all_to_all x4, waiting for transfers between devices, exchange(): return lax.all_to_all(x, names, 0, 0, tiled=True)  15.8 us
    ppermute x10, waiting for transfers between devices, three(): lax.ppermute(x, names, [(i, i ^ 3) for i in range(4)])  13 us
    ppermute x10, starting transfers between devices, three(): lax.ppermute(x, names, [(i, i ^ 3) for i in range(4)])  11.7 us
    pallas_call x7, Pallas kernels, product(): pl.pallas_call(functools.partial(product_kernel, len(vs), begun is not No...  11.1 us
  transfers between devices with their start and end apart: 41, of which 21 were waited for; matrix products, arithmetic and copies ran while one was open for 2% of the time, Pallas kernels for 6%

profile of v4, /device:TPU:1, one launch (start us, length us, event | category | flops | bytes accessed | tf_op | source)
XLA Modules:
  0.0 213.3 jit_solution(8877108720492334084)
XLA Ops:
  2.4 3.7 %collective-permute-start = (f32[1024,128]{1,0:T(8,128)S(1)}, f32[1024,128]{1,0:T(8,128)S(1)}, u32[]{:S(2)}, u32[]{:S(2)}) collective-permute-start(f32[1024,128]{1,0:T(8,128)S(1)} %get-tuple-element.37), channel_id=1, source_target_pairs={{0,1},{1,0},{2,3},{3,2},{4,5},{5,4},{6,7},{7,6},{8,9},{9,8},{10,11... | collective-permute-start | bytes 1572872 | tf_op jit(solution)/shard_map/ppermute | solution.py:32
  6.1 2.8 %collective-permute-start.2 = (f32[1024,128]{1,0:T(8,128)}, f32[1024,128]{1,0:T(8,128)}, u32[]{:S(2)}, u32[]{:S(2)}) collective-permute-start(f32[1024,128]{1,0:T(8,128)} %get-tuple-element.38), channel_id=1, source_target_pairs={{0,4},{4,0},{1,5},{5,1},{2,6},{6,2},{3,7},{7,3},{8,12},{12,8},{9,1... | collective-permute-start | bytes 1572872 | tf_op jit(solution)/shard_map/ppermute | solution.py:32
  11.7 5.2 %all-to-all-start = ((f32[16,40,128]{2,1,0:T(8,128)}), f32[16,40,128]{2,1,0:T(8,128)}, u32[]{:S(2)}, u32[]{:S(2)}) async-start(f32[16,40,128]{2,1,0:T(8,128)} %bitcast.5), calls=%async_computation | async-start | bytes 655360 | tf_op jit(solution)/shard_map/all_to_all | solution.py:42
  16.9 2.9 %collective-permute-start.4 = (f32[1024,128]{1,0:T(8,128)S(1)}, f32[1024,128]{1,0:T(8,128)S(1)}, u32[]{:S(2)}, u32[]{:S(2)}) collective-permute-start(f32[1024,128]{1,0:T(8,128)S(1)} %get-tuple-element.37), channel_id=1, source_target_pairs={{0,4},{4,0},{1,5},{5,1},{2,6},{6,2},{3,7},{7,3},{8,12},{12,8},{9,1... | collective-permute-start | bytes 1572872 | tf_op jit(solution)/shard_map/ppermute | solution.py:32
  19.7 2.7 %collective-permute-start.5 = (f32[1024,128]{1,0:T(8,128)}, f32[1024,128]{1,0:T(8,128)S(1)}, u32[]{:S(2)}, u32[]{:S(2)}) collective-permute-start(f32[1024,128]{1,0:T(8,128)} %get-tuple-element.38), channel_id=1, source_target_pairs={{0,1},{1,0},{2,3},{3,2},{4,5},{5,4},{6,7},{7,6},{8,9},{9,8},{10,11... | collective-permute-start | bytes 1572872 | tf_op jit(solution)/shard_map/ppermute | solution.py:32
  23.3 3.4 %all-to-all-done = f32[16,40,128]{2,1,0:T(8,128)} async-done(((f32[16,40,128]{2,1,0:T(8,128)}), f32[16,40,128]{2,1,0:T(8,128)}, u32[]{:S(2)}, u32[]{:S(2)}) %all-to-all-start) | async-done | bytes 327712 | tf_op jit(solution)/shard_map/all_to_all | solution.py:42
  28.9 7.1 %collective-permute-done.4.refs_2_ = f32[1024,128]{1,0:T(8,128)S(1)} collective-permute-done((f32[1024,128]{1,0:T(8,128)S(1)}, f32[1024,128]{1,0:T(8,128)S(1)}, u32[]{:S(2)}, u32[]{:S(2)}) %collective-permute-start.4) | collective-permute-done | bytes 524320 | tf_op jit(solution)/shard_map/ppermute | solution.py:32
  36.0 2.5 %turn.1.refs_1_.refs_4_ = bf16[16,128,128]{2,1,0:T(8,128)(2,1)} custom-call(bf16[16,128,128]{2,1,0:T(8,128)(2,1)} %tiles_ref.2), custom_call_target="tpu_custom_call" | custom-call | tf_op jit(solution)/shard_map/turn/pallas_call | solution.py:78
  43.8 3.4 %collective-permute-done.1.refs_0_ = f32[1024,128]{1,0:T(8,128)S(1)} collective-permute-done((f32[1024,128]{1,0:T(8,128)S(1)}, f32[1024,128]{1,0:T(8,128)S(1)}, u32[]{:S(2)}, u32[]{:S(2)}) %collective-permute-start.1) | collective-permute-done | bytes 524320 | tf_op jit(solution)/shard_map/ppermute | solution.py:32
  48.7 12.7 %all_to_all.40 = f32[8,4,32,128]{3,2,1,0:T(8,128)S(1)} all-to-all(f32[8,4,32,128]{3,2,1,0:T(8,128)S(1)} %bitcast.32), channel_id=1, replica_groups=mesh['ylo'=2,'core'=2,'zhi'=2,'zlo'=2,'xhi'=2,'xlo'=2,'yhi'=2] {'xlo','z..., dimensions={0} | all-to-all | bytes 1048576 | tf_op jit(solution)/shard_map/all_to_all | solution.py:42
  62.1 3.0 %collective-permute-start.6 = (f32[4,32,128]{2,1,0:T(8,128)S(1)}, f32[4,32,128]{2,1,0:T(8,128)S(1)}, u32[]{:S(2)}, u32[]{:S(2)}) collective-permute-start(f32[4,32,128]{2,1,0:T(8,128)S(1)} %subtract_divide_fusion.1.refs_0_), channel_id=1, source_target_pairs={{0,32},{32,0},{1,33},{33,1},{2,34},{34,2},{3,35},{35,3},{4,36},{36... | collective-permute-start | bytes 196616 | tf_op jit(solution)/shard_map/ppermute | solution.py:32
  71.7 11.4 %all_to_all.41 = f32[8,4,32,128]{3,2,1,0:T(8,128)S(1)} all-to-all(f32[8,4,32,128]{3,2,1,0:T(8,128)S(1)} %bitcast.33), channel_id=1, replica_groups=mesh['ylo'=2,'core'=2,'zhi'=2,'zlo'=2,'xhi'=2,'xlo'=2,'yhi'=2] {'xlo','z..., dimensions={0} | all-to-all | bytes 1048576 | tf_op jit(solution)/shard_map/all_to_all | solution.py:42
  84.4 2.4 %collective-permute-start.11 = (f32[4,32,128]{2,1,0:T(8,128)S(1)}, f32[4,32,128]{2,1,0:T(8,128)S(1)}, u32[]{:S(2)}, u32[]{:S(2)}) collective-permute-start(f32[4,32,128]{2,1,0:T(8,128)S(1)} %divide_subtract_fusion.3.refs_0_), channel_id=1, source_target_pairs={{0,96},{32,64},{64,32},{96,0},{1,97},{33,65},{65,33},{97,1},{2,98}... | collective-permute-start | bytes 196616 | tf_op jit(solution)/shard_map/ppermute | solution.py:36
  86.8 3.5 %collective-permute-done.11.refs_3_ = f32[4,32,128]{2,1,0:T(8,128)S(1)} collective-permute-done((f32[4,32,128]{2,1,0:T(8,128)S(1)}, f32[4,32,128]{2,1,0:T(8,128)S(1)}, u32[]{:S(2)}, u32[]{:S(2)}) %collective-permute-start.11) | collective-permute-done | bytes 65568 | tf_op jit(solution)/shard_map/ppermute | solution.py:36
  91.6 11.4 %all_to_all.42 = f32[8,4,32,128]{3,2,1,0:T(8,128)S(1)} all-to-all(f32[8,4,32,128]{3,2,1,0:T(8,128)S(1)} %bitcast.34), channel_id=1, replica_groups=mesh['ylo'=2,'core'=2,'zhi'=2,'zlo'=2,'xhi'=2,'xlo'=2,'yhi'=2] {'xlo','z..., dimensions={0} | all-to-all | bytes 1048576 | tf_op jit(solution)/shard_map/all_to_all | solution.py:42
  110.4 2.1 product.11
  112.5 3.5 %all-to-all-start.4 = ((f32[8,4,32,128]{3,2,1,0:T(8,128)}), f32[8,4,32,128]{3,2,1,0:T(8,128)S(1)}, u32[]{:S(2)}, u32[]{:S(2)}) async-start(f32[8,4,32,128]{3,2,1,0:T(8,128)} %bitcast.15), calls=%async_computation.4 | async-start | bytes 1048576 | tf_op jit(solution)/shard_map/all_to_all | solution.py:42
  116.0 2.6 %collective-permute-start.15 = (f32[4,32,128]{2,1,0:T(8,128)S(1)}, f32[4,32,128]{2,1,0:T(8,128)S(1)}, u32[]{:S(2)}, u32[]{:S(2)}) collective-permute-start(f32[4,32,128]{2,1,0:T(8,128)S(1)} %divide_subtract_fusion.2.refs_0_), channel_id=1, source_target_pairs={{0,1},{1,0},{2,3},{3,2},{4,5},{5,4},{6,7},{7,6},{8,9},{9,8},{10,11... | collective-permute-start | bytes 196616 | tf_op jit(solution)/shard_map/ppermute | solution.py:32
  121.7 2.8 %all-to-all-done.4 = f32[8,4,32,128]{3,2,1,0:T(8,128)S(1)} async-done(((f32[8,4,32,128]{3,2,1,0:T(8,128)}), f32[8,4,32,128]{3,2,1,0:T(8,128)S(1)}, u32[]{:S(2)}, u32[]{:S(2)}) %all-to-all-start.4) | async-done | bytes 524320 | tf_op jit(solution)/shard_map/all_to_all | solution.py:42
  124.6 2.3 %collective-permute-done.16.refs_2_ = f32[4,32,128]{2,1,0:T(8,128)S(1)} collective-permute-done((f32[4,32,128]{2,1,0:T(8,128)S(1)}, f32[4,32,128]{2,1,0:T(8,128)S(1)}, u32[]{:S(2)}, u32[]{:S(2)}) %collective-permute-start.16) | collective-permute-done | bytes 65568 | tf_op jit(solution)/shard_map/ppermute | solution.py:32
  135.2 4.9 %all-to-all-start.5 = ((f32[8,4,32,128]{3,2,1,0:T(8,128)}), f32[8,4,32,128]{3,2,1,0:T(8,128)S(1)}, u32[]{:S(2)}, u32[]{:S(2)}) async-start(f32[8,4,32,128]{3,2,1,0:T(8,128)} %bitcast.16), calls=%async_computation.5 | async-start | bytes 1048576 | tf_op jit(solution)/shard_map/all_to_all | solution.py:42
  144.3 4.1 %all-to-all-done.5 = f32[8,4,32,128]{3,2,1,0:T(8,128)S(1)} async-done(((f32[8,4,32,128]{3,2,1,0:T(8,128)}), f32[8,4,32,128]{3,2,1,0:T(8,128)S(1)}, u32[]{:S(2)}, u32[]{:S(2)}) %all-to-all-start.5) | async-done | bytes 524320 | tf_op jit(solution)/shard_map/all_to_all | solution.py:42
  149.3 2.2 %collective-permute-start.27 = (f32[128,128]{1,0:T(8,128)S(1)}, f32[128,128]{1,0:T(8,128)S(1)}, u32[]{:S(2)}, u32[]{:S(2)}) collective-permute-start(f32[128,128]{1,0:T(8,128)S(1)} %add_add_fusion.1), channel_id=1, source_target_pairs={{0,16},{16,0},{1,17},{17,1},{2,18},{18,2},{3,19},{19,3},{4,20},{20... | collective-permute-start | bytes 196616 | tf_op jit(solution)/shard_map/ppermute | solution.py:32
  158.3 2.1 product.13
  160.4 3.6 %all-to-all-start.6 = ((f32[8,4,32,128]{3,2,1,0:T(8,128)}), f32[8,4,32,128]{3,2,1,0:T(8,128)S(1)}, u32[]{:S(2)}, u32[]{:S(2)}) async-start(f32[8,4,32,128]{3,2,1,0:T(8,128)} %bitcast.17), calls=%async_computation.6 | async-start | bytes 1048576 | tf_op jit(solution)/shard_map/all_to_all | solution.py:42
  166.9 5.5 %all-to-all-done.6 = f32[8,4,32,128]{3,2,1,0:T(8,128)S(1)} async-done(((f32[8,4,32,128]{3,2,1,0:T(8,128)}), f32[8,4,32,128]{3,2,1,0:T(8,128)S(1)}, u32[]{:S(2)}, u32[]{:S(2)}) %all-to-all-start.6) | async-done | bytes 524320 | tf_op jit(solution)/shard_map/all_to_all | solution.py:42
  175.9 3.0 %collective-permute-start.32 = (f32[4,32,128]{2,1,0:T(8,128)S(1)}, f32[4,32,128]{2,1,0:T(8,128)S(1)}, u32[]{:S(2)}, u32[]{:S(2)}) collective-permute-start(f32[4,32,128]{2,1,0:T(8,128)S(1)} %divide_subtract_fusion.refs_0_), channel_id=1, source_target_pairs={{0,4},{4,0},{1,5},{5,1},{2,6},{6,2},{3,7},{7,3},{8,12},{12,8},{9,1... | collective-permute-start | bytes 196616 | tf_op jit(solution)/shard_map/ppermute | solution.py:32
  181.2 5.3 %factor.1.inverse_ref = f32[128,128]{1,0:T(8,128)} custom-call(f32[128,128]{1,0:T(8,128)} %add_add_fusion.gram_ref), custom_call_target="tpu_custom_call" | custom-call | tf_op jit(solution)/shard_map/factor/pallas_call | solution.py:201
  187.8 2.5 %normal.1 = (f32[128,128]{1,0:T(8,128)}, f32[72,128]{1,0:T(8,128)}) custom-call(s32[1]{0:T(128)} %bitcast.own_ref, f32[128,128]{1,0:T(8,128)} %factor.1.inverse_ref, f32[4,32,128]{2,1,0:T(8,128)} %copy-done.10, f32[4,32,128]{2,1,0:T(8,128)} %copy-done.14, f32[4,32,128]{2,1,0:T(8,128)} %copy-done.15, f32[4,32,128]{2,1,0:T(8,128)} %copy-done.16), custom_call_target="tpu_custom_call" | custom-call | tf_op jit(solution)/shard_map/normal/pallas_call | solution.py:293
  190.3 2.6 %collective-permute-start.34 = (f32[72,128]{1,0:T(8,128)}, f32[72,128]{1,0:T(8,128)S(1)}, u32[]{:S(2)}, u32[]{:S(2)}) collective-permute-start(f32[72,128]{1,0:T(8,128)} %get-tuple-element.61), channel_id=1, source_target_pairs={{0,32},{32,0},{1,33},{33,1},{2,34},{34,2},{3,35},{35,3},{4,36},{36... | collective-permute-start | bytes 110600 | tf_op jit(solution)/shard_map/ppermute | solution.py:32
  198.0 10.7 %all_to_all.43.folded_ref = f32[8,72,128]{2,1,0:T(8,128)S(1)} all-to-all(f32[8,72,128]{2,1,0:T(8,128)S(1)} %broadcast_in_dim.15), channel_id=1, replica_groups=mesh['ylo'=2,'core'=2,'zhi'=2,'zlo'=2,'xhi'=2,'xlo'=2,'yhi'=2] {'xlo','z..., dimensions={0} | all-to-all | bytes 589824 | tf_op jit(solution)/shard_map/all_to_all | solution.py:42
  208.7 4.7 %finish.1 = f32[128,128]{1,0:T(8,128)} custom-call(f32[8,72,128]{2,1,0:T(8,128)S(1)} %all_to_all.43.folded_ref, f32[128,128]{1,0:T(8,128)S(1)} %copy-done.8), custom_call_target="tpu_custom_call" | custom-call | tf_op jit(solution)/shard_map/finish/pallas_call | solution.py:239
  (148 shorter events, 70.5 us)
Async XLA Ops:
  2.4 20.2 %collective-permute-start = (f32[1024,128]{1,0:T(8,128)S(1)}, f32[1024,128]{1,0:T(8,128)S(1)}, u32[]{:S(2)}, u32[]{:S(2)}) collective-permute-start(f32[1024,128]{1,0:T(8,128)S(1)} %get-tuple-element.37), channel_id=1, source_target_pairs={{0,1},{1,0},{2,3},{3,2},{4,5},{5,4},{6,7},{7,6},{8,9},{9,8},{10,11... | collective-permute-start | bytes 1572872 | tf_op jit(solution)/shard_map/ppermute | solution.py:32
  6.1 16.7 %collective-permute-start.2 = (f32[1024,128]{1,0:T(8,128)}, f32[1024,128]{1,0:T(8,128)}, u32[]{:S(2)}, u32[]{:S(2)}) collective-permute-start(f32[1024,128]{1,0:T(8,128)} %get-tuple-element.38), channel_id=1, source_target_pairs={{0,4},{4,0},{1,5},{5,1},{2,6},{6,2},{3,7},{7,3},{8,12},{12,8},{9,1... | collective-permute-start | bytes 1572872 | tf_op jit(solution)/shard_map/ppermute | solution.py:32
  11.7 15.0 %all-to-all-start = ((f32[16,40,128]{2,1,0:T(8,128)}), f32[16,40,128]{2,1,0:T(8,128)}, u32[]{:S(2)}, u32[]{:S(2)}) async-start(f32[16,40,128]{2,1,0:T(8,128)} %bitcast.5), calls=%async_computation | async-start | bytes 655360 | tf_op jit(solution)/shard_map/all_to_all | solution.py:42
  16.9 19.1 %collective-permute-start.4 = (f32[1024,128]{1,0:T(8,128)S(1)}, f32[1024,128]{1,0:T(8,128)S(1)}, u32[]{:S(2)}, u32[]{:S(2)}) collective-permute-start(f32[1024,128]{1,0:T(8,128)S(1)} %get-tuple-element.37), channel_id=1, source_target_pairs={{0,4},{4,0},{1,5},{5,1},{2,6},{6,2},{3,7},{7,3},{8,12},{12,8},{9,1... | collective-permute-start | bytes 1572872 | tf_op jit(solution)/shard_map/ppermute | solution.py:32
  19.7 18.8 %collective-permute-start.5 = (f32[1024,128]{1,0:T(8,128)}, f32[1024,128]{1,0:T(8,128)S(1)}, u32[]{:S(2)}, u32[]{:S(2)}) collective-permute-start(f32[1024,128]{1,0:T(8,128)} %get-tuple-element.38), channel_id=1, source_target_pairs={{0,1},{1,0},{2,3},{3,2},{4,5},{5,4},{6,7},{7,6},{8,9},{9,8},{10,11... | collective-permute-start | bytes 1572872 | tf_op jit(solution)/shard_map/ppermute | solution.py:32
  22.5 24.7 %collective-permute-start.1 = (f32[1024,128]{1,0:T(8,128)S(1)}, f32[1024,128]{1,0:T(8,128)S(1)}, u32[]{:S(2)}, u32[]{:S(2)}) collective-permute-start(f32[1024,128]{1,0:T(8,128)S(1)} %collective-permute-done.refs_0_), channel_id=1, source_target_pairs={{0,4},{4,0},{1,5},{5,1},{2,6},{6,2},{3,7},{7,3},{8,12},{12,8},{9,1... | collective-permute-start | bytes 1572872 | tf_op jit(solution)/shard_map/ppermute | solution.py:32
  22.8 24.9 %collective-permute-start.3 = (f32[1024,128]{1,0:T(8,128)}, f32[1024,128]{1,0:T(8,128)S(1)}, u32[]{:S(2)}, u32[]{:S(2)}) collective-permute-start(f32[1024,128]{1,0:T(8,128)} %collective-permute-done.2.refs_3_), channel_id=1, source_target_pairs={{0,1},{1,0},{2,3},{3,2},{4,5},{5,4},{6,7},{7,6},{8,9},{9,8},{10,11... | collective-permute-start | bytes 1572872 | tf_op jit(solution)/shard_map/ppermute | solution.py:32
  62.1 4.7 %collective-permute-start.6 = (f32[4,32,128]{2,1,0:T(8,128)S(1)}, f32[4,32,128]{2,1,0:T(8,128)S(1)}, u32[]{:S(2)}, u32[]{:S(2)}) collective-permute-start(f32[4,32,128]{2,1,0:T(8,128)S(1)} %subtract_divide_fusion.1.refs_0_), channel_id=1, source_target_pairs={{0,32},{32,0},{1,33},{33,1},{2,34},{34,2},{3,35},{35,3},{4,36},{36... | collective-permute-start | bytes 196616 | tf_op jit(solution)/shard_map/ppermute | solution.py:32
  66.1 4.3 %collective-permute-start.8 = (f32[4,32,128]{2,1,0:T(8,128)S(1)}, f32[4,32,128]{2,1,0:T(8,128)S(1)}, u32[]{:S(2)}, u32[]{:S(2)}) collective-permute-start(f32[4,32,128]{2,1,0:T(8,128)S(1)} %subtract_divide_fusion.1.refs_0_), channel_id=1, source_target_pairs={{0,96},{32,64},{64,32},{96,0},{1,97},{33,65},{65,33},{97,1},{2,98}... | collective-permute-start | bytes 196616 | tf_op jit(solution)/shard_map/ppermute | solution.py:36
  84.4 5.9 %collective-permute-start.11 = (f32[4,32,128]{2,1,0:T(8,128)S(1)}, f32[4,32,128]{2,1,0:T(8,128)S(1)}, u32[]{:S(2)}, u32[]{:S(2)}) collective-permute-start(f32[4,32,128]{2,1,0:T(8,128)S(1)} %divide_subtract_fusion.3.refs_0_), channel_id=1, source_target_pairs={{0,96},{32,64},{64,32},{96,0},{1,97},{33,65},{65,33},{97,1},{2,98}... | collective-permute-start | bytes 196616 | tf_op jit(solution)/shard_map/ppermute | solution.py:36
  105.9 4.5 %collective-permute-start.14 = (f32[4,32,128]{2,1,0:T(8,128)S(1)}, f32[4,32,128]{2,1,0:T(8,128)S(1)}, u32[]{:S(2)}, u32[]{:S(2)}) collective-permute-start(f32[4,32,128]{2,1,0:T(8,128)S(1)} %divide_subtract_fusion.2.refs_0_), channel_id=1, source_target_pairs={{0,96},{32,64},{64,32},{96,0},{1,97},{33,65},{65,33},{97,1},{2,98}... | collective-permute-start | bytes 196616 | tf_op jit(solution)/shard_map/ppermute | solution.py:36
  112.5 12.0 %all-to-all-start.4 = ((f32[8,4,32,128]{3,2,1,0:T(8,128)}), f32[8,4,32,128]{3,2,1,0:T(8,128)S(1)}, u32[]{:S(2)}, u32[]{:S(2)}) async-start(f32[8,4,32,128]{3,2,1,0:T(8,128)} %bitcast.15), calls=%async_computation.4 | async-start | bytes 1048576 | tf_op jit(solution)/shard_map/all_to_all | solution.py:42
  116.0 8.6 %collective-permute-start.15 = (f32[4,32,128]{2,1,0:T(8,128)S(1)}, f32[4,32,128]{2,1,0:T(8,128)S(1)}, u32[]{:S(2)}, u32[]{:S(2)}) collective-permute-start(f32[4,32,128]{2,1,0:T(8,128)S(1)} %divide_subtract_fusion.2.refs_0_), channel_id=1, source_target_pairs={{0,1},{1,0},{2,3},{3,2},{4,5},{5,4},{6,7},{7,6},{8,9},{9,8},{10,11... | collective-permute-start | bytes 196616 | tf_op jit(solution)/shard_map/ppermute | solution.py:32
  118.6 8.3 %collective-permute-start.16 = (f32[4,32,128]{2,1,0:T(8,128)S(1)}, f32[4,32,128]{2,1,0:T(8,128)S(1)}, u32[]{:S(2)}, u32[]{:S(2)}) collective-permute-start(f32[4,32,128]{2,1,0:T(8,128)S(1)} %divide_subtract_fusion.2.refs_0_), channel_id=1, source_target_pairs={{0,4},{4,0},{1,5},{5,1},{2,6},{6,2},{3,7},{7,3},{8,12},{12,8},{9,1... | collective-permute-start | bytes 196616 | tf_op jit(solution)/shard_map/ppermute | solution.py:32
  119.7 9.8 %collective-permute-start.20 = (f32[4,32,128]{2,1,0:T(8,128)S(1)}, f32[4,32,128]{2,1,0:T(8,128)S(1)}, u32[]{:S(2)}, u32[]{:S(2)}) collective-permute-start(f32[4,32,128]{2,1,0:T(8,128)S(1)} %divide_subtract_fusion.2.refs_0_), channel_id=1, source_target_pairs={{0,5},{1,4},{4,1},{5,0},{2,7},{3,6},{6,3},{7,2},{8,13},{9,12},{12,... | collective-permute-start | bytes 196616 | tf_op jit(solution)/shard_map/ppermute | solution.py:36
  127.9 3.7 %collective-permute-start.18 = (f32[4,32,128]{2,1,0:T(8,128)S(1)}, f32[4,32,128]{2,1,0:T(8,128)S(1)}, u32[]{:S(2)}, u32[]{:S(2)}) collective-permute-start(f32[4,32,128]{2,1,0:T(8,128)S(1)} %subtract_divide_fusion.refs_0_), channel_id=1, source_target_pairs={{0,64},{64,0},{1,65},{65,1},{2,66},{66,2},{3,67},{67,3},{4,68},{68... | collective-permute-start | bytes 196616 | tf_op jit(solution)/shard_map/ppermute | solution.py:32
  128.6 4.5 %collective-permute-start.19 = (f32[4,32,128]{2,1,0:T(8,128)S(1)}, f32[4,32,128]{2,1,0:T(8,128)S(1)}, u32[]{:S(2)}, u32[]{:S(2)}) collective-permute-start(f32[4,32,128]{2,1,0:T(8,128)S(1)} %subtract_divide_fusion.refs_0_), channel_id=1, source_target_pairs={{0,96},{32,64},{64,32},{96,0},{1,97},{33,65},{65,33},{97,1},{2,98}... | collective-permute-start | bytes 196616 | tf_op jit(solution)/shard_map/ppermute | solution.py:36
  135.2 13.2 %all-to-all-start.5 = ((f32[8,4,32,128]{3,2,1,0:T(8,128)}), f32[8,4,32,128]{3,2,1,0:T(8,128)S(1)}, u32[]{:S(2)}, u32[]{:S(2)}) async-start(f32[8,4,32,128]{3,2,1,0:T(8,128)} %bitcast.16), calls=%async_computation.5 | async-start | bytes 1048576 | tf_op jit(solution)/shard_map/all_to_all | solution.py:42
  142.1 6.4 %collective-permute-start.21 = (f32[128,128]{1,0:T(8,128)}, f32[128,128]{1,0:T(8,128)S(1)}, u32[]{:S(2)}, u32[]{:S(2)}) collective-permute-start(f32[128,128]{1,0:T(8,128)} %gram.1), channel_id=1, source_target_pairs={{0,32},{32,0},{1,33},{33,1},{2,34},{34,2},{3,35},{35,3},{4,36},{36... | collective-permute-start | bytes 196616 | tf_op jit(solution)/shard_map/ppermute | solution.py:32
  142.6 5.9 %collective-permute-start.22 = (f32[128,128]{1,0:T(8,128)}, f32[128,128]{1,0:T(8,128)S(1)}, u32[]{:S(2)}, u32[]{:S(2)}) collective-permute-start(f32[128,128]{1,0:T(8,128)} %gram.1), channel_id=1, source_target_pairs={{0,64},{64,0},{1,65},{65,1},{2,66},{66,2},{3,67},{67,3},{4,68},{68... | collective-permute-start | bytes 196616 | tf_op jit(solution)/shard_map/ppermute | solution.py:32
  143.3 5.2 %collective-permute-start.23 = (f32[128,128]{1,0:T(8,128)}, f32[128,128]{1,0:T(8,128)S(1)}, u32[]{:S(2)}, u32[]{:S(2)}) collective-permute-start(f32[128,128]{1,0:T(8,128)} %gram.1), channel_id=1, source_target_pairs={{0,96},{32,64},{64,32},{96,0},{1,97},{33,65},{65,33},{97,1},{2,98}... | collective-permute-start | bytes 196616 | tf_op jit(solution)/shard_map/ppermute | solution.py:36
  149.3 5.4 %collective-permute-start.27 = (f32[128,128]{1,0:T(8,128)S(1)}, f32[128,128]{1,0:T(8,128)S(1)}, u32[]{:S(2)}, u32[]{:S(2)}) collective-permute-start(f32[128,128]{1,0:T(8,128)S(1)} %add_add_fusion.1), channel_id=1, source_target_pairs={{0,16},{16,0},{1,17},{17,1},{2,18},{18,2},{3,19},{19,3},{4,20},{20... | collective-permute-start | bytes 196616 | tf_op jit(solution)/shard_map/ppermute | solution.py:32
  153.0 3.7 %collective-permute-start.25 = (f32[4,32,128]{2,1,0:T(8,128)S(1)}, f32[4,32,128]{2,1,0:T(8,128)S(1)}, u32[]{:S(2)}, u32[]{:S(2)}) collective-permute-start(f32[4,32,128]{2,1,0:T(8,128)S(1)} %divide_subtract_fusion.1.refs_0_), channel_id=1, source_target_pairs={{0,64},{64,0},{1,65},{65,1},{2,66},{66,2},{3,67},{67,3},{4,68},{68... | collective-permute-start | bytes 196616 | tf_op jit(solution)/shard_map/ppermute | solution.py:32
  153.6 4.6 %collective-permute-start.26 = (f32[4,32,128]{2,1,0:T(8,128)S(1)}, f32[4,32,128]{2,1,0:T(8,128)S(1)}, u32[]{:S(2)}, u32[]{:S(2)}) collective-permute-start(f32[4,32,128]{2,1,0:T(8,128)S(1)} %divide_subtract_fusion.1.refs_0_), channel_id=1, source_target_pairs={{0,96},{32,64},{64,32},{96,0},{1,97},{33,65},{65,33},{97,1},{2,98}... | collective-permute-start | bytes 196616 | tf_op jit(solution)/shard_map/ppermute | solution.py:36
  160.4 11.9 %all-to-all-start.6 = ((f32[8,4,32,128]{3,2,1,0:T(8,128)}), f32[8,4,32,128]{3,2,1,0:T(8,128)S(1)}, u32[]{:S(2)}, u32[]{:S(2)}) async-start(f32[8,4,32,128]{3,2,1,0:T(8,128)} %bitcast.17), calls=%async_computation.6 | async-start | bytes 1048576 | tf_op jit(solution)/shard_map/all_to_all | solution.py:42
  164.0 8.9 %collective-permute-start.28 = (f32[128,128]{1,0:T(8,128)S(1)}, f32[128,128]{1,0:T(8,128)S(1)}, u32[]{:S(2)}, u32[]{:S(2)}) collective-permute-start(f32[128,128]{1,0:T(8,128)S(1)} %add.94), channel_id=1, source_target_pairs={{0,2},{2,0},{1,3},{3,1},{4,6},{6,4},{5,7},{7,5},{8,10},{10,8},{9,1... | collective-permute-start | bytes 196616 | tf_op jit(solution)/shard_map/ppermute | solution.py:32
  165.6 7.4 %collective-permute-start.29 = (f32[128,128]{1,0:T(8,128)S(1)}, f32[128,128]{1,0:T(8,128)S(1)}, u32[]{:S(2)}, u32[]{:S(2)}) collective-permute-start(f32[128,128]{1,0:T(8,128)S(1)} %add.94), channel_id=1, source_target_pairs={{0,8},{8,0},{1,9},{9,1},{2,10},{10,2},{3,11},{11,3},{4,12},{12,4},... | collective-permute-start | bytes 196616 | tf_op jit(solution)/shard_map/ppermute | solution.py:32
  166.8 8.2 %collective-permute-start.30 = (f32[128,128]{1,0:T(8,128)S(1)}, f32[128,128]{1,0:T(8,128)S(1)}, u32[]{:S(2)}, u32[]{:S(2)}) collective-permute-start(f32[128,128]{1,0:T(8,128)S(1)} %add.94), channel_id=1, source_target_pairs={{0,10},{2,8},{8,2},{10,0},{1,11},{3,9},{9,3},{11,1},{4,14},{6,12},... | collective-permute-start | bytes 196616 | tf_op jit(solution)/shard_map/ppermute | solution.py:36
  174.9 11.6 %collective-permute-start.31 = (f32[4,32,128]{2,1,0:T(8,128)S(1)}, f32[4,32,128]{2,1,0:T(8,128)S(1)}, u32[]{:S(2)}, u32[]{:S(2)}) collective-permute-start(f32[4,32,128]{2,1,0:T(8,128)S(1)} %divide_subtract_fusion.refs_0_), channel_id=1, source_target_pairs={{0,1},{1,0},{2,3},{3,2},{4,5},{5,4},{6,7},{7,6},{8,9},{9,8},{10,11... | collective-permute-start | bytes 196616 | tf_op jit(solution)/shard_map/ppermute | solution.py:32
  175.9 10.6 %collective-permute-start.32 = (f32[4,32,128]{2,1,0:T(8,128)S(1)}, f32[4,32,128]{2,1,0:T(8,128)S(1)}, u32[]{:S(2)}, u32[]{:S(2)}) collective-permute-start(f32[4,32,128]{2,1,0:T(8,128)S(1)} %divide_subtract_fusion.refs_0_), channel_id=1, source_target_pairs={{0,4},{4,0},{1,5},{5,1},{2,6},{6,2},{3,7},{7,3},{8,12},{12,8},{9,1... | collective-permute-start | bytes 196616 | tf_op jit(solution)/shard_map/ppermute | solution.py:32
  178.9 7.6 %collective-permute-start.33 = (f32[4,32,128]{2,1,0:T(8,128)S(1)}, f32[4,32,128]{2,1,0:T(8,128)S(1)}, u32[]{:S(2)}, u32[]{:S(2)}) collective-permute-start(f32[4,32,128]{2,1,0:T(8,128)S(1)} %divide_subtract_fusion.refs_0_), channel_id=1, source_target_pairs={{0,5},{1,4},{4,1},{5,0},{2,7},{3,6},{6,3},{7,2},{8,13},{9,12},{12,... | collective-permute-start | bytes 196616 | tf_op jit(solution)/shard_map/ppermute | solution.py:36
  190.3 4.2 %collective-permute-start.34 = (f32[72,128]{1,0:T(8,128)}, f32[72,128]{1,0:T(8,128)S(1)}, u32[]{:S(2)}, u32[]{:S(2)}) collective-permute-start(f32[72,128]{1,0:T(8,128)} %get-tuple-element.61), channel_id=1, source_target_pairs={{0,32},{32,0},{1,33},{33,1},{2,34},{34,2},{3,35},{35,3},{4,36},{36... | collective-permute-start | bytes 110600 | tf_op jit(solution)/shard_map/ppermute | solution.py:32
  (31 other events, 127.7 us)

commit v5 on v4

--- a/solution.py
+++ b/solution.py
@@ -18,6 +18,7 @@
 SCATTER = ("xlo", "zlo", "zhi")
 NS = 2 ** len(SPLIT)
 NM = 2 ** len(SCATTER)
+GRANT = pltpu.CompilerParams(vmem_limit_bytes=16 * 2**20)
 
 
 def digits(index, names):
@@ -64,7 +65,7 @@
     return pl.pallas_call(
         widen_kernel,
         out_shape=(wide, wide),
-        compiler_params=pltpu.CompilerParams(vmem_limit_bytes=32 * 2**20),
+        compiler_params=GRANT,
         name="widen",
     )(tiles)
 
@@ -76,7 +77,10 @@
 
 def turn_all(tiles):
     return pl.pallas_call(
-        turn_kernel, out_shape=jax.ShapeDtypeStruct(tiles.shape, tiles.dtype), name="turn"
+        turn_kernel,
+        out_shape=jax.ShapeDtypeStruct(tiles.shape, tiles.dtype),
+        compiler_params=GRANT,
+        name="turn",
     )(tiles)
 
 
@@ -98,7 +102,7 @@
         out_shape=jax.ShapeDtypeStruct((len(parts), slots, blk, blk), jnp.bfloat16),
         in_specs=[spec] * len(parts),
         out_specs=pl.BlockSpec((len(parts), step, blk, blk), lambda i: (0, i, 0, 0)),
-        compiler_params=pltpu.CompilerParams(vmem_limit_bytes=32 * 2**20),
+        compiler_params=GRANT,
         name="pack",
     )(*parts).reshape(-1, blk, blk)
 
@@ -113,21 +117,24 @@
     return (turn_all(tiles), pack([a_y, b_y, a_x, b_x], half), pack([a_xy, b_xy], half)), small
 
 
-def product_kernel(count, begun, start, own_ref, place_ref, source_ref, *refs):
-    v_refs, tile_refs, o_ref, parts = refs[:count], refs[count : -2 - begun], refs[-2], refs[-1]
-    blocks, width, blk = v_refs[0].shape
-    for i, v_ref in enumerate(v_refs):
-        v = v_ref[...]
-        high = v.astype(jnp.bfloat16)
-        rest = v - high.astype(jnp.float32)
-        middle = rest.astype(jnp.bfloat16)
-        low = (rest - middle.astype(jnp.float32)).astype(jnp.bfloat16)
-        at = slice(i * blocks, (i + 1) * blocks)
-        parts[at, 0:width, :] = high
-        parts[at, width : 2 * width, :] = middle
-        parts[at, 2 * width : 3 * width, :] = low
-    parts[count * blocks] = jnp.zeros(parts.shape[1:], jnp.bfloat16)
-    o_ref[...] = refs[-3][...] if begun else jnp.zeros_like(o_ref)
+def product_kernel(count, begun, rider, start, own_ref, place_ref, source_ref, *refs):
+    v_refs, refs, o_ref, parts = refs[:count], refs[count:-2], refs[-2], refs[-1]
+    tile_refs = refs[: len(refs) - begun - (rider == "cut")]
+    blocks, rows, blk = parts.shape
+    width = rows // 3
+    at = 0
+    for v_ref in v_refs:
+        for i in range((blocks - 1) // count):
+            v = v_ref[i, :width] if len(v_ref.shape) == 3 else v_ref[i * width : (i + 1) * width]
+            high = v.astype(jnp.bfloat16)
+            rest = v - high.astype(jnp.float32)
+            middle = rest.astype(jnp.bfloat16)
+            parts[at, 0:width, :] = high
+            parts[at, width : 2 * width, :] = middle
+            parts[at, 2 * width :, :] = (rest - middle.astype(jnp.float32)).astype(jnp.bfloat16)
+            at += 1
+    parts[at] = jnp.zeros(parts.shape[1:], jnp.bfloat16)
+    o_ref[...] = refs[-1][...] if begun else jnp.zeros_like(o_ref)
     slots = place_ref.shape[0] // NS
     at = start
     for tiles_ref in tile_refs:
@@ -140,22 +147,36 @@
                 (((1,), (0,)), ((), ())),
                 preferred_element_type=jnp.float32,
             )
-            o_ref[place_ref[slot]] += p[0:width] + p[width : 2 * width] + p[2 * width :]
-
-
-def product(own, place, source, vs, tiles, out_blocks, start=0, begun=None):
-    blocks, width, blk = vs[0].shape
+            place = place_ref[slot]
+            to = pl.ds(pl.multiple_of(place % NS * width, width), width)
+            o_ref[place // NS, to, :] += p[0:width] + p[width : 2 * width] + p[2 * width :]
+    members, total, _ = o_ref.shape
+    extra = total - NS * width
+    for m in range(members):
+        if rider == "cut":
+            o_ref[m, NS * width :, :] = refs[-1][m * extra : (m + 1) * extra, :]
+        if rider == "sum":
+            x = [r[NS * width :, :] for r in v_refs]
+            o_ref[m, NS * width :, :] = (x[0] + x[1]) + (x[2] + x[3])
+
+
+def product(own, place, source, vs, tiles, width, start=0, begun=None, cut=None, add=False):
+    blk = tiles[0].shape[-1]
+    blocks = 4 * NS
+    rider = "cut" if cut is not None else "sum" if add else None
+    extra = cut.shape[0] // NM if cut is not None else vs[0].shape[0] - NS * width if add else 0
     smem = pl.BlockSpec(memory_space=pltpu.SMEM)
     vmem = pl.BlockSpec(memory_space=pltpu.VMEM)
-    return pl.pallas_call(
-        functools.partial(product_kernel, len(vs), begun is not None, start),
-        out_shape=jax.ShapeDtypeStruct((out_blocks, width, blk), jnp.float32),
-        in_specs=[smem] * 3 + [vmem] * (len(vs) + len(tiles) + (begun is not None)),
+    last = [x for x in (begun, cut) if x is not None]
+    return pl.pallas_call(
+        functools.partial(product_kernel, len(vs), begun is not None, rider, start),
+        out_shape=jax.ShapeDtypeStruct((NM, NS * width + extra, blk), jnp.float32),
+        in_specs=[smem] * 3 + [vmem] * (len(vs) + len(tiles) + len(last)),
         out_specs=vmem,
-        scratch_shapes=[pltpu.VMEM((len(vs) * blocks + 1, 3 * width, blk), jnp.bfloat16)],
-        compiler_params=pltpu.CompilerParams(vmem_limit_bytes=32 * 2**20),
+        scratch_shapes=[pltpu.VMEM((blocks + 1, 3 * width, blk), jnp.bfloat16)],
+        compiler_params=GRANT,
         name="product",
-    )(own.reshape(1), place, source, *vs, *tiles, *([] if begun is None else [begun]))
+    )(own.reshape(1), place, source, *vs, *tiles, *last)
 
 
 def factor_solve(gram, right):
@@ -188,17 +209,25 @@
     return out
 
 
-def factor_kernel(gram_ref, o_ref):
-    size = gram_ref.shape[0]
+def factor_kernel(got_ref, o_ref):
+    size = o_ref.shape[0]
+    extra = size // got_ref.shape[0]
+    gram = jnp.concatenate([got_ref[m, got_ref.shape[1] - extra :, :] for m in range(got_ref.shape[0])], axis=0)
     lane = lax.broadcasted_iota(jnp.int32, (8, size), 1)
     sub = lax.broadcasted_iota(jnp.int32, (8, size), 0)
     identity = [jnp.where(lane == sub + 8 * r, 1.0, 0.0) for r in range(size // 8)]
-    for i, rows in enumerate(factor_solve(gram_ref[...], identity)):
+    for i, rows in enumerate(factor_solve(gram, identity)):
         o_ref[8 * i : 8 * i + 8, :] = rows
 
 
-def factor(gram):
-    return pl.pallas_call(factor_kernel, out_shape=jax.ShapeDtypeStruct(gram.shape, jnp.float32), name="factor")(gram)
+def factor(got):
+    size = got.shape[2]
+    return pl.pallas_call(
+        factor_kernel,
+        out_shape=jax.ShapeDtypeStruct((size, size), jnp.float32),
+        compiler_params=GRANT,
+        name="factor",
+    )(got)
 
 
 def fold(gram):
@@ -239,17 +268,18 @@
     return pl.pallas_call(
         functools.partial(finish_kernel, scale),
         out_shape=jax.ShapeDtypeStruct(x.shape[::-1], jnp.float32),
-        compiler_params=pltpu.CompilerParams(vmem_limit_bytes=32 * 2**20),
+        compiler_params=GRANT,
         name="finish",
     )(folded, x)
 
 
 def join(own, refs, x_ref):
+    blk = refs[0].shape[1]
+    width = x_ref.shape[0] // NS
     for i, r in enumerate(refs):
-        blocks, width, blk = r.shape
         rows = pl.ds(pl.multiple_of((own ^ i) * width, width), width)
-        for b in range(blocks):
-            x_ref[rows, b * blk : (b + 1) * blk] = r[b]
+        for b in range(NS):
+            x_ref[rows, b * blk : (b + 1) * blk] = r[b * width : (b + 1) * width]
 
 
 def inner(x):
@@ -263,14 +293,15 @@
 
 
 def gram(own, slices):
-    blocks, width, blk = slices[0].shape
-    width *= len(slices)
+    width, blk = slices[0].shape
+    blocks = NS
     vmem = pl.BlockSpec(memory_space=pltpu.VMEM)
     return pl.pallas_call(
         gram_kernel,
         out_shape=jax.ShapeDtypeStruct((width, width), jnp.float32),
         in_specs=[pl.BlockSpec(memory_space=pltpu.SMEM)] + [vmem] * len(slices),
         scratch_shapes=[pltpu.VMEM((width, blocks * blk), jnp.float32)],
+        compiler_params=GRANT,
         name="gram",
     )(own.reshape(1), *slices)
 
@@ -287,8 +318,8 @@
 
 
 def normal(own, inverse, slices):
-    blocks, width, blk = slices[0].shape
-    width *= len(slices)
+    width, blk = slices[0].shape
+    blocks = NS
     vmem = pl.BlockSpec(memory_space=pltpu.VMEM)
     return pl.pallas_call(
         normal_kernel,
@@ -301,7 +332,7 @@
             pltpu.VMEM((width, blocks * blk), jnp.float32),
             pltpu.VMEM((blocks, width, blk), jnp.float32),
         ],
-        compiler_params=pltpu.CompilerParams(vmem_limit_bytes=56 * 2**20),
+        compiler_params=GRANT,
         name="normal",
     )(own.reshape(1), inverse, *slices)
 
@@ -314,7 +345,11 @@
 def ends(bounds, width):
     row = jax.ShapeDtypeStruct((1, width), jnp.float32)
     return pl.pallas_call(
-        ends_kernel, out_shape=(row, row), in_specs=[pl.BlockSpec(memory_space=pltpu.SMEM)], name="ends"
+        ends_kernel,
+        out_shape=(row, row),
+        in_specs=[pl.BlockSpec(memory_space=pltpu.SMEM)],
+        compiler_params=GRANT,
+        name="ends",
     )(bounds)
 
 
@@ -336,9 +371,9 @@
     slices = jnp.concatenate([slices, jnp.broadcast_to(notes, (NS, *notes.shape))], axis=1)
     got = exchange(jnp.broadcast_to(slices, (4, *slices.shape)).reshape(4 * NS, *slices.shape[1:]), ROW + SPLIT)
     tile_sets, got = share_tiles(tiles, got)
-    begun = got[:, : width // NS]
+    begun = got
     got = lax.dynamic_index_in_dim(got.reshape(4, NS, *got.shape[1:]), own_row, 0, keepdims=False)
-    current = got[:, : width // NS]
+    current = got[:, : width // NS].reshape(width, blk)
     all_rows, all_cols = (got[:, width // NS + i, :slots].astype(jnp.int32) for i in range(2))
     live = all_rows >= 0
     member = jnp.arange(NS, dtype=jnp.int32)[:, None]
@@ -347,40 +382,36 @@
     place = jnp.where(live, digits(all_rows, SCATTER) * NS + digits(all_rows, SPLIT), 0).reshape(-1)
     early = sum(t.shape[0] for t in tile_sets[:-1])
 
-    def add_up(prods):
-        return jnp.sum(exchange(prods.reshape(NM, NS, width // NS, blk), SCATTER), axis=0)
-
-    def multiply(v, others):
-        return add_up(product(own, place, source, [v, *others], tile_sets, NM * NS))
-
-    def multiply_first(v):
-        prods = product(own, place, source_begun, [v], tile_sets[:-1], NM * NS)
-        return add_up(product(own, place, source_begun, [v], tile_sets[-1:], NM * NS, early, prods))
-
-    def apply(v):
-        return multiply(v, three(v, ROW))
+    part = width // NS
+
+    def multiply(v, others, **riders):
+        return exchange(product(own, place, source, [v, *others], tile_sets, part, **riders), SCATTER)
+
+    def multiply_first():
+        prods = product(own, place, source_begun, [begun], tile_sets[:-1], part)
+        return exchange(product(own, place, source_begun, [begun], tile_sets[-1:], part, early, prods), SCATTER)
+
+    def add_up(got):
+        return jnp.sum(got, axis=0)
 
     def add_three(x, others):
         return (x + others[0]) + (others[1] + others[2])
 
-    first = (multiply_first(begun) - centre * current) / half
-    second = 2.0 * (apply(first) - centre * first) / half - current
-    third = 2.0 * (apply(second) - centre * second) / half - first
+    current, centre, half = tie((current, centre, half))
+    first = (add_up(multiply_first()) - centre * current) / half
+    second = 2.0 * (add_up(multiply(first, three(first, ROW))) - centre * first) / half - current
+    third = 2.0 * (add_up(multiply(second, three(second, ROW))) - centre * second) / half - first
 
     current = third
-    first = (apply(current) - centre * current) / half
+    first = (add_up(multiply(current, three(current, ROW))) - centre * current) / half
     slices = three(current, SPLIT)
-    first, *slices[:2] = tie((first, *slices[:2]))
-    others, slices[2] = tie((three(first, ROW), slices[2]))
-    second = 2.0 * (multiply(first, others) - centre * first) / half - current
-    local = gram(own, [current, *slices])
-    second, sums = tie((second, three(local, ROW)))
-    local = add_three(local, sums)
-    others, other = tie((three(second, ROW), swap(local, "zhi")))
-    local = local + other
-    third = 2.0 * (multiply(second, others) - centre * second) / half - first
-    third, sums = tie((third, three(local, ("zlo", "xlo"))))
-    inverse = factor(add_three(local, sums))
+    others = three(first, ROW)
+    got = add_up(multiply(first, others, cut=gram(own, [current, *slices])))
+    second = 2.0 * (got[:width] - centre * first) / half - current
+    second = jnp.concatenate([second, got[width:]], axis=0)
+    got = multiply(second, three(second, ROW), add=True)
+    third = 2.0 * (add_up(got[:, :width]) - centre * second[:width]) / half - first
+    inverse = factor(got)
 
     block, local = normal(own, inverse, [third, *three(third, SPLIT)])
     local = add_three(local, three(local, ROW))

time: 215 us -> 203 us (0.944)
  blocking collectives: 46.2 us -> 60 us
  Pallas kernels: 31.8 us -> 23.9 us
  waiting for transfers between devices: 51.9 us -> 44.8 us
  starting transfers between devices: 70.6 us -> 65.9 us
  local copies, waits for them, and re-layouts: 10.5 us -> 6.24 us
    all_to_all x4 -> x5, blocking collectives: 46.2 us -> 60 us  [exchange(): return lax.all_to_all(x, names, 0, 0, tiled=True)]
    ppermute x27 -> x22, waiting for transfers between devices: 23.2 us -> 15.7 us  [swap(): return lax.ppermute(x, name, [(0, 1), (1, 0)])]
    all_to_all x4 -> x3, starting transfers between devices: 17.2 us -> 14 us  [exchange(): return lax.all_to_all(x, names, 0, 0, tiled=True)]
    unnamed x44 -> x24, local copies, waits for them, and re-layouts: 7.32 us -> 4.91 us
    ppermute x27 -> x22, starting transfers between devices: 41.7 us -> 39.8 us  [swap(): return lax.ppermute(x, name, [(0, 1), (1, 0)])]
    ppermute x10 -> x8, waiting for transfers between devices: 13 us -> 13.7 us  [three(): lax.ppermute(x, names, [(i, i ^ 3) for i in range(4)])]
    all_to_all x4 -> x3, waiting for transfers between devices: 15.8 us -> 15.3 us  [exchange(): return lax.all_to_all(x, names, 0, 0, tiled=True)]
    ppermute x10 -> x8, starting transfers between devices: 11.7 us -> 12.1 us  [three(): lax.ppermute(x, names, [(i, i ^ 3) for i in range(4)])]
  transfers between devices with their start and end apart: 41 -> 33, of which waited for: 21 -> 19; matrix products, arithmetic and copies ran while one was open for 2% -> 1% of each run, Pallas kernels for 6% -> 4%
where the time goes in v5:
time: 203 us; the launch traced here: 202 us
  starting transfers between devices  65.9 us (32%)
  blocking collectives  60 us (30%)
  waiting for transfers between devices  44.8 us (22%)
  Pallas kernels  23.9 us (12%)
  local copies, waits for them, and re-layouts  6.24 us (3%)
    all_to_all x5, blocking collectives, exchange(): return lax.all_to_all(x, names, 0, 0, tiled=True)  60 us
    ppermute x22, starting transfers between devices, swap(): return lax.ppermute(x, name, [(0, 1), (1, 0)])  39.8 us
    ppermute x22, waiting for transfers between devices, swap(): return lax.ppermute(x, name, [(0, 1), (1, 0)])  15.7 us
    all_to_all x3, waiting for transfers between devices, exchange(): return lax.all_to_all(x, names, 0, 0, tiled=True)  15.3 us
    all_to_all x3, starting transfers between devices, exchange(): return lax.all_to_all(x, names, 0, 0, tiled=True)  14 us
    ppermute x8, waiting for transfers between devices, three(): lax.ppermute(x, names, [(i, i ^ 3) for i in range(4)])  13.7 us
    ppermute x8, starting transfers between devices, three(): lax.ppermute(x, names, [(i, i ^ 3) for i in range(4)])  12.1 us
    pallas_call x7, Pallas kernels, product(): pl.pallas_call(functools.partial(product_kernel, len(vs), begun is not No...  10.4 us
  transfers between devices with their start and end apart: 33, of which 19 were waited for; matrix products, arithmetic and copies ran while one was open for 1% of the time, Pallas kernels for 4%

profile of v5, /device:TPU:1, one launch (start us, length us, event | category | flops | bytes accessed | tf_op | source)
XLA Modules:
  0.0 202.1 jit_solution(8573890414932291839)
XLA Ops:
  2.3 3.7 %collective-permute-start = (f32[1024,128]{1,0:T(8,128)S(1)}, f32[1024,128]{1,0:T(8,128)}, u32[]{:S(2)}, u32[]{:S(2)}) collective-permute-start(f32[1024,128]{1,0:T(8,128)S(1)} %get-tuple-element.21), channel_id=1, source_target_pairs={{0,1},{1,0},{2,3},{3,2},{4,5},{5,4},{6,7},{7,6},{8,9},{9,8},{10,11... | collective-permute-start | bytes 1572872 | tf_op jit(solution)/shard_map/ppermute | solution.py:33
  6.1 2.8 %collective-permute-start.2 = (f32[1024,128]{1,0:T(8,128)}, f32[1024,128]{1,0:T(8,128)}, u32[]{:S(2)}, u32[]{:S(2)}) collective-permute-start(f32[1024,128]{1,0:T(8,128)} %get-tuple-element.22), channel_id=1, source_target_pairs={{0,4},{4,0},{1,5},{5,1},{2,6},{6,2},{3,7},{7,3},{8,12},{12,8},{9,1... | collective-permute-start | bytes 1572872 | tf_op jit(solution)/shard_map/ppermute | solution.py:33
  10.9 4.7 %all-to-all-start = ((f32[16,40,128]{2,1,0:T(8,128)}), f32[16,40,128]{2,1,0:T(8,128)S(1)}, u32[]{:S(2)}, u32[]{:S(2)}) async-start(f32[16,40,128]{2,1,0:T(8,128)} %bitcast.5), calls=%async_computation | async-start | bytes 655360 | tf_op jit(solution)/shard_map/all_to_all | solution.py:43
  15.6 2.9 %collective-permute-start.4 = (f32[1024,128]{1,0:T(8,128)S(1)}, f32[1024,128]{1,0:T(8,128)S(1)}, u32[]{:S(2)}, u32[]{:S(2)}) collective-permute-start(f32[1024,128]{1,0:T(8,128)S(1)} %get-tuple-element.21), channel_id=1, source_target_pairs={{0,4},{4,0},{1,5},{5,1},{2,6},{6,2},{3,7},{7,3},{8,12},{12,8},{9,1... | collective-permute-start | bytes 1572872 | tf_op jit(solution)/shard_map/ppermute | solution.py:33
  18.5 2.7 %collective-permute-start.5 = (f32[1024,128]{1,0:T(8,128)}, f32[1024,128]{1,0:T(8,128)S(1)}, u32[]{:S(2)}, u32[]{:S(2)}) collective-permute-start(f32[1024,128]{1,0:T(8,128)} %get-tuple-element.22), channel_id=1, source_target_pairs={{0,1},{1,0},{2,3},{3,2},{4,5},{5,4},{6,7},{7,6},{8,9},{9,8},{10,11... | collective-permute-start | bytes 1572872 | tf_op jit(solution)/shard_map/ppermute | solution.py:33
  21.3 5.4 %all-to-all-done.refs_0_ = f32[16,40,128]{2,1,0:T(8,128)S(1)} async-done(((f32[16,40,128]{2,1,0:T(8,128)}), f32[16,40,128]{2,1,0:T(8,128)S(1)}, u32[]{:S(2)}, u32[]{:S(2)}) %all-to-all-start) | async-done | bytes 327712 | tf_op jit(solution)/shard_map/all_to_all | solution.py:43
  26.7 3.0 %collective-permute-start.1 = (f32[1024,128]{1,0:T(8,128)}, f32[1024,128]{1,0:T(8,128)S(1)}, u32[]{:S(2)}, u32[]{:S(2)}) collective-permute-start(f32[1024,128]{1,0:T(8,128)} %collective-permute-done.refs_0_), channel_id=1, source_target_pairs={{0,4},{4,0},{1,5},{5,1},{2,6},{6,2},{3,7},{7,3},{8,12},{12,8},{9,1... | collective-permute-start | bytes 1572872 | tf_op jit(solution)/shard_map/ppermute | solution.py:33
  32.2 2.8 %collective-permute-done.4.refs_2_ = f32[1024,128]{1,0:T(8,128)S(1)} collective-permute-done((f32[1024,128]{1,0:T(8,128)S(1)}, f32[1024,128]{1,0:T(8,128)S(1)}, u32[]{:S(2)}, u32[]{:S(2)}) %collective-permute-start.4) | collective-permute-done | bytes 524320 | tf_op jit(solution)/shard_map/ppermute | solution.py:33
  41.2 5.1 %collective-permute-done.1.refs_0_ = f32[1024,128]{1,0:T(8,128)S(1)} collective-permute-done((f32[1024,128]{1,0:T(8,128)}, f32[1024,128]{1,0:T(8,128)S(1)}, u32[]{:S(2)}, u32[]{:S(2)}) %collective-permute-start.1) | collective-permute-done | bytes 524320 | tf_op jit(solution)/shard_map/ppermute | solution.py:33
  48.3 5.8 %all-to-all-start.1 = ((f32[8,128,128]{2,1,0:T(8,128)}), f32[8,128,128]{2,1,0:T(8,128)S(1)}, u32[]{:S(2)}, u32[]{:S(2)}) async-start(f32[8,128,128]{2,1,0:T(8,128)} %product.8), calls=%async_computation.1 | async-start | bytes 1048576 | tf_op jit(solution)/shard_map/all_to_all | solution.py:43
  54.2 7.1 %all-to-all-done.1 = f32[8,128,128]{2,1,0:T(8,128)S(1)} async-done(((f32[8,128,128]{2,1,0:T(8,128)}), f32[8,128,128]{2,1,0:T(8,128)S(1)}, u32[]{:S(2)}, u32[]{:S(2)}) %all-to-all-start.1) | async-done | bytes 524320 | tf_op jit(solution)/shard_map/all_to_all | solution.py:43
  61.4 3.3 %collective-permute-start.6 = (f32[128,128]{1,0:T(8,128)S(1)}, f32[128,128]{1,0:T(8,128)S(1)}, u32[]{:S(2)}, u32[]{:S(2)}) collective-permute-start(f32[128,128]{1,0:T(8,128)S(1)} %subtract_divide_fusion.1.refs_0_), channel_id=1, source_target_pairs={{0,32},{32,0},{1,33},{33,1},{2,34},{34,2},{3,35},{35,3},{4,36},{36... | collective-permute-start | bytes 196616 | tf_op jit(solution)/shard_map/ppermute | solution.py:33
  66.4 1.9 collective-permute-done.7.refs_2_
  71.3 11.9 %all_to_all.40 = f32[8,128,128]{2,1,0:T(8,128)S(1)} all-to-all(f32[8,128,128]{2,1,0:T(8,128)S(1)} %product.9), channel_id=1, replica_groups=mesh['ylo'=2,'core'=2,'zhi'=2,'zlo'=2,'xhi'=2,'xlo'=2,'yhi'=2] {'xlo','z..., dimensions={0} | all-to-all | bytes 1048576 | tf_op jit(solution)/shard_map/all_to_all | solution.py:43
  83.6 3.1 %collective-permute-start.11 = (f32[128,128]{1,0:T(8,128)S(1)}, f32[128,128]{1,0:T(8,128)S(1)}, u32[]{:S(2)}, u32[]{:S(2)}) collective-permute-start(f32[128,128]{1,0:T(8,128)S(1)} %divide_subtract_fusion.2.refs_0_), channel_id=1, source_target_pairs={{0,96},{32,64},{64,32},{96,0},{1,97},{33,65},{65,33},{97,1},{2,98}... | collective-permute-start | bytes 196616 | tf_op jit(solution)/shard_map/ppermute | solution.py:37
  86.7 3.3 %collective-permute-done.11.refs_3_ = f32[128,128]{1,0:T(8,128)S(1)} collective-permute-done((f32[128,128]{1,0:T(8,128)S(1)}, f32[128,128]{1,0:T(8,128)S(1)}, u32[]{:S(2)}, u32[]{:S(2)}) %collective-permute-start.11) | collective-permute-done | bytes 65568 | tf_op jit(solution)/shard_map/ppermute | solution.py:37
  91.3 11.7 %all_to_all.41 = f32[8,128,128]{2,1,0:T(8,128)S(1)} all-to-all(f32[8,128,128]{2,1,0:T(8,128)S(1)} %product.10), channel_id=1, replica_groups=mesh['ylo'=2,'core'=2,'zhi'=2,'zlo'=2,'xhi'=2,'xlo'=2,'yhi'=2] {'xlo','z..., dimensions={0} | all-to-all | bytes 1048576 | tf_op jit(solution)/shard_map/all_to_all | solution.py:43
  106.5 1.9 collective-permute-done.13.refs_2_
  110.0 2.1 %product.11 = f32[8,128,128]{2,1,0:T(8,128)} custom-call(s32[1]{0:T(128)} %bitcast.own_ref, s32[64]{0:T(128)S(1)} %get-tuple-element.36.place_ref, s32[64]{0:T(128)S(1)} %get-tuple-element.35.source_ref, f32[128,128]{1,0:T(8,128)S(1)} %divide_subtract_fusion.1.refs_0_, f32[128,128]{1,0:T(8,128)S(1)} %collective-permute-done.12.refs_1_, ...), custom_call_target="tpu_custom_call" | custom-call | tf_op jit(solution)/shard_map/product/pallas_call | solution.py:171
  112.2 3.5 %all-to-all-start.4 = ((f32[8,128,128]{2,1,0:T(8,128)}), f32[8,128,128]{2,1,0:T(8,128)S(1)}, u32[]{:S(2)}, u32[]{:S(2)}) async-start(f32[8,128,128]{2,1,0:T(8,128)} %product.11), calls=%async_computation.4 | async-start | bytes 1048576 | tf_op jit(solution)/shard_map/all_to_all | solution.py:43
  115.7 2.6 %collective-permute-start.18 = (f32[128,128]{1,0:T(8,128)S(1)}, f32[128,128]{1,0:T(8,128)S(1)}, u32[]{:S(2)}, u32[]{:S(2)}) collective-permute-start(f32[128,128]{1,0:T(8,128)S(1)} %divide_subtract_fusion.1.refs_0_), channel_id=1, source_target_pairs={{0,1},{1,0},{2,3},{3,2},{4,5},{5,4},{6,7},{7,6},{8,9},{9,8},{10,11... | collective-permute-start | bytes 196616 | tf_op jit(solution)/shard_map/ppermute | solution.py:33
  121.4 2.8 %all-to-all-done.4 = f32[8,128,128]{2,1,0:T(8,128)S(1)} async-done(((f32[8,128,128]{2,1,0:T(8,128)}), f32[8,128,128]{2,1,0:T(8,128)S(1)}, u32[]{:S(2)}, u32[]{:S(2)}) %all-to-all-start.4) | async-done | bytes 524320 | tf_op jit(solution)/shard_map/all_to_all | solution.py:43
  124.3 1.8 collective-permute-start.15
  132.7 13.9 %all_to_all.42 = f32[8,144,128]{2,1,0:T(8,128)S(1)} all-to-all(f32[8,144,128]{2,1,0:T(8,128)S(1)} %product.12), channel_id=1, replica_groups=mesh['ylo'=2,'core'=2,'zhi'=2,'zlo'=2,'xhi'=2,'xlo'=2,'yhi'=2] {'xlo','z..., dimensions={0} | all-to-all | bytes 1179648 | tf_op jit(solution)/shard_map/all_to_all | solution.py:43
  146.7 1.9 collective-permute-start.21
  150.3 2.1 %collective-permute-done.22.refs_2_ = f32[144,128]{1,0:T(8,128)S(1)} collective-permute-done((f32[144,128]{1,0:T(8,128)S(1)}, f32[144,128]{1,0:T(8,128)S(1)}, u32[]{:S(2)}, u32[]{:S(2)}) %collective-permute-start.22) | collective-permute-done | bytes 73760 | tf_op jit(solution)/shard_map/ppermute | solution.py:33
  155.5 12.8 %all_to_all.43.got_ref = f32[8,144,128]{2,1,0:T(8,128)S(1)} all-to-all(f32[8,144,128]{2,1,0:T(8,128)S(1)} %product.13), channel_id=1, replica_groups=mesh['ylo'=2,'core'=2,'zhi'=2,'zlo'=2,'xhi'=2,'xlo'=2,'yhi'=2] {'xlo','z..., dimensions={0} | all-to-all | bytes 1179648 | tf_op jit(solution)/shard_map/all_to_all | solution.py:43
  170.1 2.5 %collective-permute-start.25 = (f32[128,128]{1,0:T(8,128)S(1)}, f32[128,128]{1,0:T(8,128)S(1)}, u32[]{:S(2)}, u32[]{:S(2)}) collective-permute-start(f32[128,128]{1,0:T(8,128)S(1)} %divide_subtract_fusion.refs_0_), channel_id=1, source_target_pairs={{0,4},{4,0},{1,5},{5,1},{2,6},{6,2},{3,7},{7,3},{8,12},{12,8},{9,1... | collective-permute-start | bytes 196616 | tf_op jit(solution)/shard_map/ppermute | solution.py:33
  174.1 3.9 %factor.1.inverse_ref = f32[128,128]{1,0:T(8,128)S(1)} custom-call(f32[8,144,128]{2,1,0:T(8,128)S(1)} %all_to_all.43.got_ref), custom_call_target="tpu_custom_call" | custom-call | tf_op jit(solution)/shard_map/factor/pallas_call | solution.py:225
  180.5 3.2 %collective-permute-start.27 = (f32[72,128]{1,0:T(8,128)S(1)}, f32[72,128]{1,0:T(8,128)S(1)}, u32[]{:S(2)}, u32[]{:S(2)}) collective-permute-start(f32[72,128]{1,0:T(8,128)S(1)} %get-tuple-element.29), channel_id=1, source_target_pairs={{0,32},{32,0},{1,33},{33,1},{2,34},{34,2},{3,35},{35,3},{4,36},{36... | collective-permute-start | bytes 110600 | tf_op jit(solution)/shard_map/ppermute | solution.py:33
  187.8 9.7 %all_to_all.44.folded_ref = f32[8,72,128]{2,1,0:T(8,128)S(1)} all-to-all(f32[8,72,128]{2,1,0:T(8,128)S(1)} %broadcast_in_dim.19), channel_id=1, replica_groups=mesh['ylo'=2,'core'=2,'zhi'=2,'zlo'=2,'xhi'=2,'xlo'=2,'yhi'=2] {'xlo','z..., dimensions={0} | all-to-all | bytes 589824 | tf_op jit(solution)/shard_map/all_to_all | solution.py:43
  197.5 4.7 %finish.1 = f32[128,128]{1,0:T(8,128)} custom-call(f32[8,72,128]{2,1,0:T(8,128)S(1)} %all_to_all.44.folded_ref, f32[128,128]{1,0:T(8,128)S(1)} %get-tuple-element.30.x_ref), custom_call_target="tpu_custom_call" | custom-call | tf_op jit(solution)/shard_map/finish/pallas_call | solution.py:268
  (114 shorter events, 51.4 us)
Async XLA Ops:
  2.3 24.4 %collective-permute-start = (f32[1024,128]{1,0:T(8,128)S(1)}, f32[1024,128]{1,0:T(8,128)}, u32[]{:S(2)}, u32[]{:S(2)}) collective-permute-start(f32[1024,128]{1,0:T(8,128)S(1)} %get-tuple-element.21), channel_id=1, source_target_pairs={{0,1},{1,0},{2,3},{3,2},{4,5},{5,4},{6,7},{7,6},{8,9},{9,8},{10,11... | collective-permute-start | bytes 1572872 | tf_op jit(solution)/shard_map/ppermute | solution.py:33
  6.1 23.7 %collective-permute-start.2 = (f32[1024,128]{1,0:T(8,128)}, f32[1024,128]{1,0:T(8,128)}, u32[]{:S(2)}, u32[]{:S(2)}) collective-permute-start(f32[1024,128]{1,0:T(8,128)} %get-tuple-element.22), channel_id=1, source_target_pairs={{0,4},{4,0},{1,5},{5,1},{2,6},{6,2},{3,7},{7,3},{8,12},{12,8},{9,1... | collective-permute-start | bytes 1572872 | tf_op jit(solution)/shard_map/ppermute | solution.py:33
  10.9 15.7 %all-to-all-start = ((f32[16,40,128]{2,1,0:T(8,128)}), f32[16,40,128]{2,1,0:T(8,128)S(1)}, u32[]{:S(2)}, u32[]{:S(2)}) async-start(f32[16,40,128]{2,1,0:T(8,128)} %bitcast.5), calls=%async_computation | async-start | bytes 655360 | tf_op jit(solution)/shard_map/all_to_all | solution.py:43
  15.6 19.3 %collective-permute-start.4 = (f32[1024,128]{1,0:T(8,128)S(1)}, f32[1024,128]{1,0:T(8,128)S(1)}, u32[]{:S(2)}, u32[]{:S(2)}) collective-permute-start(f32[1024,128]{1,0:T(8,128)S(1)} %get-tuple-element.21), channel_id=1, source_target_pairs={{0,4},{4,0},{1,5},{5,1},{2,6},{6,2},{3,7},{7,3},{8,12},{12,8},{9,1... | collective-permute-start | bytes 1572872 | tf_op jit(solution)/shard_map/ppermute | solution.py:33
  18.5 17.3 %collective-permute-start.5 = (f32[1024,128]{1,0:T(8,128)}, f32[1024,128]{1,0:T(8,128)S(1)}, u32[]{:S(2)}, u32[]{:S(2)}) collective-permute-start(f32[1024,128]{1,0:T(8,128)} %get-tuple-element.22), channel_id=1, source_target_pairs={{0,1},{1,0},{2,3},{3,2},{4,5},{5,4},{6,7},{7,6},{8,9},{9,8},{10,11... | collective-permute-start | bytes 1572872 | tf_op jit(solution)/shard_map/ppermute | solution.py:33
  26.7 19.5 %collective-permute-start.1 = (f32[1024,128]{1,0:T(8,128)}, f32[1024,128]{1,0:T(8,128)S(1)}, u32[]{:S(2)}, u32[]{:S(2)}) collective-permute-start(f32[1024,128]{1,0:T(8,128)} %collective-permute-done.refs_0_), channel_id=1, source_target_pairs={{0,4},{4,0},{1,5},{5,1},{2,6},{6,2},{3,7},{7,3},{8,12},{12,8},{9,1... | collective-permute-start | bytes 1572872 | tf_op jit(solution)/shard_map/ppermute | solution.py:33
  29.8 16.8 %collective-permute-start.3 = (f32[1024,128]{1,0:T(8,128)}, f32[1024,128]{1,0:T(8,128)S(1)}, u32[]{:S(2)}, u32[]{:S(2)}) collective-permute-start(f32[1024,128]{1,0:T(8,128)} %collective-permute-done.2.refs_3_), channel_id=1, source_target_pairs={{0,1},{1,0},{2,3},{3,2},{4,5},{5,4},{6,7},{7,6},{8,9},{9,8},{10,11... | collective-permute-start | bytes 1572872 | tf_op jit(solution)/shard_map/ppermute | solution.py:33
  48.3 13.0 %all-to-all-start.1 = ((f32[8,128,128]{2,1,0:T(8,128)}), f32[8,128,128]{2,1,0:T(8,128)S(1)}, u32[]{:S(2)}, u32[]{:S(2)}) async-start(f32[8,128,128]{2,1,0:T(8,128)} %product.8), calls=%async_computation.1 | async-start | bytes 1048576 | tf_op jit(solution)/shard_map/all_to_all | solution.py:43
  61.4 5.1 %collective-permute-start.6 = (f32[128,128]{1,0:T(8,128)S(1)}, f32[128,128]{1,0:T(8,128)S(1)}, u32[]{:S(2)}, u32[]{:S(2)}) collective-permute-start(f32[128,128]{1,0:T(8,128)S(1)} %subtract_divide_fusion.1.refs_0_), channel_id=1, source_target_pairs={{0,32},{32,0},{1,33},{33,1},{2,34},{34,2},{3,35},{35,3},{4,36},{36... | collective-permute-start | bytes 196616 | tf_op jit(solution)/shard_map/ppermute | solution.py:33
  64.7 3.6 %collective-permute-start.7 = (f32[128,128]{1,0:T(8,128)S(1)}, f32[128,128]{1,0:T(8,128)S(1)}, u32[]{:S(2)}, u32[]{:S(2)}) collective-permute-start(f32[128,128]{1,0:T(8,128)S(1)} %subtract_divide_fusion.1.refs_0_), channel_id=1, source_target_pairs={{0,64},{64,0},{1,65},{65,1},{2,66},{66,2},{3,67},{67,3},{4,68},{68... | collective-permute-start | bytes 196616 | tf_op jit(solution)/shard_map/ppermute | solution.py:33
  65.1 4.8 %collective-permute-start.8 = (f32[128,128]{1,0:T(8,128)S(1)}, f32[128,128]{1,0:T(8,128)S(1)}, u32[]{:S(2)}, u32[]{:S(2)}) collective-permute-start(f32[128,128]{1,0:T(8,128)S(1)} %subtract_divide_fusion.1.refs_0_), channel_id=1, source_target_pairs={{0,96},{32,64},{64,32},{96,0},{1,97},{33,65},{65,33},{97,1},{2,98}... | collective-permute-start | bytes 196616 | tf_op jit(solution)/shard_map/ppermute | solution.py:37
  83.2 3.4 %collective-permute-start.10 = (f32[128,128]{1,0:T(8,128)S(1)}, f32[128,128]{1,0:T(8,128)S(1)}, u32[]{:S(2)}, u32[]{:S(2)}) collective-permute-start(f32[128,128]{1,0:T(8,128)S(1)} %divide_subtract_fusion.2.refs_0_), channel_id=1, source_target_pairs={{0,64},{64,0},{1,65},{65,1},{2,66},{66,2},{3,67},{67,3},{4,68},{68... | collective-permute-start | bytes 196616 | tf_op jit(solution)/shard_map/ppermute | solution.py:33
  83.6 6.4 %collective-permute-start.11 = (f32[128,128]{1,0:T(8,128)S(1)}, f32[128,128]{1,0:T(8,128)S(1)}, u32[]{:S(2)}, u32[]{:S(2)}) collective-permute-start(f32[128,128]{1,0:T(8,128)S(1)} %divide_subtract_fusion.2.refs_0_), channel_id=1, source_target_pairs={{0,96},{32,64},{64,32},{96,0},{1,97},{33,65},{65,33},{97,1},{2,98}... | collective-permute-start | bytes 196616 | tf_op jit(solution)/shard_map/ppermute | solution.py:37
  86.6 3.4 %collective-permute-start.9 = (f32[128,128]{1,0:T(8,128)S(1)}, f32[128,128]{1,0:T(8,128)S(1)}, u32[]{:S(2)}, u32[]{:S(2)}) collective-permute-start(f32[128,128]{1,0:T(8,128)S(1)} %divide_subtract_fusion.2.refs_0_), channel_id=1, source_target_pairs={{0,32},{32,0},{1,33},{33,1},{2,34},{34,2},{3,35},{35,3},{4,36},{36... | collective-permute-start | bytes 196616 | tf_op jit(solution)/shard_map/ppermute | solution.py:33
  103.1 3.4 %collective-permute-start.12 = (f32[128,128]{1,0:T(8,128)S(1)}, f32[128,128]{1,0:T(8,128)S(1)}, u32[]{:S(2)}, u32[]{:S(2)}) collective-permute-start(f32[128,128]{1,0:T(8,128)S(1)} %divide_subtract_fusion.1.refs_0_), channel_id=1, source_target_pairs={{0,32},{32,0},{1,33},{33,1},{2,34},{34,2},{3,35},{35,3},{4,36},{36... | collective-permute-start | bytes 196616 | tf_op jit(solution)/shard_map/ppermute | solution.py:33
  104.8 3.6 %collective-permute-start.13 = (f32[128,128]{1,0:T(8,128)S(1)}, f32[128,128]{1,0:T(8,128)S(1)}, u32[]{:S(2)}, u32[]{:S(2)}) collective-permute-start(f32[128,128]{1,0:T(8,128)S(1)} %divide_subtract_fusion.1.refs_0_), channel_id=1, source_target_pairs={{0,64},{64,0},{1,65},{65,1},{2,66},{66,2},{3,67},{67,3},{4,68},{68... | collective-permute-start | bytes 196616 | tf_op jit(solution)/shard_map/ppermute | solution.py:33
  105.5 4.5 %collective-permute-start.14 = (f32[128,128]{1,0:T(8,128)S(1)}, f32[128,128]{1,0:T(8,128)S(1)}, u32[]{:S(2)}, u32[]{:S(2)}) collective-permute-start(f32[128,128]{1,0:T(8,128)S(1)} %divide_subtract_fusion.1.refs_0_), channel_id=1, source_target_pairs={{0,96},{32,64},{64,32},{96,0},{1,97},{33,65},{65,33},{97,1},{2,98}... | collective-permute-start | bytes 196616 | tf_op jit(solution)/shard_map/ppermute | solution.py:37
  112.2 12.0 %all-to-all-start.4 = ((f32[8,128,128]{2,1,0:T(8,128)}), f32[8,128,128]{2,1,0:T(8,128)S(1)}, u32[]{:S(2)}, u32[]{:S(2)}) async-start(f32[8,128,128]{2,1,0:T(8,128)} %product.11), calls=%async_computation.4 | async-start | bytes 1048576 | tf_op jit(solution)/shard_map/all_to_all | solution.py:43
  115.7 11.2 %collective-permute-start.18 = (f32[128,128]{1,0:T(8,128)S(1)}, f32[128,128]{1,0:T(8,128)S(1)}, u32[]{:S(2)}, u32[]{:S(2)}) collective-permute-start(f32[128,128]{1,0:T(8,128)S(1)} %divide_subtract_fusion.1.refs_0_), channel_id=1, source_target_pairs={{0,1},{1,0},{2,3},{3,2},{4,5},{5,4},{6,7},{7,6},{8,9},{9,8},{10,11... | collective-permute-start | bytes 196616 | tf_op jit(solution)/shard_map/ppermute | solution.py:33
  118.2 9.6 %collective-permute-start.19 = (f32[128,128]{1,0:T(8,128)S(1)}, f32[128,128]{1,0:T(8,128)S(1)}, u32[]{:S(2)}, u32[]{:S(2)}) collective-permute-start(f32[128,128]{1,0:T(8,128)S(1)} %divide_subtract_fusion.1.refs_0_), channel_id=1, source_target_pairs={{0,4},{4,0},{1,5},{5,1},{2,6},{6,2},{3,7},{7,3},{8,12},{12,8},{9,1... | collective-permute-start | bytes 196616 | tf_op jit(solution)/shard_map/ppermute | solution.py:33
  119.7 9.1 %collective-permute-start.20 = (f32[128,128]{1,0:T(8,128)S(1)}, f32[128,128]{1,0:T(8,128)S(1)}, u32[]{:S(2)}, u32[]{:S(2)}) collective-permute-start(f32[128,128]{1,0:T(8,128)S(1)} %divide_subtract_fusion.1.refs_0_), channel_id=1, source_target_pairs={{0,5},{1,4},{4,1},{5,0},{2,7},{3,6},{6,3},{7,2},{8,13},{9,12},{12,... | collective-permute-start | bytes 196616 | tf_op jit(solution)/shard_map/ppermute | solution.py:37
  124.3 5.0 %collective-permute-start.15 = (f32[128,128]{1,0:T(8,128)S(1)}, f32[128,128]{1,0:T(8,128)S(1)}, u32[]{:S(2)}, u32[]{:S(2)}) collective-permute-start(f32[128,128]{1,0:T(8,128)S(1)} %subtract_divide_fusion.refs_0_), channel_id=1, source_target_pairs={{0,32},{32,0},{1,33},{33,1},{2,34},{34,2},{3,35},{35,3},{4,36},{36... | collective-permute-start | bytes 196616 | tf_op jit(solution)/shard_map/ppermute | solution.py:33
  126.1 3.6 %collective-permute-start.16 = (f32[128,128]{1,0:T(8,128)S(1)}, f32[128,128]{1,0:T(8,128)S(1)}, u32[]{:S(2)}, u32[]{:S(2)}) collective-permute-start(f32[128,128]{1,0:T(8,128)S(1)} %subtract_divide_fusion.refs_0_), channel_id=1, source_target_pairs={{0,64},{64,0},{1,65},{65,1},{2,66},{66,2},{3,67},{67,3},{4,68},{68... | collective-permute-start | bytes 196616 | tf_op jit(solution)/shard_map/ppermute | solution.py:33
  126.9 4.5 %collective-permute-start.17 = (f32[128,128]{1,0:T(8,128)S(1)}, f32[128,128]{1,0:T(8,128)S(1)}, u32[]{:S(2)}, u32[]{:S(2)}) collective-permute-start(f32[128,128]{1,0:T(8,128)S(1)} %subtract_divide_fusion.refs_0_), channel_id=1, source_target_pairs={{0,96},{32,64},{64,32},{96,0},{1,97},{33,65},{65,33},{97,1},{2,98}... | collective-permute-start | bytes 196616 | tf_op jit(solution)/shard_map/ppermute | solution.py:37
  146.7 3.6 %collective-permute-start.21 = (f32[144,128]{1,0:T(8,128)S(1)}, f32[144,128]{1,0:T(8,128)S(1)}, u32[]{:S(2)}, u32[]{:S(2)}) collective-permute-start(f32[144,128]{1,0:T(8,128)S(1)} %pad_maximum_fusion.1.refs_0_), channel_id=1, source_target_pairs={{0,32},{32,0},{1,33},{33,1},{2,34},{34,2},{3,35},{35,3},{4,36},{36... | collective-permute-start | bytes 221192 | tf_op jit(solution)/shard_map/ppermute | solution.py:33
  148.5 3.8 %collective-permute-start.22 = (f32[144,128]{1,0:T(8,128)S(1)}, f32[144,128]{1,0:T(8,128)S(1)}, u32[]{:S(2)}, u32[]{:S(2)}) collective-permute-start(f32[144,128]{1,0:T(8,128)S(1)} %pad_maximum_fusion.1.refs_0_), channel_id=1, source_target_pairs={{0,64},{64,0},{1,65},{65,1},{2,66},{66,2},{3,67},{67,3},{4,68},{68... | collective-permute-start | bytes 221192 | tf_op jit(solution)/shard_map/ppermute | solution.py:33
  149.3 4.8 %collective-permute-start.23 = (f32[144,128]{1,0:T(8,128)S(1)}, f32[144,128]{1,0:T(8,128)S(1)}, u32[]{:S(2)}, u32[]{:S(2)}) collective-permute-start(f32[144,128]{1,0:T(8,128)S(1)} %pad_maximum_fusion.1.refs_0_), channel_id=1, source_target_pairs={{0,96},{32,64},{64,32},{96,0},{1,97},{33,65},{65,33},{97,1},{2,98}... | collective-permute-start | bytes 221192 | tf_op jit(solution)/shard_map/ppermute | solution.py:37
  168.3 9.6 %collective-permute-start.24 = (f32[128,128]{1,0:T(8,128)S(1)}, f32[128,128]{1,0:T(8,128)S(1)}, u32[]{:S(2)}, u32[]{:S(2)}) collective-permute-start(f32[128,128]{1,0:T(8,128)S(1)} %divide_subtract_fusion.refs_0_), channel_id=1, source_target_pairs={{0,1},{1,0},{2,3},{3,2},{4,5},{5,4},{6,7},{7,6},{8,9},{9,8},{10,11... | collective-permute-start | bytes 196616 | tf_op jit(solution)/shard_map/ppermute | solution.py:33
  170.1 7.8 %collective-permute-start.25 = (f32[128,128]{1,0:T(8,128)S(1)}, f32[128,128]{1,0:T(8,128)S(1)}, u32[]{:S(2)}, u32[]{:S(2)}) collective-permute-start(f32[128,128]{1,0:T(8,128)S(1)} %divide_subtract_fusion.refs_0_), channel_id=1, source_target_pairs={{0,4},{4,0},{1,5},{5,1},{2,6},{6,2},{3,7},{7,3},{8,12},{12,8},{9,1... | collective-permute-start | bytes 196616 | tf_op jit(solution)/shard_map/ppermute | solution.py:33
  172.6 7.0 %collective-permute-start.26 = (f32[128,128]{1,0:T(8,128)S(1)}, f32[128,128]{1,0:T(8,128)S(1)}, u32[]{:S(2)}, u32[]{:S(2)}) collective-permute-start(f32[128,128]{1,0:T(8,128)S(1)} %divide_subtract_fusion.refs_0_), channel_id=1, source_target_pairs={{0,5},{1,4},{4,1},{5,0},{2,7},{3,6},{6,3},{7,2},{8,13},{9,12},{12,... | collective-permute-start | bytes 196616 | tf_op jit(solution)/shard_map/ppermute | solution.py:37
  180.5 4.9 %collective-permute-start.27 = (f32[72,128]{1,0:T(8,128)S(1)}, f32[72,128]{1,0:T(8,128)S(1)}, u32[]{:S(2)}, u32[]{:S(2)}) collective-permute-start(f32[72,128]{1,0:T(8,128)S(1)} %get-tuple-element.29), channel_id=1, source_target_pairs={{0,32},{32,0},{1,33},{33,1},{2,34},{34,2},{3,35},{35,3},{4,36},{36... | collective-permute-start | bytes 110600 | tf_op jit(solution)/shard_map/ppermute | solution.py:33
  183.7 4.0 %collective-permute-start.29 = (f32[72,128]{1,0:T(8,128)S(1)}, f32[72,128]{1,0:T(8,128)S(1)}, u32[]{:S(2)}, u32[]{:S(2)}) collective-permute-start(f32[72,128]{1,0:T(8,128)S(1)} %get-tuple-element.29), channel_id=1, source_target_pairs={{0,96},{32,64},{64,32},{96,0},{1,97},{33,65},{65,33},{97,1},{2,98}... | collective-permute-start | bytes 110600 | tf_op jit(solution)/shard_map/ppermute | solution.py:37
  (13 other events, 58.0 us)

commit v6 on v5

--- a/solution.py
+++ b/solution.py
@@ -369,16 +369,17 @@
     notes = jnp.pad(jnp.stack([tile_rows, tile_cols]).astype(jnp.float32), ((0, 6), (0, blk - slots)))
     slices = start_block.T.reshape(NS, width // NS, blk)
     slices = jnp.concatenate([slices, jnp.broadcast_to(notes, (NS, *notes.shape))], axis=1)
-    got = exchange(jnp.broadcast_to(slices, (4, *slices.shape)).reshape(4 * NS, *slices.shape[1:]), ROW + SPLIT)
-    tile_sets, got = share_tiles(tiles, got)
-    begun = got
-    got = lax.dynamic_index_in_dim(got.reshape(4, NS, *got.shape[1:]), own_row, 0, keepdims=False)
+    near = exchange(jnp.concatenate([slices, slices], axis=0), ("ylo",) + SPLIT)
+    tile_sets, near = share_tiles(tiles, near)
+    begun = [near, swap(near, "core")]
+    got = lax.dynamic_index_in_dim(near.reshape(2, NS, *near.shape[1:]), lax.axis_index("ylo"), 0, keepdims=False)
     current = got[:, : width // NS].reshape(width, blk)
     all_rows, all_cols = (got[:, width // NS + i, :slots].astype(jnp.int32) for i in range(2))
     live = all_rows >= 0
     member = jnp.arange(NS, dtype=jnp.int32)[:, None]
     source = jnp.where(live, (all_cols ^ own_row) * NS + member, 4 * NS).reshape(-1)
-    source_begun = jnp.where(live, all_cols * NS + member, 4 * NS).reshape(-1)
+    column = (all_cols ^ lax.axis_index("core")) % 2 * 2 + all_cols // 2
+    source_begun = jnp.where(live, column * NS + member, 4 * NS).reshape(-1)
     place = jnp.where(live, digits(all_rows, SCATTER) * NS + digits(all_rows, SPLIT), 0).reshape(-1)
     early = sum(t.shape[0] for t in tile_sets[:-1])
 
@@ -387,9 +388,10 @@
     def multiply(v, others, **riders):
         return exchange(product(own, place, source, [v, *others], tile_sets, part, **riders), SCATTER)
 
-    def multiply_first():
-        prods = product(own, place, source_begun, [begun], tile_sets[:-1], part)
-        return exchange(product(own, place, source_begun, [begun], tile_sets[-1:], part, early, prods), SCATTER)
+    def multiply_first(small):
+        prods = product(own, place, source_begun, begun, tile_sets[:-1], part)
+        prods, small = tie((prods, small))
+        return small, exchange(product(own, place, source_begun, begun, tile_sets[-1:], part, early, prods), SCATTER)
 
     def add_up(got):
         return jnp.sum(got, axis=0)
@@ -397,8 +399,8 @@
     def add_three(x, others):
         return (x + others[0]) + (others[1] + others[2])
 
-    current, centre, half = tie((current, centre, half))
-    first = (add_up(multiply_first()) - centre * current) / half
+    (current, centre, half), got = multiply_first((current, centre, half))
+    first = (add_up(got) - centre * current) / half
     second = 2.0 * (add_up(multiply(first, three(first, ROW))) - centre * first) / half - current
     third = 2.0 * (add_up(multiply(second, three(second, ROW))) - centre * second) / half - first
 

time: 203 us -> 199 us (0.980)
  blocking collectives: 60 us -> 72.8 us
  waiting for transfers between devices: 44.8 us -> 35 us
  starting transfers between devices: 65.9 us -> 62.6 us
  local copies, waits for them, and re-layouts: 6.24 us -> 3.57 us
    all_to_all x5 -> x6, blocking collectives: 60 us -> 72.8 us  [exchange(): return lax.all_to_all(x, names, 0, 0, tiled=True)]
    all_to_all x3 -> x2, waiting for transfers between devices: 15.3 us -> 5.4 us  [exchange(): return lax.all_to_all(x, names, 0, 0, tiled=True)]
    all_to_all x3 -> x2, starting transfers between devices: 14 us -> 7 us  [exchange(): return lax.all_to_all(x, names, 0, 0, tiled=True)]
    ppermute x22 -> x23, waiting for transfers between devices: 15.7 us -> 19.4 us  [swap(): return lax.ppermute(x, name, [(0, 1), (1, 0)])]
    ppermute x22 -> x23, starting transfers between devices: 39.8 us -> 43.4 us  [swap(): return lax.ppermute(x, name, [(0, 1), (1, 0)])]
    ppermute x8, waiting for transfers between devices: 13.7 us -> 10.2 us  [three(): lax.ppermute(x, names, [(i, i ^ 3) for i in range(4)])]
    unnamed x24 -> x16, local copies, waits for them, and re-layouts: 4.91 us -> 3.07 us
  transfers between devices with their start and end apart: 33 -> 33, of which waited for: 19 -> 18; matrix products, arithmetic and copies ran while one was open for 1% -> 1% of each run, Pallas kernels for 4% -> 4%
where the time goes in v6:
time: 199 us; the launch traced here: 198 us
  blocking collectives  72.8 us (37%)
  starting transfers between devices  62.6 us (31%)
  waiting for transfers between devices  35 us (18%)
  Pallas kernels  23.2 us (12%)
  local copies, waits for them, and re-layouts  3.57 us (2%)
    all_to_all x6, blocking collectives, exchange(): return lax.all_to_all(x, names, 0, 0, tiled=True)  72.8 us
    ppermute x23, starting transfers between devices, swap(): return lax.ppermute(x, name, [(0, 1), (1, 0)])  43.4 us
    ppermute x23, waiting for transfers between devices, swap(): return lax.ppermute(x, name, [(0, 1), (1, 0)])  19.4 us
    ppermute x8, starting transfers between devices, three(): lax.ppermute(x, names, [(i, i ^ 3) for i in range(4)])  12.2 us
    ppermute x8, waiting for transfers between devices, three(): lax.ppermute(x, names, [(i, i ^ 3) for i in range(4)])  10.2 us
    pallas_call x7, Pallas kernels, product(): pl.pallas_call(functools.partial(product_kernel, len(vs), begun is not No...  9.7 us
    all_to_all x2, starting transfers between devices, exchange(): return lax.all_to_all(x, names, 0, 0, tiled=True)  7 us
    all_to_all x2, waiting for transfers between devices, exchange(): return lax.all_to_all(x, names, 0, 0, tiled=True)  5.4 us
  transfers between devices with their start and end apart: 33, of which 18 were waited for; matrix products, arithmetic and copies ran while one was open for 1% of the time, Pallas kernels for 4%

profile of v6, /device:TPU:1, one launch (start us, length us, event | category | flops | bytes accessed | tf_op | source)
XLA Modules:
  0.0 198.5 jit_solution(7310523059962868400)
XLA Ops:
  2.3 3.7 %collective-permute-start.1 = (f32[1024,128]{1,0:T(8,128)S(1)}, f32[1024,128]{1,0:T(8,128)S(1)}, u32[]{:S(2)}, u32[]{:S(2)}) collective-permute-start(f32[1024,128]{1,0:T(8,128)S(1)} %get-tuple-element.22), channel_id=1, source_target_pairs={{0,1},{1,0},{2,3},{3,2},{4,5},{5,4},{6,7},{7,6},{8,9},{9,8},{10,11... | collective-permute-start | bytes 1572872 | tf_op jit(solution)/shard_map/ppermute | solution.py:33
  6.1 2.8 %collective-permute-start.3 = (f32[1024,128]{1,0:T(8,128)}, f32[1024,128]{1,0:T(8,128)}, u32[]{:S(2)}, u32[]{:S(2)}) collective-permute-start(f32[1024,128]{1,0:T(8,128)} %get-tuple-element.23), channel_id=1, source_target_pairs={{0,4},{4,0},{1,5},{5,1},{2,6},{6,2},{3,7},{7,3},{8,12},{12,8},{9,1... | collective-permute-start | bytes 1572872 | tf_op jit(solution)/shard_map/ppermute | solution.py:33
  10.9 3.5 %all-to-all-start = ((f32[8,40,128]{2,1,0:T(8,128)}), f32[8,40,128]{2,1,0:T(8,128)S(1)}, u32[]{:S(2)}, u32[]{:S(2)}) async-start(f32[8,40,128]{2,1,0:T(8,128)} %maximum_maximum_fusion), calls=%async_computation | async-start | bytes 327680 | tf_op jit(solution)/shard_map/all_to_all | solution.py:43
  14.4 2.9 %collective-permute-start.5 = (f32[1024,128]{1,0:T(8,128)S(1)}, f32[1024,128]{1,0:T(8,128)S(1)}, u32[]{:S(2)}, u32[]{:S(2)}) collective-permute-start(f32[1024,128]{1,0:T(8,128)S(1)} %get-tuple-element.22), channel_id=1, source_target_pairs={{0,4},{4,0},{1,5},{5,1},{2,6},{6,2},{3,7},{7,3},{8,12},{12,8},{9,1... | collective-permute-start | bytes 1572872 | tf_op jit(solution)/shard_map/ppermute | solution.py:33
  17.3 2.7 %collective-permute-start.6 = (f32[1024,128]{1,0:T(8,128)}, f32[1024,128]{1,0:T(8,128)}, u32[]{:S(2)}, u32[]{:S(2)}) collective-permute-start(f32[1024,128]{1,0:T(8,128)} %get-tuple-element.23), channel_id=1, source_target_pairs={{0,1},{1,0},{2,3},{3,2},{4,5},{5,4},{6,7},{7,6},{8,9},{9,8},{10,11... | collective-permute-start | bytes 1572872 | tf_op jit(solution)/shard_map/ppermute | solution.py:33
  20.1 2.6 %all-to-all-done.refs_0_ = f32[8,40,128]{2,1,0:T(8,128)S(1)} async-done(((f32[8,40,128]{2,1,0:T(8,128)}), f32[8,40,128]{2,1,0:T(8,128)S(1)}, u32[]{:S(2)}, u32[]{:S(2)}) %all-to-all-start) | async-done | bytes 163872 | tf_op jit(solution)/shard_map/all_to_all | solution.py:43
  22.7 2.4 %collective-permute-start.2 = (f32[1024,128]{1,0:T(8,128)S(1)}, f32[1024,128]{1,0:T(8,128)S(1)}, u32[]{:S(2)}, u32[]{:S(2)}) collective-permute-start(f32[1024,128]{1,0:T(8,128)S(1)} %collective-permute-done.1.refs_0_), channel_id=1, source_target_pairs={{0,4},{4,0},{1,5},{5,1},{2,6},{6,2},{3,7},{7,3},{8,12},{12,8},{9,1... | collective-permute-start | bytes 1572872 | tf_op jit(solution)/shard_map/ppermute | solution.py:33
  27.2 3.8 %collective-permute-start = (f32[8,40,128]{2,1,0:T(8,128)S(1)}, f32[8,40,128]{2,1,0:T(8,128)S(1)}, u32[]{:S(2)}, u32[]{:S(2)}) collective-permute-start(f32[8,40,128]{2,1,0:T(8,128)S(1)} %all-to-all-done.refs_0_), channel_id=1, source_target_pairs={{0,32},{32,0},{1,33},{33,1},{2,34},{34,2},{3,35},{35,3},{4,36},{36... | collective-permute-start | bytes 491528 | tf_op jit(solution)/shard_map/ppermute | solution.py:33
  31.1 2.3 %collective-permute-done.5.refs_2_ = f32[1024,128]{1,0:T(8,128)S(1)} collective-permute-done((f32[1024,128]{1,0:T(8,128)S(1)}, f32[1024,128]{1,0:T(8,128)S(1)}, u32[]{:S(2)}, u32[]{:S(2)}) %collective-permute-start.5) | collective-permute-done | bytes 524320 | tf_op jit(solution)/shard_map/ppermute | solution.py:33
  37.7 6.8 %collective-permute-done.2.refs_0_ = f32[1024,128]{1,0:T(8,128)S(1)} collective-permute-done((f32[1024,128]{1,0:T(8,128)S(1)}, f32[1024,128]{1,0:T(8,128)S(1)}, u32[]{:S(2)}, u32[]{:S(2)}) %collective-permute-start.2) | collective-permute-done | bytes 524320 | tf_op jit(solution)/shard_map/ppermute | solution.py:33
  45.5 13.2 %all_to_all.40 = f32[8,128,128]{2,1,0:T(8,128)S(1)} all-to-all(f32[8,128,128]{2,1,0:T(8,128)S(1)} %product.8), channel_id=1, replica_groups=mesh['ylo'=2,'core'=2,'zhi'=2,'zlo'=2,'xhi'=2,'xlo'=2,'yhi'=2] {'xlo','z..., dimensions={0} | all-to-all | bytes 1048576 | tf_op jit(solution)/shard_map/all_to_all | solution.py:43
  58.8 3.3 %collective-permute-start.7 = (f32[128,128]{1,0:T(8,128)S(1)}, f32[128,128]{1,0:T(8,128)S(1)}, u32[]{:S(2)}, u32[]{:S(2)}) collective-permute-start(f32[128,128]{1,0:T(8,128)S(1)} %subtract_divide_fusion.1.refs_0_), channel_id=1, source_target_pairs={{0,32},{32,0},{1,33},{33,1},{2,34},{34,2},{3,35},{35,3},{4,36},{36... | collective-permute-start | bytes 196616 | tf_op jit(solution)/shard_map/ppermute | solution.py:33
  63.8 1.9 collective-permute-done.8.refs_2_
  68.7 11.6 %all_to_all.41 = f32[8,128,128]{2,1,0:T(8,128)S(1)} all-to-all(f32[8,128,128]{2,1,0:T(8,128)S(1)} %product.9), channel_id=1, replica_groups=mesh['ylo'=2,'core'=2,'zhi'=2,'zlo'=2,'xhi'=2,'xlo'=2,'yhi'=2] {'xlo','z..., dimensions={0} | all-to-all | bytes 1048576 | tf_op jit(solution)/shard_map/all_to_all | solution.py:43
  83.9 1.9 collective-permute-done.11.refs_2_
  88.7 11.6 %all_to_all.42 = f32[8,128,128]{2,1,0:T(8,128)S(1)} all-to-all(f32[8,128,128]{2,1,0:T(8,128)S(1)} %product.10), channel_id=1, replica_groups=mesh['ylo'=2,'core'=2,'zhi'=2,'zlo'=2,'xhi'=2,'xlo'=2,'yhi'=2] {'xlo','z..., dimensions={0} | all-to-all | bytes 1048576 | tf_op jit(solution)/shard_map/all_to_all | solution.py:43
  103.9 1.9 collective-permute-done.14.refs_2_
  107.4 2.2 %product.11 = f32[8,128,128]{2,1,0:T(8,128)} custom-call(s32[1]{0:T(128)} %bitcast.own_ref, s32[64]{0:T(128)S(1)} %get-tuple-element.35.place_ref, s32[64]{0:T(128)S(1)} %get-tuple-element.34.source_ref, f32[128,128]{1,0:T(8,128)S(1)} %divide_subtract_fusion.1.refs_0_, f32[128,128]{1,0:T(8,128)S(1)} %collective-permute-done.13.refs_1_, ...), custom_call_target="tpu_custom_call" | custom-call | tf_op jit(solution)/shard_map/product/pallas_call | solution.py:171
  109.6 3.5 %all-to-all-start.4 = ((f32[8,128,128]{2,1,0:T(8,128)}), f32[8,128,128]{2,1,0:T(8,128)S(1)}, u32[]{:S(2)}, u32[]{:S(2)}) async-start(f32[8,128,128]{2,1,0:T(8,128)} %product.11), calls=%async_computation.4 | async-start | bytes 1048576 | tf_op jit(solution)/shard_map/all_to_all | solution.py:43
  113.9 2.5 %collective-permute-start.20 = (f32[128,128]{1,0:T(8,128)S(1)}, f32[128,128]{1,0:T(8,128)S(1)}, u32[]{:S(2)}, u32[]{:S(2)}) collective-permute-start(f32[128,128]{1,0:T(8,128)S(1)} %divide_subtract_fusion.1.refs_0_), channel_id=1, source_target_pairs={{0,4},{4,0},{1,5},{5,1},{2,6},{6,2},{3,7},{7,3},{8,12},{12,8},{9,1... | collective-permute-start | bytes 196616 | tf_op jit(solution)/shard_map/ppermute | solution.py:33
  116.4 2.4 %collective-permute-start.21 = (f32[128,128]{1,0:T(8,128)S(1)}, f32[128,128]{1,0:T(8,128)S(1)}, u32[]{:S(2)}, u32[]{:S(2)}) collective-permute-start(f32[128,128]{1,0:T(8,128)S(1)} %divide_subtract_fusion.1.refs_0_), channel_id=1, source_target_pairs={{0,5},{1,4},{4,1},{5,0},{2,7},{3,6},{6,3},{7,2},{8,13},{9,12},{12,... | collective-permute-start | bytes 196616 | tf_op jit(solution)/shard_map/ppermute | solution.py:37
  118.8 2.8 %all-to-all-done.4 = f32[8,128,128]{2,1,0:T(8,128)S(1)} async-done(((f32[8,128,128]{2,1,0:T(8,128)}), f32[8,128,128]{2,1,0:T(8,128)S(1)}, u32[]{:S(2)}, u32[]{:S(2)}) %all-to-all-start.4) | async-done | bytes 524320 | tf_op jit(solution)/shard_map/all_to_all | solution.py:43
  130.0 13.9 %all_to_all.43 = f32[8,144,128]{2,1,0:T(8,128)S(1)} all-to-all(f32[8,144,128]{2,1,0:T(8,128)S(1)} %product.12), channel_id=1, replica_groups=mesh['ylo'=2,'core'=2,'zhi'=2,'zlo'=2,'xhi'=2,'xlo'=2,'yhi'=2] {'xlo','z..., dimensions={0} | all-to-all | bytes 1179648 | tf_op jit(solution)/shard_map/all_to_all | solution.py:43
  144.0 1.9 collective-permute-start.22
  147.6 2.1 %collective-permute-done.23.refs_2_ = f32[144,128]{1,0:T(8,128)S(1)} collective-permute-done((f32[144,128]{1,0:T(8,128)S(1)}, f32[144,128]{1,0:T(8,128)S(1)}, u32[]{:S(2)}, u32[]{:S(2)}) %collective-permute-start.23) | collective-permute-done | bytes 73760 | tf_op jit(solution)/shard_map/ppermute | solution.py:33
  152.8 12.8 %all_to_all.44.got_ref = f32[8,144,128]{2,1,0:T(8,128)S(1)} all-to-all(f32[8,144,128]{2,1,0:T(8,128)S(1)} %product.13), channel_id=1, replica_groups=mesh['ylo'=2,'core'=2,'zhi'=2,'zlo'=2,'xhi'=2,'xlo'=2,'yhi'=2] {'xlo','z..., dimensions={0} | all-to-all | bytes 1179648 | tf_op jit(solution)/shard_map/all_to_all | solution.py:43
  166.8 2.2 %collective-permute-start.26 = (f32[128,128]{1,0:T(8,128)S(1)}, f32[128,128]{1,0:T(8,128)S(1)}, u32[]{:S(2)}, u32[]{:S(2)}) collective-permute-start(f32[128,128]{1,0:T(8,128)S(1)} %divide_subtract_fusion.refs_0_), channel_id=1, source_target_pairs={{0,4},{4,0},{1,5},{5,1},{2,6},{6,2},{3,7},{7,3},{8,12},{12,8},{9,1... | collective-permute-start | bytes 196616 | tf_op jit(solution)/shard_map/ppermute | solution.py:33
  169.0 2.5 %collective-permute-start.27 = (f32[128,128]{1,0:T(8,128)S(1)}, f32[128,128]{1,0:T(8,128)S(1)}, u32[]{:S(2)}, u32[]{:S(2)}) collective-permute-start(f32[128,128]{1,0:T(8,128)S(1)} %divide_subtract_fusion.refs_0_), channel_id=1, source_target_pairs={{0,5},{1,4},{4,1},{5,0},{2,7},{3,6},{6,3},{7,2},{8,13},{9,12},{12,... | collective-permute-start | bytes 196616 | tf_op jit(solution)/shard_map/ppermute | solution.py:37
  171.4 3.8 %factor.1.inverse_ref = f32[128,128]{1,0:T(8,128)S(1)} custom-call(f32[8,144,128]{2,1,0:T(8,128)S(1)} %all_to_all.44.got_ref), custom_call_target="tpu_custom_call" | custom-call | tf_op jit(solution)/shard_map/factor/pallas_call | solution.py:225
  176.9 3.1 %collective-permute-start.28 = (f32[72,128]{1,0:T(8,128)S(1)}, f32[72,128]{1,0:T(8,128)S(1)}, u32[]{:S(2)}, u32[]{:S(2)}) collective-permute-start(f32[72,128]{1,0:T(8,128)S(1)} %get-tuple-element.31), channel_id=1, source_target_pairs={{0,32},{32,0},{1,33},{33,1},{2,34},{34,2},{3,35},{35,3},{4,36},{36... | collective-permute-start | bytes 110600 | tf_op jit(solution)/shard_map/ppermute | solution.py:33
  184.1 9.7 %all_to_all.45.folded_ref = f32[8,72,128]{2,1,0:T(8,128)S(1)} all-to-all(f32[8,72,128]{2,1,0:T(8,128)S(1)} %broadcast_in_dim.15), channel_id=1, replica_groups=mesh['ylo'=2,'core'=2,'zhi'=2,'zlo'=2,'xhi'=2,'xlo'=2,'yhi'=2] {'xlo','z..., dimensions={0} | all-to-all | bytes 589824 | tf_op jit(solution)/shard_map/all_to_all | solution.py:43
  193.8 4.7 %finish.1 = f32[128,128]{1,0:T(8,128)} custom-call(f32[8,72,128]{2,1,0:T(8,128)S(1)} %all_to_all.45.folded_ref, f32[128,128]{1,0:T(8,128)S(1)} %get-tuple-element.32.x_ref), custom_call_target="tpu_custom_call" | custom-call | tf_op jit(solution)/shard_map/finish/pallas_call | solution.py:268
  (106 shorter events, 49.3 us)
Async XLA Ops:
  2.3 20.3 %collective-permute-start.1 = (f32[1024,128]{1,0:T(8,128)S(1)}, f32[1024,128]{1,0:T(8,128)S(1)}, u32[]{:S(2)}, u32[]{:S(2)}) collective-permute-start(f32[1024,128]{1,0:T(8,128)S(1)} %get-tuple-element.22), channel_id=1, source_target_pairs={{0,1},{1,0},{2,3},{3,2},{4,5},{5,4},{6,7},{7,6},{8,9},{9,8},{10,11... | collective-permute-start | bytes 1572872 | tf_op jit(solution)/shard_map/ppermute | solution.py:33
  6.1 18.9 %collective-permute-start.3 = (f32[1024,128]{1,0:T(8,128)}, f32[1024,128]{1,0:T(8,128)}, u32[]{:S(2)}, u32[]{:S(2)}) collective-permute-start(f32[1024,128]{1,0:T(8,128)} %get-tuple-element.23), channel_id=1, source_target_pairs={{0,4},{4,0},{1,5},{5,1},{2,6},{6,2},{3,7},{7,3},{8,12},{12,8},{9,1... | collective-permute-start | bytes 1572872 | tf_op jit(solution)/shard_map/ppermute | solution.py:33
  10.9 11.7 %all-to-all-start = ((f32[8,40,128]{2,1,0:T(8,128)}), f32[8,40,128]{2,1,0:T(8,128)S(1)}, u32[]{:S(2)}, u32[]{:S(2)}) async-start(f32[8,40,128]{2,1,0:T(8,128)} %maximum_maximum_fusion), calls=%async_computation | async-start | bytes 327680 | tf_op jit(solution)/shard_map/all_to_all | solution.py:43
  14.4 19.0 %collective-permute-start.5 = (f32[1024,128]{1,0:T(8,128)S(1)}, f32[1024,128]{1,0:T(8,128)S(1)}, u32[]{:S(2)}, u32[]{:S(2)}) collective-permute-start(f32[1024,128]{1,0:T(8,128)S(1)} %get-tuple-element.22), channel_id=1, source_target_pairs={{0,4},{4,0},{1,5},{5,1},{2,6},{6,2},{3,7},{7,3},{8,12},{12,8},{9,1... | collective-permute-start | bytes 1572872 | tf_op jit(solution)/shard_map/ppermute | solution.py:33
  17.3 16.9 %collective-permute-start.6 = (f32[1024,128]{1,0:T(8,128)}, f32[1024,128]{1,0:T(8,128)}, u32[]{:S(2)}, u32[]{:S(2)}) collective-permute-start(f32[1024,128]{1,0:T(8,128)} %get-tuple-element.23), channel_id=1, source_target_pairs={{0,1},{1,0},{2,3},{3,2},{4,5},{5,4},{6,7},{7,6},{8,9},{9,8},{10,11... | collective-permute-start | bytes 1572872 | tf_op jit(solution)/shard_map/ppermute | solution.py:33
  22.7 21.8 %collective-permute-start.2 = (f32[1024,128]{1,0:T(8,128)S(1)}, f32[1024,128]{1,0:T(8,128)S(1)}, u32[]{:S(2)}, u32[]{:S(2)}) collective-permute-start(f32[1024,128]{1,0:T(8,128)S(1)} %collective-permute-done.1.refs_0_), channel_id=1, source_target_pairs={{0,4},{4,0},{1,5},{5,1},{2,6},{6,2},{3,7},{7,3},{8,12},{12,8},{9,1... | collective-permute-start | bytes 1572872 | tf_op jit(solution)/shard_map/ppermute | solution.py:33
  25.0 19.5 %collective-permute-start.4 = (f32[1024,128]{1,0:T(8,128)}, f32[1024,128]{1,0:T(8,128)S(1)}, u32[]{:S(2)}, u32[]{:S(2)}) collective-permute-start(f32[1024,128]{1,0:T(8,128)} %collective-permute-done.3.refs_3_), channel_id=1, source_target_pairs={{0,1},{1,0},{2,3},{3,2},{4,5},{5,4},{6,7},{7,6},{8,9},{9,8},{10,11... | collective-permute-start | bytes 1572872 | tf_op jit(solution)/shard_map/ppermute | solution.py:33
  27.2 9.3 %collective-permute-start = (f32[8,40,128]{2,1,0:T(8,128)S(1)}, f32[8,40,128]{2,1,0:T(8,128)S(1)}, u32[]{:S(2)}, u32[]{:S(2)}) collective-permute-start(f32[8,40,128]{2,1,0:T(8,128)S(1)} %all-to-all-done.refs_0_), channel_id=1, source_target_pairs={{0,32},{32,0},{1,33},{33,1},{2,34},{34,2},{3,35},{35,3},{4,36},{36... | collective-permute-start | bytes 491528 | tf_op jit(solution)/shard_map/ppermute | solution.py:33
  58.8 5.0 %collective-permute-start.7 = (f32[128,128]{1,0:T(8,128)S(1)}, f32[128,128]{1,0:T(8,128)S(1)}, u32[]{:S(2)}, u32[]{:S(2)}) collective-permute-start(f32[128,128]{1,0:T(8,128)S(1)} %subtract_divide_fusion.1.refs_0_), channel_id=1, source_target_pairs={{0,32},{32,0},{1,33},{33,1},{2,34},{34,2},{3,35},{35,3},{4,36},{36... | collective-permute-start | bytes 196616 | tf_op jit(solution)/shard_map/ppermute | solution.py:33
  62.1 3.6 %collective-permute-start.8 = (f32[128,128]{1,0:T(8,128)S(1)}, f32[128,128]{1,0:T(8,128)S(1)}, u32[]{:S(2)}, u32[]{:S(2)}) collective-permute-start(f32[128,128]{1,0:T(8,128)S(1)} %subtract_divide_fusion.1.refs_0_), channel_id=1, source_target_pairs={{0,64},{64,0},{1,65},{65,1},{2,66},{66,2},{3,67},{67,3},{4,68},{68... | collective-permute-start | bytes 196616 | tf_op jit(solution)/shard_map/ppermute | solution.py:33
  62.5 4.8 %collective-permute-start.9 = (f32[128,128]{1,0:T(8,128)S(1)}, f32[128,128]{1,0:T(8,128)S(1)}, u32[]{:S(2)}, u32[]{:S(2)}) collective-permute-start(f32[128,128]{1,0:T(8,128)S(1)} %subtract_divide_fusion.1.refs_0_), channel_id=1, source_target_pairs={{0,96},{32,64},{64,32},{96,0},{1,97},{33,65},{65,33},{97,1},{2,98}... | collective-permute-start | bytes 196616 | tf_op jit(solution)/shard_map/ppermute | solution.py:37
  80.3 3.5 %collective-permute-start.10 = (f32[128,128]{1,0:T(8,128)S(1)}, f32[128,128]{1,0:T(8,128)S(1)}, u32[]{:S(2)}, u32[]{:S(2)}) collective-permute-start(f32[128,128]{1,0:T(8,128)S(1)} %divide_subtract_fusion.2.refs_0_), channel_id=1, source_target_pairs={{0,32},{32,0},{1,33},{33,1},{2,34},{34,2},{3,35},{35,3},{4,36},{36... | collective-permute-start | bytes 196616 | tf_op jit(solution)/shard_map/ppermute | solution.py:33
  82.1 3.6 %collective-permute-start.11 = (f32[128,128]{1,0:T(8,128)S(1)}, f32[128,128]{1,0:T(8,128)S(1)}, u32[]{:S(2)}, u32[]{:S(2)}) collective-permute-start(f32[128,128]{1,0:T(8,128)S(1)} %divide_subtract_fusion.2.refs_0_), channel_id=1, source_target_pairs={{0,64},{64,0},{1,65},{65,1},{2,66},{66,2},{3,67},{67,3},{4,68},{68... | collective-permute-start | bytes 196616 | tf_op jit(solution)/shard_map/ppermute | solution.py:33
  82.6 4.8 %collective-permute-start.12 = (f32[128,128]{1,0:T(8,128)S(1)}, f32[128,128]{1,0:T(8,128)S(1)}, u32[]{:S(2)}, u32[]{:S(2)}) collective-permute-start(f32[128,128]{1,0:T(8,128)S(1)} %divide_subtract_fusion.2.refs_0_), channel_id=1, source_target_pairs={{0,96},{32,64},{64,32},{96,0},{1,97},{33,65},{65,33},{97,1},{2,98}... | collective-permute-start | bytes 196616 | tf_op jit(solution)/shard_map/ppermute | solution.py:37
  100.4 3.5 %collective-permute-start.13 = (f32[128,128]{1,0:T(8,128)S(1)}, f32[128,128]{1,0:T(8,128)S(1)}, u32[]{:S(2)}, u32[]{:S(2)}) collective-permute-start(f32[128,128]{1,0:T(8,128)S(1)} %divide_subtract_fusion.1.refs_0_), channel_id=1, source_target_pairs={{0,32},{32,0},{1,33},{33,1},{2,34},{34,2},{3,35},{35,3},{4,36},{36... | collective-permute-start | bytes 196616 | tf_op jit(solution)/shard_map/ppermute | solution.py:33
  102.1 3.6 %collective-permute-start.14 = (f32[128,128]{1,0:T(8,128)S(1)}, f32[128,128]{1,0:T(8,128)S(1)}, u32[]{:S(2)}, u32[]{:S(2)}) collective-permute-start(f32[128,128]{1,0:T(8,128)S(1)} %divide_subtract_fusion.1.refs_0_), channel_id=1, source_target_pairs={{0,64},{64,0},{1,65},{65,1},{2,66},{66,2},{3,67},{67,3},{4,68},{68... | collective-permute-start | bytes 196616 | tf_op jit(solution)/shard_map/ppermute | solution.py:33
  102.7 4.7 %collective-permute-start.15 = (f32[128,128]{1,0:T(8,128)S(1)}, f32[128,128]{1,0:T(8,128)S(1)}, u32[]{:S(2)}, u32[]{:S(2)}) collective-permute-start(f32[128,128]{1,0:T(8,128)S(1)} %divide_subtract_fusion.1.refs_0_), channel_id=1, source_target_pairs={{0,96},{32,64},{64,32},{96,0},{1,97},{33,65},{65,33},{97,1},{2,98}... | collective-permute-start | bytes 196616 | tf_op jit(solution)/shard_map/ppermute | solution.py:37
  109.6 12.1 %all-to-all-start.4 = ((f32[8,128,128]{2,1,0:T(8,128)}), f32[8,128,128]{2,1,0:T(8,128)S(1)}, u32[]{:S(2)}, u32[]{:S(2)}) async-start(f32[8,128,128]{2,1,0:T(8,128)} %product.11), calls=%async_computation.4 | async-start | bytes 1048576 | tf_op jit(solution)/shard_map/all_to_all | solution.py:43
  113.1 11.1 %collective-permute-start.19 = (f32[128,128]{1,0:T(8,128)S(1)}, f32[128,128]{1,0:T(8,128)S(1)}, u32[]{:S(2)}, u32[]{:S(2)}) collective-permute-start(f32[128,128]{1,0:T(8,128)S(1)} %divide_subtract_fusion.1.refs_0_), channel_id=1, source_target_pairs={{0,1},{1,0},{2,3},{3,2},{4,5},{5,4},{6,7},{7,6},{8,9},{9,8},{10,11... | collective-permute-start | bytes 196616 | tf_op jit(solution)/shard_map/ppermute | solution.py:33
  113.9 11.3 %collective-permute-start.20 = (f32[128,128]{1,0:T(8,128)S(1)}, f32[128,128]{1,0:T(8,128)S(1)}, u32[]{:S(2)}, u32[]{:S(2)}) collective-permute-start(f32[128,128]{1,0:T(8,128)S(1)} %divide_subtract_fusion.1.refs_0_), channel_id=1, source_target_pairs={{0,4},{4,0},{1,5},{5,1},{2,6},{6,2},{3,7},{7,3},{8,12},{12,8},{9,1... | collective-permute-start | bytes 196616 | tf_op jit(solution)/shard_map/ppermute | solution.py:33
  116.4 9.0 %collective-permute-start.21 = (f32[128,128]{1,0:T(8,128)S(1)}, f32[128,128]{1,0:T(8,128)S(1)}, u32[]{:S(2)}, u32[]{:S(2)}) collective-permute-start(f32[128,128]{1,0:T(8,128)S(1)} %divide_subtract_fusion.1.refs_0_), channel_id=1, source_target_pairs={{0,5},{1,4},{4,1},{5,0},{2,7},{3,6},{6,3},{7,2},{8,13},{9,12},{12,... | collective-permute-start | bytes 196616 | tf_op jit(solution)/shard_map/ppermute | solution.py:37
  121.7 4.1 %collective-permute-start.16 = (f32[128,128]{1,0:T(8,128)S(1)}, f32[128,128]{1,0:T(8,128)S(1)}, u32[]{:S(2)}, u32[]{:S(2)}) collective-permute-start(f32[128,128]{1,0:T(8,128)S(1)} %subtract_divide_fusion.refs_0_), channel_id=1, source_target_pairs={{0,32},{32,0},{1,33},{33,1},{2,34},{34,2},{3,35},{35,3},{4,36},{36... | collective-permute-start | bytes 196616 | tf_op jit(solution)/shard_map/ppermute | solution.py:33
  123.4 3.6 %collective-permute-start.17 = (f32[128,128]{1,0:T(8,128)S(1)}, f32[128,128]{1,0:T(8,128)S(1)}, u32[]{:S(2)}, u32[]{:S(2)}) collective-permute-start(f32[128,128]{1,0:T(8,128)S(1)} %subtract_divide_fusion.refs_0_), channel_id=1, source_target_pairs={{0,64},{64,0},{1,65},{65,1},{2,66},{66,2},{3,67},{67,3},{4,68},{68... | collective-permute-start | bytes 196616 | tf_op jit(solution)/shard_map/ppermute | solution.py:33
  124.2 4.5 %collective-permute-start.18 = (f32[128,128]{1,0:T(8,128)S(1)}, f32[128,128]{1,0:T(8,128)S(1)}, u32[]{:S(2)}, u32[]{:S(2)}) collective-permute-start(f32[128,128]{1,0:T(8,128)S(1)} %subtract_divide_fusion.refs_0_), channel_id=1, source_target_pairs={{0,96},{32,64},{64,32},{96,0},{1,97},{33,65},{65,33},{97,1},{2,98}... | collective-permute-start | bytes 196616 | tf_op jit(solution)/shard_map/ppermute | solution.py:37
  144.0 3.6 %collective-permute-start.22 = (f32[144,128]{1,0:T(8,128)S(1)}, f32[144,128]{1,0:T(8,128)S(1)}, u32[]{:S(2)}, u32[]{:S(2)}) collective-permute-start(f32[144,128]{1,0:T(8,128)S(1)} %pad_maximum_fusion.refs_0_), channel_id=1, source_target_pairs={{0,32},{32,0},{1,33},{33,1},{2,34},{34,2},{3,35},{35,3},{4,36},{36... | collective-permute-start | bytes 221192 | tf_op jit(solution)/shard_map/ppermute | solution.py:33
  145.9 3.8 %collective-permute-start.23 = (f32[144,128]{1,0:T(8,128)S(1)}, f32[144,128]{1,0:T(8,128)S(1)}, u32[]{:S(2)}, u32[]{:S(2)}) collective-permute-start(f32[144,128]{1,0:T(8,128)S(1)} %pad_maximum_fusion.refs_0_), channel_id=1, source_target_pairs={{0,64},{64,0},{1,65},{65,1},{2,66},{66,2},{3,67},{67,3},{4,68},{68... | collective-permute-start | bytes 221192 | tf_op jit(solution)/shard_map/ppermute | solution.py:33
  146.7 4.8 %collective-permute-start.24 = (f32[144,128]{1,0:T(8,128)S(1)}, f32[144,128]{1,0:T(8,128)S(1)}, u32[]{:S(2)}, u32[]{:S(2)}) collective-permute-start(f32[144,128]{1,0:T(8,128)S(1)} %pad_maximum_fusion.refs_0_), channel_id=1, source_target_pairs={{0,96},{32,64},{64,32},{96,0},{1,97},{33,65},{65,33},{97,1},{2,98}... | collective-permute-start | bytes 221192 | tf_op jit(solution)/shard_map/ppermute | solution.py:37
  165.7 9.6 %collective-permute-start.25 = (f32[128,128]{1,0:T(8,128)S(1)}, f32[128,128]{1,0:T(8,128)S(1)}, u32[]{:S(2)}, u32[]{:S(2)}) collective-permute-start(f32[128,128]{1,0:T(8,128)S(1)} %divide_subtract_fusion.refs_0_), channel_id=1, source_target_pairs={{0,1},{1,0},{2,3},{3,2},{4,5},{5,4},{6,7},{7,6},{8,9},{9,8},{10,11... | collective-permute-start | bytes 196616 | tf_op jit(solution)/shard_map/ppermute | solution.py:33
  166.8 8.5 %collective-permute-start.26 = (f32[128,128]{1,0:T(8,128)S(1)}, f32[128,128]{1,0:T(8,128)S(1)}, u32[]{:S(2)}, u32[]{:S(2)}) collective-permute-start(f32[128,128]{1,0:T(8,128)S(1)} %divide_subtract_fusion.refs_0_), channel_id=1, source_target_pairs={{0,4},{4,0},{1,5},{5,1},{2,6},{6,2},{3,7},{7,3},{8,12},{12,8},{9,1... | collective-permute-start | bytes 196616 | tf_op jit(solution)/shard_map/ppermute | solution.py:33
  169.0 7.0 %collective-permute-start.27 = (f32[128,128]{1,0:T(8,128)S(1)}, f32[128,128]{1,0:T(8,128)S(1)}, u32[]{:S(2)}, u32[]{:S(2)}) collective-permute-start(f32[128,128]{1,0:T(8,128)S(1)} %divide_subtract_fusion.refs_0_), channel_id=1, source_target_pairs={{0,5},{1,4},{4,1},{5,0},{2,7},{3,6},{6,3},{7,2},{8,13},{9,12},{12,... | collective-permute-start | bytes 196616 | tf_op jit(solution)/shard_map/ppermute | solution.py:37
  176.9 4.9 %collective-permute-start.28 = (f32[72,128]{1,0:T(8,128)S(1)}, f32[72,128]{1,0:T(8,128)S(1)}, u32[]{:S(2)}, u32[]{:S(2)}) collective-permute-start(f32[72,128]{1,0:T(8,128)S(1)} %get-tuple-element.31), channel_id=1, source_target_pairs={{0,32},{32,0},{1,33},{33,1},{2,34},{34,2},{3,35},{35,3},{4,36},{36... | collective-permute-start | bytes 110600 | tf_op jit(solution)/shard_map/ppermute | solution.py:33
  180.0 4.0 %collective-permute-start.30 = (f32[72,128]{1,0:T(8,128)S(1)}, f32[72,128]{1,0:T(8,128)S(1)}, u32[]{:S(2)}, u32[]{:S(2)}) collective-permute-start(f32[72,128]{1,0:T(8,128)S(1)} %get-tuple-element.31), channel_id=1, source_target_pairs={{0,96},{32,64},{64,32},{96,0},{1,97},{33,65},{65,33},{97,1},{2,98}... | collective-permute-start | bytes 110600 | tf_op jit(solution)/shard_map/ppermute | solution.py:37
  (9 other events, 44.4 us)

commit v7 on v6

--- a/solution.py
+++ b/solution.py
@@ -34,7 +34,7 @@
 
 
 def three(x, names):
-    return [swap(x, names[1]), swap(x, names[0]), lax.ppermute(x, names, [(i, i ^ 3) for i in range(4)])]
+    return [lax.ppermute(x, names, [(i, i ^ 3) for i in range(4)]), swap(x, names[0]), swap(x, names[1])]
 
 
 def exchange(x, names):
@@ -277,7 +277,7 @@
     blk = refs[0].shape[1]
     width = x_ref.shape[0] // NS
     for i, r in enumerate(refs):
-        rows = pl.ds(pl.multiple_of((own ^ i) * width, width), width)
+        rows = pl.ds(pl.multiple_of((own ^ (4 - i) % 4) * width, width), width)
         for b in range(NS):
             x_ref[rows, b * blk : (b + 1) * blk] = r[b * width : (b + 1) * width]
 
@@ -377,7 +377,7 @@
     all_rows, all_cols = (got[:, width // NS + i, :slots].astype(jnp.int32) for i in range(2))
     live = all_rows >= 0
     member = jnp.arange(NS, dtype=jnp.int32)[:, None]
-    source = jnp.where(live, (all_cols ^ own_row) * NS + member, 4 * NS).reshape(-1)
+    source = jnp.where(live, (4 - (all_cols ^ own_row)) % 4 * NS + member, 4 * NS).reshape(-1)
     column = (all_cols ^ lax.axis_index("core")) % 2 * 2 + all_cols // 2
     source_begun = jnp.where(live, column * NS + member, 4 * NS).reshape(-1)
     place = jnp.where(live, digits(all_rows, SCATTER) * NS + digits(all_rows, SPLIT), 0).reshape(-1)

time: 199 us -> 195 us (0.980)
  waiting for transfers between devices: 35 us -> 33 us
    ppermute x23, starting transfers between devices: 43.4 us -> 30.7 us  [swap(): return lax.ppermute(x, name, [(0, 1), (1, 0)])]
    ppermute x8, starting transfers between devices: 12.2 us -> 23.7 us  [three(): lax.ppermute(x, names, [(i, i ^ 3) for i in range(4)])]
  transfers between devices with their start and end apart: 33 -> 33, of which waited for: 18 -> 17; matrix products, arithmetic and copies ran while one was open for 1% -> 1% of each run, Pallas kernels for 4% -> 4%
where the time goes in v7:
time: 195 us; the launch traced here: 194 us
  blocking collectives  71.5 us (37%)
  starting transfers between devices  61.4 us (31%)
  waiting for transfers between devices  33 us (17%)
  Pallas kernels  23.2 us (12%)
  local copies, waits for them, and re-layouts  3.57 us (2%)
    all_to_all x6, blocking collectives, exchange(): return lax.all_to_all(x, names, 0, 0, tiled=True)  71.5 us
    ppermute x23, starting transfers between devices, swap(): return lax.ppermute(x, name, [(0, 1), (1, 0)])  30.7 us
    ppermute x8, starting transfers between devices, three(): lax.ppermute(x, names, [(i, i ^ 3) for i in range(4)])  23.7 us
    ppermute x23, waiting for transfers between devices, swap(): return lax.ppermute(x, name, [(0, 1), (1, 0)])  19.2 us
    pallas_call x7, Pallas kernels, product(): pl.pallas_call(functools.partial(product_kernel, len(vs), begun is not No...  9.69 us
    ppermute x8, waiting for transfers between devices, three(): lax.ppermute(x, names, [(i, i ^ 3) for i in range(4)])  8.5 us
    all_to_all x2, starting transfers between devices, exchange(): return lax.all_to_all(x, names, 0, 0, tiled=True)  7 us
    all_to_all x2, waiting for transfers between devices, exchange(): return lax.all_to_all(x, names, 0, 0, tiled=True)  5.29 us
  transfers between devices with their start and end apart: 33, of which 17 were waited for; matrix products, arithmetic and copies ran while one was open for 1% of the time, Pallas kernels for 4%

profile of v7, /device:TPU:1, one launch (start us, length us, event | category | flops | bytes accessed | tf_op | source)
XLA Modules:
  0.0 194.0 jit_solution(17701645761578444518)
XLA Ops:
  2.3 3.7 %collective-permute-start.1 = (f32[1024,128]{1,0:T(8,128)S(1)}, f32[1024,128]{1,0:T(8,128)S(1)}, u32[]{:S(2)}, u32[]{:S(2)}) collective-permute-start(f32[1024,128]{1,0:T(8,128)S(1)} %get-tuple-element.22), channel_id=1, source_target_pairs={{0,1},{1,0},{2,3},{3,2},{4,5},{5,4},{6,7},{7,6},{8,9},{9,8},{10,11... | collective-permute-start | bytes 1572872 | tf_op jit(solution)/shard_map/ppermute | solution.py:33
  6.1 2.8 %collective-permute-start.3 = (f32[1024,128]{1,0:T(8,128)}, f32[1024,128]{1,0:T(8,128)}, u32[]{:S(2)}, u32[]{:S(2)}) collective-permute-start(f32[1024,128]{1,0:T(8,128)} %get-tuple-element.23), channel_id=1, source_target_pairs={{0,4},{4,0},{1,5},{5,1},{2,6},{6,2},{3,7},{7,3},{8,12},{12,8},{9,1... | collective-permute-start | bytes 1572872 | tf_op jit(solution)/shard_map/ppermute | solution.py:33
  10.9 3.5 %all-to-all-start = ((f32[8,40,128]{2,1,0:T(8,128)}), f32[8,40,128]{2,1,0:T(8,128)S(1)}, u32[]{:S(2)}, u32[]{:S(2)}) async-start(f32[8,40,128]{2,1,0:T(8,128)} %maximum_maximum_fusion), calls=%async_computation | async-start | bytes 327680 | tf_op jit(solution)/shard_map/all_to_all | solution.py:43
  14.4 2.9 %collective-permute-start.5 = (f32[1024,128]{1,0:T(8,128)S(1)}, f32[1024,128]{1,0:T(8,128)S(1)}, u32[]{:S(2)}, u32[]{:S(2)}) collective-permute-start(f32[1024,128]{1,0:T(8,128)S(1)} %get-tuple-element.22), channel_id=1, source_target_pairs={{0,4},{4,0},{1,5},{5,1},{2,6},{6,2},{3,7},{7,3},{8,12},{12,8},{9,1... | collective-permute-start | bytes 1572872 | tf_op jit(solution)/shard_map/ppermute | solution.py:33
  17.3 2.7 %collective-permute-start.6 = (f32[1024,128]{1,0:T(8,128)}, f32[1024,128]{1,0:T(8,128)}, u32[]{:S(2)}, u32[]{:S(2)}) collective-permute-start(f32[1024,128]{1,0:T(8,128)} %get-tuple-element.23), channel_id=1, source_target_pairs={{0,1},{1,0},{2,3},{3,2},{4,5},{5,4},{6,7},{7,6},{8,9},{9,8},{10,11... | collective-permute-start | bytes 1572872 | tf_op jit(solution)/shard_map/ppermute | solution.py:33
  20.1 2.6 %all-to-all-done.refs_0_ = f32[8,40,128]{2,1,0:T(8,128)S(1)} async-done(((f32[8,40,128]{2,1,0:T(8,128)}), f32[8,40,128]{2,1,0:T(8,128)S(1)}, u32[]{:S(2)}, u32[]{:S(2)}) %all-to-all-start) | async-done | bytes 163872 | tf_op jit(solution)/shard_map/all_to_all | solution.py:43
  22.7 2.4 %collective-permute-start.2 = (f32[1024,128]{1,0:T(8,128)S(1)}, f32[1024,128]{1,0:T(8,128)S(1)}, u32[]{:S(2)}, u32[]{:S(2)}) collective-permute-start(f32[1024,128]{1,0:T(8,128)S(1)} %collective-permute-done.1.refs_0_), channel_id=1, source_target_pairs={{0,4},{4,0},{1,5},{5,1},{2,6},{6,2},{3,7},{7,3},{8,12},{12,8},{9,1... | collective-permute-start | bytes 1572872 | tf_op jit(solution)/shard_map/ppermute | solution.py:33
  27.2 3.8 %collective-permute-start = (f32[8,40,128]{2,1,0:T(8,128)S(1)}, f32[8,40,128]{2,1,0:T(8,128)S(1)}, u32[]{:S(2)}, u32[]{:S(2)}) collective-permute-start(f32[8,40,128]{2,1,0:T(8,128)S(1)} %all-to-all-done.refs_0_), channel_id=1, source_target_pairs={{0,32},{32,0},{1,33},{33,1},{2,34},{34,2},{3,35},{35,3},{4,36},{36... | collective-permute-start | bytes 491528 | tf_op jit(solution)/shard_map/ppermute | solution.py:33
  31.1 2.3 %collective-permute-done.5.refs_2_ = f32[1024,128]{1,0:T(8,128)S(1)} collective-permute-done((f32[1024,128]{1,0:T(8,128)S(1)}, f32[1024,128]{1,0:T(8,128)S(1)}, u32[]{:S(2)}, u32[]{:S(2)}) %collective-permute-start.5) | collective-permute-done | bytes 524320 | tf_op jit(solution)/shard_map/ppermute | solution.py:33
  37.7 6.8 %collective-permute-done.2.refs_0_ = f32[1024,128]{1,0:T(8,128)S(1)} collective-permute-done((f32[1024,128]{1,0:T(8,128)S(1)}, f32[1024,128]{1,0:T(8,128)S(1)}, u32[]{:S(2)}, u32[]{:S(2)}) %collective-permute-start.2) | collective-permute-done | bytes 524320 | tf_op jit(solution)/shard_map/ppermute | solution.py:33
  45.5 13.2 %all_to_all.40 = f32[8,128,128]{2,1,0:T(8,128)S(1)} all-to-all(f32[8,128,128]{2,1,0:T(8,128)S(1)} %product.8), channel_id=1, replica_groups=mesh['ylo'=2,'core'=2,'zhi'=2,'zlo'=2,'xhi'=2,'xlo'=2,'yhi'=2] {'xlo','z..., dimensions={0} | all-to-all | bytes 1048576 | tf_op jit(solution)/shard_map/all_to_all | solution.py:43
  58.8 3.6 %collective-permute-start.7 = (f32[128,128]{1,0:T(8,128)S(1)}, f32[128,128]{1,0:T(8,128)S(1)}, u32[]{:S(2)}, u32[]{:S(2)}) collective-permute-start(f32[128,128]{1,0:T(8,128)S(1)} %subtract_divide_fusion.1.refs_0_), channel_id=1, source_target_pairs={{0,96},{32,64},{64,32},{96,0},{1,97},{33,65},{65,33},{97,1},{2,98}... | collective-permute-start | bytes 196616 | tf_op jit(solution)/shard_map/ppermute | solution.py:37
  64.3 2.4 %collective-permute-done.8.refs_2_ = f32[128,128]{1,0:T(8,128)S(1)} collective-permute-done((f32[128,128]{1,0:T(8,128)S(1)}, f32[128,128]{1,0:T(8,128)S(1)}, u32[]{:S(2)}, u32[]{:S(2)}) %collective-permute-start.8) | collective-permute-done | bytes 65568 | tf_op jit(solution)/shard_map/ppermute | solution.py:33
  68.1 11.4 %all_to_all.41 = f32[8,128,128]{2,1,0:T(8,128)S(1)} all-to-all(f32[8,128,128]{2,1,0:T(8,128)S(1)} %product.9), channel_id=1, replica_groups=mesh['ylo'=2,'core'=2,'zhi'=2,'zlo'=2,'xhi'=2,'xlo'=2,'yhi'=2] {'xlo','z..., dimensions={0} | all-to-all | bytes 1048576 | tf_op jit(solution)/shard_map/all_to_all | solution.py:43
  79.5 2.8 %collective-permute-start.10 = (f32[128,128]{1,0:T(8,128)S(1)}, f32[128,128]{1,0:T(8,128)S(1)}, u32[]{:S(2)}, u32[]{:S(2)}) collective-permute-start(f32[128,128]{1,0:T(8,128)S(1)} %divide_subtract_fusion.2.refs_0_), channel_id=1, source_target_pairs={{0,96},{32,64},{64,32},{96,0},{1,97},{33,65},{65,33},{97,1},{2,98}... | collective-permute-start | bytes 196616 | tf_op jit(solution)/shard_map/ppermute | solution.py:37
  82.9 2.3 %collective-permute-done.10.refs_1_ = f32[128,128]{1,0:T(8,128)S(1)} collective-permute-done((f32[128,128]{1,0:T(8,128)S(1)}, f32[128,128]{1,0:T(8,128)S(1)}, u32[]{:S(2)}, u32[]{:S(2)}) %collective-permute-start.10) | collective-permute-done | bytes 65568 | tf_op jit(solution)/shard_map/ppermute | solution.py:37
  87.9 11.4 %all_to_all.42 = f32[8,128,128]{2,1,0:T(8,128)S(1)} all-to-all(f32[8,128,128]{2,1,0:T(8,128)S(1)} %product.10), channel_id=1, replica_groups=mesh['ylo'=2,'core'=2,'zhi'=2,'zlo'=2,'xhi'=2,'xlo'=2,'yhi'=2] {'xlo','z..., dimensions={0} | all-to-all | bytes 1048576 | tf_op jit(solution)/shard_map/all_to_all | solution.py:43
  99.3 2.6 %collective-permute-start.13 = (f32[128,128]{1,0:T(8,128)S(1)}, f32[128,128]{1,0:T(8,128)S(1)}, u32[]{:S(2)}, u32[]{:S(2)}) collective-permute-start(f32[128,128]{1,0:T(8,128)S(1)} %divide_subtract_fusion.1.refs_0_), channel_id=1, source_target_pairs={{0,96},{32,64},{64,32},{96,0},{1,97},{33,65},{65,33},{97,1},{2,98}... | collective-permute-start | bytes 196616 | tf_op jit(solution)/shard_map/ppermute | solution.py:37
  106.0 2.2 %product.11 = f32[8,128,128]{2,1,0:T(8,128)} custom-call(s32[1]{0:T(128)} %bitcast.own_ref, s32[64]{0:T(128)S(1)} %get-tuple-element.35.place_ref, s32[64]{0:T(128)S(1)} %get-tuple-element.34.source_ref, f32[128,128]{1,0:T(8,128)S(1)} %divide_subtract_fusion.1.refs_0_, f32[128,128]{1,0:T(8,128)S(1)} %collective-permute-done.13.refs_1_, ...), custom_call_target="tpu_custom_call" | custom-call | tf_op jit(solution)/shard_map/product/pallas_call | solution.py:171
  108.2 3.5 %all-to-all-start.4 = ((f32[8,128,128]{2,1,0:T(8,128)}), f32[8,128,128]{2,1,0:T(8,128)S(1)}, u32[]{:S(2)}, u32[]{:S(2)}) async-start(f32[8,128,128]{2,1,0:T(8,128)} %product.11), calls=%async_computation.4 | async-start | bytes 1048576 | tf_op jit(solution)/shard_map/all_to_all | solution.py:43
  111.7 3.2 %collective-permute-start.19 = (f32[128,128]{1,0:T(8,128)S(1)}, f32[128,128]{1,0:T(8,128)S(1)}, u32[]{:S(2)}, u32[]{:S(2)}) collective-permute-start(f32[128,128]{1,0:T(8,128)S(1)} %divide_subtract_fusion.1.refs_0_), channel_id=1, source_target_pairs={{0,5},{1,4},{4,1},{5,0},{2,7},{3,6},{6,3},{7,2},{8,13},{9,12},{12,... | collective-permute-start | bytes 196616 | tf_op jit(solution)/shard_map/ppermute | solution.py:37
  117.4 2.7 %all-to-all-done.4 = f32[8,128,128]{2,1,0:T(8,128)S(1)} async-done(((f32[8,128,128]{2,1,0:T(8,128)}), f32[8,128,128]{2,1,0:T(8,128)S(1)}, u32[]{:S(2)}, u32[]{:S(2)}) %all-to-all-start.4) | async-done | bytes 524320 | tf_op jit(solution)/shard_map/all_to_all | solution.py:43
  120.2 2.6 %collective-permute-start.16 = (f32[128,128]{1,0:T(8,128)S(1)}, f32[128,128]{1,0:T(8,128)S(1)}, u32[]{:S(2)}, u32[]{:S(2)}) collective-permute-start(f32[128,128]{1,0:T(8,128)S(1)} %subtract_divide_fusion.refs_0_), channel_id=1, source_target_pairs={{0,96},{32,64},{64,32},{96,0},{1,97},{33,65},{65,33},{97,1},{2,98}... | collective-permute-start | bytes 196616 | tf_op jit(solution)/shard_map/ppermute | solution.py:37
  128.2 13.8 %all_to_all.43 = f32[8,144,128]{2,1,0:T(8,128)S(1)} all-to-all(f32[8,144,128]{2,1,0:T(8,128)S(1)} %product.12), channel_id=1, replica_groups=mesh['ylo'=2,'core'=2,'zhi'=2,'zlo'=2,'xhi'=2,'xlo'=2,'yhi'=2] {'xlo','z..., dimensions={0} | all-to-all | bytes 1179648 | tf_op jit(solution)/shard_map/all_to_all | solution.py:43
  142.1 2.5 %collective-permute-start.22 = (f32[144,128]{1,0:T(8,128)S(1)}, f32[144,128]{1,0:T(8,128)S(1)}, u32[]{:S(2)}, u32[]{:S(2)}) collective-permute-start(f32[144,128]{1,0:T(8,128)S(1)} %pad_maximum_fusion.refs_0_), channel_id=1, source_target_pairs={{0,96},{32,64},{64,32},{96,0},{1,97},{33,65},{65,33},{97,1},{2,98}... | collective-permute-start | bytes 221192 | tf_op jit(solution)/shard_map/ppermute | solution.py:37
  145.4 2.0 %collective-permute-done.22.refs_1_ = f32[144,128]{1,0:T(8,128)S(1)} collective-permute-done((f32[144,128]{1,0:T(8,128)S(1)}, f32[144,128]{1,0:T(8,128)S(1)}, u32[]{:S(2)}, u32[]{:S(2)}) %collective-permute-start.22) | collective-permute-done | bytes 73760 | tf_op jit(solution)/shard_map/ppermute | solution.py:37
  150.4 12.3 %all_to_all.44.got_ref = f32[8,144,128]{2,1,0:T(8,128)S(1)} all-to-all(f32[8,144,128]{2,1,0:T(8,128)S(1)} %product.13), channel_id=1, replica_groups=mesh['ylo'=2,'core'=2,'zhi'=2,'zlo'=2,'xhi'=2,'xlo'=2,'yhi'=2] {'xlo','z..., dimensions={0} | all-to-all | bytes 1179648 | tf_op jit(solution)/shard_map/all_to_all | solution.py:43
  162.7 3.1 %collective-permute-start.25 = (f32[128,128]{1,0:T(8,128)S(1)}, f32[128,128]{1,0:T(8,128)S(1)}, u32[]{:S(2)}, u32[]{:S(2)}) collective-permute-start(f32[128,128]{1,0:T(8,128)S(1)} %divide_subtract_fusion.refs_0_), channel_id=1, source_target_pairs={{0,5},{1,4},{4,1},{5,0},{2,7},{3,6},{6,3},{7,2},{8,13},{9,12},{12,... | collective-permute-start | bytes 196616 | tf_op jit(solution)/shard_map/ppermute | solution.py:37
  168.5 3.8 %factor.1.inverse_ref = f32[128,128]{1,0:T(8,128)S(1)} custom-call(f32[8,144,128]{2,1,0:T(8,128)S(1)} %all_to_all.44.got_ref), custom_call_target="tpu_custom_call" | custom-call | tf_op jit(solution)/shard_map/factor/pallas_call | solution.py:225
  173.4 3.3 %collective-permute-start.28 = (f32[72,128]{1,0:T(8,128)S(1)}, f32[72,128]{1,0:T(8,128)S(1)}, u32[]{:S(2)}, u32[]{:S(2)}) collective-permute-start(f32[72,128]{1,0:T(8,128)S(1)} %get-tuple-element.31), channel_id=1, source_target_pairs={{0,96},{32,64},{64,32},{96,0},{1,97},{33,65},{65,33},{97,1},{2,98}... | collective-permute-start | bytes 110600 | tf_op jit(solution)/shard_map/ppermute | solution.py:37
  180.0 9.3 %all_to_all.45.folded_ref = f32[8,72,128]{2,1,0:T(8,128)S(1)} all-to-all(f32[8,72,128]{2,1,0:T(8,128)S(1)} %broadcast_in_dim.15), channel_id=1, replica_groups=mesh['ylo'=2,'core'=2,'zhi'=2,'zlo'=2,'xhi'=2,'xlo'=2,'yhi'=2] {'xlo','z..., dimensions={0} | all-to-all | bytes 589824 | tf_op jit(solution)/shard_map/all_to_all | solution.py:43
  189.3 4.7 %finish.1 = f32[128,128]{1,0:T(8,128)} custom-call(f32[8,72,128]{2,1,0:T(8,128)S(1)} %all_to_all.45.folded_ref, f32[128,128]{1,0:T(8,128)S(1)} %get-tuple-element.32.x_ref), custom_call_target="tpu_custom_call" | custom-call | tf_op jit(solution)/shard_map/finish/pallas_call | solution.py:268
  (106 shorter events, 41.5 us)
Async XLA Ops:
  2.3 20.3 %collective-permute-start.1 = (f32[1024,128]{1,0:T(8,128)S(1)}, f32[1024,128]{1,0:T(8,128)S(1)}, u32[]{:S(2)}, u32[]{:S(2)}) collective-permute-start(f32[1024,128]{1,0:T(8,128)S(1)} %get-tuple-element.22), channel_id=1, source_target_pairs={{0,1},{1,0},{2,3},{3,2},{4,5},{5,4},{6,7},{7,6},{8,9},{9,8},{10,11... | collective-permute-start | bytes 1572872 | tf_op jit(solution)/shard_map/ppermute | solution.py:33
  6.1 18.9 %collective-permute-start.3 = (f32[1024,128]{1,0:T(8,128)}, f32[1024,128]{1,0:T(8,128)}, u32[]{:S(2)}, u32[]{:S(2)}) collective-permute-start(f32[1024,128]{1,0:T(8,128)} %get-tuple-element.23), channel_id=1, source_target_pairs={{0,4},{4,0},{1,5},{5,1},{2,6},{6,2},{3,7},{7,3},{8,12},{12,8},{9,1... | collective-permute-start | bytes 1572872 | tf_op jit(solution)/shard_map/ppermute | solution.py:33
  10.9 11.7 %all-to-all-start = ((f32[8,40,128]{2,1,0:T(8,128)}), f32[8,40,128]{2,1,0:T(8,128)S(1)}, u32[]{:S(2)}, u32[]{:S(2)}) async-start(f32[8,40,128]{2,1,0:T(8,128)} %maximum_maximum_fusion), calls=%async_computation | async-start | bytes 327680 | tf_op jit(solution)/shard_map/all_to_all | solution.py:43
  14.4 19.0 %collective-permute-start.5 = (f32[1024,128]{1,0:T(8,128)S(1)}, f32[1024,128]{1,0:T(8,128)S(1)}, u32[]{:S(2)}, u32[]{:S(2)}) collective-permute-start(f32[1024,128]{1,0:T(8,128)S(1)} %get-tuple-element.22), channel_id=1, source_target_pairs={{0,4},{4,0},{1,5},{5,1},{2,6},{6,2},{3,7},{7,3},{8,12},{12,8},{9,1... | collective-permute-start | bytes 1572872 | tf_op jit(solution)/shard_map/ppermute | solution.py:33
  17.3 16.9 %collective-permute-start.6 = (f32[1024,128]{1,0:T(8,128)}, f32[1024,128]{1,0:T(8,128)}, u32[]{:S(2)}, u32[]{:S(2)}) collective-permute-start(f32[1024,128]{1,0:T(8,128)} %get-tuple-element.23), channel_id=1, source_target_pairs={{0,1},{1,0},{2,3},{3,2},{4,5},{5,4},{6,7},{7,6},{8,9},{9,8},{10,11... | collective-permute-start | bytes 1572872 | tf_op jit(solution)/shard_map/ppermute | solution.py:33
  22.7 21.8 %collective-permute-start.2 = (f32[1024,128]{1,0:T(8,128)S(1)}, f32[1024,128]{1,0:T(8,128)S(1)}, u32[]{:S(2)}, u32[]{:S(2)}) collective-permute-start(f32[1024,128]{1,0:T(8,128)S(1)} %collective-permute-done.1.refs_0_), channel_id=1, source_target_pairs={{0,4},{4,0},{1,5},{5,1},{2,6},{6,2},{3,7},{7,3},{8,12},{12,8},{9,1... | collective-permute-start | bytes 1572872 | tf_op jit(solution)/shard_map/ppermute | solution.py:33
  25.0 19.5 %collective-permute-start.4 = (f32[1024,128]{1,0:T(8,128)}, f32[1024,128]{1,0:T(8,128)S(1)}, u32[]{:S(2)}, u32[]{:S(2)}) collective-permute-start(f32[1024,128]{1,0:T(8,128)} %collective-permute-done.3.refs_3_), channel_id=1, source_target_pairs={{0,1},{1,0},{2,3},{3,2},{4,5},{5,4},{6,7},{7,6},{8,9},{9,8},{10,11... | collective-permute-start | bytes 1572872 | tf_op jit(solution)/shard_map/ppermute | solution.py:33
  27.2 9.3 %collective-permute-start = (f32[8,40,128]{2,1,0:T(8,128)S(1)}, f32[8,40,128]{2,1,0:T(8,128)S(1)}, u32[]{:S(2)}, u32[]{:S(2)}) collective-permute-start(f32[8,40,128]{2,1,0:T(8,128)S(1)} %all-to-all-done.refs_0_), channel_id=1, source_target_pairs={{0,32},{32,0},{1,33},{33,1},{2,34},{34,2},{3,35},{35,3},{4,36},{36... | collective-permute-start | bytes 491528 | tf_op jit(solution)/shard_map/ppermute | solution.py:33
  58.8 5.5 %collective-permute-start.7 = (f32[128,128]{1,0:T(8,128)S(1)}, f32[128,128]{1,0:T(8,128)S(1)}, u32[]{:S(2)}, u32[]{:S(2)}) collective-permute-start(f32[128,128]{1,0:T(8,128)S(1)} %subtract_divide_fusion.1.refs_0_), channel_id=1, source_target_pairs={{0,96},{32,64},{64,32},{96,0},{1,97},{33,65},{65,33},{97,1},{2,98}... | collective-permute-start | bytes 196616 | tf_op jit(solution)/shard_map/ppermute | solution.py:37
  62.4 4.3 %collective-permute-start.8 = (f32[128,128]{1,0:T(8,128)S(1)}, f32[128,128]{1,0:T(8,128)S(1)}, u32[]{:S(2)}, u32[]{:S(2)}) collective-permute-start(f32[128,128]{1,0:T(8,128)S(1)} %subtract_divide_fusion.1.refs_0_), channel_id=1, source_target_pairs={{0,64},{64,0},{1,65},{65,1},{2,66},{66,2},{3,67},{67,3},{4,68},{68... | collective-permute-start | bytes 196616 | tf_op jit(solution)/shard_map/ppermute | solution.py:33
  63.5 3.3 %collective-permute-start.9 = (f32[128,128]{1,0:T(8,128)S(1)}, f32[128,128]{1,0:T(8,128)S(1)}, u32[]{:S(2)}, u32[]{:S(2)}) collective-permute-start(f32[128,128]{1,0:T(8,128)S(1)} %subtract_divide_fusion.1.refs_0_), channel_id=1, source_target_pairs={{0,32},{32,0},{1,33},{33,1},{2,34},{34,2},{3,35},{35,3},{4,36},{36... | collective-permute-start | bytes 196616 | tf_op jit(solution)/shard_map/ppermute | solution.py:33
  79.5 5.6 %collective-permute-start.10 = (f32[128,128]{1,0:T(8,128)S(1)}, f32[128,128]{1,0:T(8,128)S(1)}, u32[]{:S(2)}, u32[]{:S(2)}) collective-permute-start(f32[128,128]{1,0:T(8,128)S(1)} %divide_subtract_fusion.2.refs_0_), channel_id=1, source_target_pairs={{0,96},{32,64},{64,32},{96,0},{1,97},{33,65},{65,33},{97,1},{2,98}... | collective-permute-start | bytes 196616 | tf_op jit(solution)/shard_map/ppermute | solution.py:37
  82.4 4.2 %collective-permute-start.11 = (f32[128,128]{1,0:T(8,128)S(1)}, f32[128,128]{1,0:T(8,128)S(1)}, u32[]{:S(2)}, u32[]{:S(2)}) collective-permute-start(f32[128,128]{1,0:T(8,128)S(1)} %divide_subtract_fusion.2.refs_0_), channel_id=1, source_target_pairs={{0,64},{64,0},{1,65},{65,1},{2,66},{66,2},{3,67},{67,3},{4,68},{68... | collective-permute-start | bytes 196616 | tf_op jit(solution)/shard_map/ppermute | solution.py:33
  82.8 3.7 %collective-permute-start.12 = (f32[128,128]{1,0:T(8,128)S(1)}, f32[128,128]{1,0:T(8,128)S(1)}, u32[]{:S(2)}, u32[]{:S(2)}) collective-permute-start(f32[128,128]{1,0:T(8,128)S(1)} %divide_subtract_fusion.2.refs_0_), channel_id=1, source_target_pairs={{0,32},{32,0},{1,33},{33,1},{2,34},{34,2},{3,35},{35,3},{4,36},{36... | collective-permute-start | bytes 196616 | tf_op jit(solution)/shard_map/ppermute | solution.py:33
  99.3 5.2 %collective-permute-start.13 = (f32[128,128]{1,0:T(8,128)S(1)}, f32[128,128]{1,0:T(8,128)S(1)}, u32[]{:S(2)}, u32[]{:S(2)}) collective-permute-start(f32[128,128]{1,0:T(8,128)S(1)} %divide_subtract_fusion.1.refs_0_), channel_id=1, source_target_pairs={{0,96},{32,64},{64,32},{96,0},{1,97},{33,65},{65,33},{97,1},{2,98}... | collective-permute-start | bytes 196616 | tf_op jit(solution)/shard_map/ppermute | solution.py:37
  101.9 4.1 %collective-permute-start.14 = (f32[128,128]{1,0:T(8,128)S(1)}, f32[128,128]{1,0:T(8,128)S(1)}, u32[]{:S(2)}, u32[]{:S(2)}) collective-permute-start(f32[128,128]{1,0:T(8,128)S(1)} %divide_subtract_fusion.1.refs_0_), channel_id=1, source_target_pairs={{0,64},{64,0},{1,65},{65,1},{2,66},{66,2},{3,67},{67,3},{4,68},{68... | collective-permute-start | bytes 196616 | tf_op jit(solution)/shard_map/ppermute | solution.py:33
  102.7 3.3 %collective-permute-start.15 = (f32[128,128]{1,0:T(8,128)S(1)}, f32[128,128]{1,0:T(8,128)S(1)}, u32[]{:S(2)}, u32[]{:S(2)}) collective-permute-start(f32[128,128]{1,0:T(8,128)S(1)} %divide_subtract_fusion.1.refs_0_), channel_id=1, source_target_pairs={{0,32},{32,0},{1,33},{33,1},{2,34},{34,2},{3,35},{35,3},{4,36},{36... | collective-permute-start | bytes 196616 | tf_op jit(solution)/shard_map/ppermute | solution.py:33
  108.2 12.0 %all-to-all-start.4 = ((f32[8,128,128]{2,1,0:T(8,128)}), f32[8,128,128]{2,1,0:T(8,128)S(1)}, u32[]{:S(2)}, u32[]{:S(2)}) async-start(f32[8,128,128]{2,1,0:T(8,128)} %product.11), calls=%async_computation.4 | async-start | bytes 1048576 | tf_op jit(solution)/shard_map/all_to_all | solution.py:43
  111.7 11.8 %collective-permute-start.19 = (f32[128,128]{1,0:T(8,128)S(1)}, f32[128,128]{1,0:T(8,128)S(1)}, u32[]{:S(2)}, u32[]{:S(2)}) collective-permute-start(f32[128,128]{1,0:T(8,128)S(1)} %divide_subtract_fusion.1.refs_0_), channel_id=1, source_target_pairs={{0,5},{1,4},{4,1},{5,0},{2,7},{3,6},{6,3},{7,2},{8,13},{9,12},{12,... | collective-permute-start | bytes 196616 | tf_op jit(solution)/shard_map/ppermute | solution.py:37
  114.9 9.3 %collective-permute-start.20 = (f32[128,128]{1,0:T(8,128)S(1)}, f32[128,128]{1,0:T(8,128)S(1)}, u32[]{:S(2)}, u32[]{:S(2)}) collective-permute-start(f32[128,128]{1,0:T(8,128)S(1)} %divide_subtract_fusion.1.refs_0_), channel_id=1, source_target_pairs={{0,4},{4,0},{1,5},{5,1},{2,6},{6,2},{3,7},{7,3},{8,12},{12,8},{9,1... | collective-permute-start | bytes 196616 | tf_op jit(solution)/shard_map/ppermute | solution.py:33
  115.5 8.7 %collective-permute-start.21 = (f32[128,128]{1,0:T(8,128)S(1)}, f32[128,128]{1,0:T(8,128)S(1)}, u32[]{:S(2)}, u32[]{:S(2)}) collective-permute-start(f32[128,128]{1,0:T(8,128)S(1)} %divide_subtract_fusion.1.refs_0_), channel_id=1, source_target_pairs={{0,1},{1,0},{2,3},{3,2},{4,5},{5,4},{6,7},{7,6},{8,9},{9,8},{10,11... | collective-permute-start | bytes 196616 | tf_op jit(solution)/shard_map/ppermute | solution.py:33
  120.2 5.2 %collective-permute-start.16 = (f32[128,128]{1,0:T(8,128)S(1)}, f32[128,128]{1,0:T(8,128)S(1)}, u32[]{:S(2)}, u32[]{:S(2)}) collective-permute-start(f32[128,128]{1,0:T(8,128)S(1)} %subtract_divide_fusion.refs_0_), channel_id=1, source_target_pairs={{0,96},{32,64},{64,32},{96,0},{1,97},{33,65},{65,33},{97,1},{2,98}... | collective-permute-start | bytes 196616 | tf_op jit(solution)/shard_map/ppermute | solution.py:37
  122.8 4.1 %collective-permute-start.17 = (f32[128,128]{1,0:T(8,128)S(1)}, f32[128,128]{1,0:T(8,128)S(1)}, u32[]{:S(2)}, u32[]{:S(2)}) collective-permute-start(f32[128,128]{1,0:T(8,128)S(1)} %subtract_divide_fusion.refs_0_), channel_id=1, source_target_pairs={{0,64},{64,0},{1,65},{65,1},{2,66},{66,2},{3,67},{67,3},{4,68},{68... | collective-permute-start | bytes 196616 | tf_op jit(solution)/shard_map/ppermute | solution.py:33
  123.5 3.3 %collective-permute-start.18 = (f32[128,128]{1,0:T(8,128)S(1)}, f32[128,128]{1,0:T(8,128)S(1)}, u32[]{:S(2)}, u32[]{:S(2)}) collective-permute-start(f32[128,128]{1,0:T(8,128)S(1)} %subtract_divide_fusion.refs_0_), channel_id=1, source_target_pairs={{0,32},{32,0},{1,33},{33,1},{2,34},{34,2},{3,35},{35,3},{4,36},{36... | collective-permute-start | bytes 196616 | tf_op jit(solution)/shard_map/ppermute | solution.py:33
  142.1 5.2 %collective-permute-start.22 = (f32[144,128]{1,0:T(8,128)S(1)}, f32[144,128]{1,0:T(8,128)S(1)}, u32[]{:S(2)}, u32[]{:S(2)}) collective-permute-start(f32[144,128]{1,0:T(8,128)S(1)} %pad_maximum_fusion.refs_0_), channel_id=1, source_target_pairs={{0,96},{32,64},{64,32},{96,0},{1,97},{33,65},{65,33},{97,1},{2,98}... | collective-permute-start | bytes 221192 | tf_op jit(solution)/shard_map/ppermute | solution.py:37
  144.6 4.4 %collective-permute-start.23 = (f32[144,128]{1,0:T(8,128)S(1)}, f32[144,128]{1,0:T(8,128)S(1)}, u32[]{:S(2)}, u32[]{:S(2)}) collective-permute-start(f32[144,128]{1,0:T(8,128)S(1)} %pad_maximum_fusion.refs_0_), channel_id=1, source_target_pairs={{0,64},{64,0},{1,65},{65,1},{2,66},{66,2},{3,67},{67,3},{4,68},{68... | collective-permute-start | bytes 221192 | tf_op jit(solution)/shard_map/ppermute | solution.py:33
  145.4 3.7 %collective-permute-start.24 = (f32[144,128]{1,0:T(8,128)S(1)}, f32[144,128]{1,0:T(8,128)S(1)}, u32[]{:S(2)}, u32[]{:S(2)}) collective-permute-start(f32[144,128]{1,0:T(8,128)S(1)} %pad_maximum_fusion.refs_0_), channel_id=1, source_target_pairs={{0,32},{32,0},{1,33},{33,1},{2,34},{34,2},{3,35},{35,3},{4,36},{36... | collective-permute-start | bytes 221192 | tf_op jit(solution)/shard_map/ppermute | solution.py:33
  162.7 9.6 %collective-permute-start.25 = (f32[128,128]{1,0:T(8,128)S(1)}, f32[128,128]{1,0:T(8,128)S(1)}, u32[]{:S(2)}, u32[]{:S(2)}) collective-permute-start(f32[128,128]{1,0:T(8,128)S(1)} %divide_subtract_fusion.refs_0_), channel_id=1, source_target_pairs={{0,5},{1,4},{4,1},{5,0},{2,7},{3,6},{6,3},{7,2},{8,13},{9,12},{12,... | collective-permute-start | bytes 196616 | tf_op jit(solution)/shard_map/ppermute | solution.py:37
  165.9 6.5 %collective-permute-start.26 = (f32[128,128]{1,0:T(8,128)S(1)}, f32[128,128]{1,0:T(8,128)S(1)}, u32[]{:S(2)}, u32[]{:S(2)}) collective-permute-start(f32[128,128]{1,0:T(8,128)S(1)} %divide_subtract_fusion.refs_0_), channel_id=1, source_target_pairs={{0,4},{4,0},{1,5},{5,1},{2,6},{6,2},{3,7},{7,3},{8,12},{12,8},{9,1... | collective-permute-start | bytes 196616 | tf_op jit(solution)/shard_map/ppermute | solution.py:33
  167.2 5.3 %collective-permute-start.27 = (f32[128,128]{1,0:T(8,128)S(1)}, f32[128,128]{1,0:T(8,128)S(1)}, u32[]{:S(2)}, u32[]{:S(2)}) collective-permute-start(f32[128,128]{1,0:T(8,128)S(1)} %divide_subtract_fusion.refs_0_), channel_id=1, source_target_pairs={{0,1},{1,0},{2,3},{3,2},{4,5},{5,4},{6,7},{7,6},{8,9},{9,8},{10,11... | collective-permute-start | bytes 196616 | tf_op jit(solution)/shard_map/ppermute | solution.py:33
  173.4 4.9 %collective-permute-start.28 = (f32[72,128]{1,0:T(8,128)S(1)}, f32[72,128]{1,0:T(8,128)S(1)}, u32[]{:S(2)}, u32[]{:S(2)}) collective-permute-start(f32[72,128]{1,0:T(8,128)S(1)} %get-tuple-element.31), channel_id=1, source_target_pairs={{0,96},{32,64},{64,32},{96,0},{1,97},{33,65},{65,33},{97,1},{2,98}... | collective-permute-start | bytes 110600 | tf_op jit(solution)/shard_map/ppermute | solution.py:37
  176.7 3.3 %collective-permute-start.29 = (f32[72,128]{1,0:T(8,128)S(1)}, f32[72,128]{1,0:T(8,128)S(1)}, u32[]{:S(2)}, u32[]{:S(2)}) collective-permute-start(f32[72,128]{1,0:T(8,128)S(1)} %get-tuple-element.31), channel_id=1, source_target_pairs={{0,64},{64,0},{1,65},{65,1},{2,66},{66,2},{3,67},{67,3},{4,68},{68... | collective-permute-start | bytes 110600 | tf_op jit(solution)/shard_map/ppermute | solution.py:33
  (9 other events, 43.8 us)

commit v8 on v7

--- a/solution.py
+++ b/solution.py
@@ -21,6 +21,10 @@
 GRANT = pltpu.CompilerParams(vmem_limit_bytes=16 * 2**20)
 
 
+def cost(micros):
+    return pl.CostEstimate(flops=0, bytes_accessed=int(micros * 1.2e6), transcendentals=0)
+
+
 def digits(index, names):
     out = 0
     for name in names:
@@ -66,7 +70,7 @@
         widen_kernel,
         out_shape=(wide, wide),
         compiler_params=GRANT,
-        name="widen",
+        cost_estimate=cost(1.3), name="widen",
     )(tiles)
 
 
@@ -80,7 +84,7 @@
         turn_kernel,
         out_shape=jax.ShapeDtypeStruct(tiles.shape, tiles.dtype),
         compiler_params=GRANT,
-        name="turn",
+        cost_estimate=cost(0.5), name="turn",
     )(tiles)
 
 
@@ -103,7 +107,7 @@
         in_specs=[spec] * len(parts),
         out_specs=pl.BlockSpec((len(parts), step, blk, blk), lambda i: (0, i, 0, 0)),
         compiler_params=GRANT,
-        name="pack",
+        cost_estimate=cost(1.3), name="pack",
     )(*parts).reshape(-1, blk, blk)
 
 
@@ -175,7 +179,7 @@
         out_specs=vmem,
         scratch_shapes=[pltpu.VMEM((blocks + 1, 3 * width, blk), jnp.bfloat16)],
         compiler_params=GRANT,
-        name="product",
+        cost_estimate=cost(1.4), name="product",
     )(own.reshape(1), place, source, *vs, *tiles, *last)
 
 
@@ -226,7 +230,7 @@
         factor_kernel,
         out_shape=jax.ShapeDtypeStruct((size, size), jnp.float32),
         compiler_params=GRANT,
-        name="factor",
+        cost_estimate=cost(3.9), name="factor",
     )(got)
 
 
@@ -269,7 +273,7 @@
         functools.partial(finish_kernel, scale),
         out_shape=jax.ShapeDtypeStruct(x.shape[::-1], jnp.float32),
         compiler_params=GRANT,
-        name="finish",
+        cost_estimate=cost(4.7), name="finish",
     )(folded, x)
 
 
@@ -302,7 +306,7 @@
         in_specs=[pl.BlockSpec(memory_space=pltpu.SMEM)] + [vmem] * len(slices),
         scratch_shapes=[pltpu.VMEM((width, blocks * blk), jnp.float32)],
         compiler_params=GRANT,
-        name="gram",
+        cost_estimate=cost(0.4), name="gram",
     )(own.reshape(1), *slices)
 
 
@@ -333,7 +337,7 @@
             pltpu.VMEM((blocks, width, blk), jnp.float32),
         ],
         compiler_params=GRANT,
-        name="normal",
+        cost_estimate=cost(0.9), name="normal",
     )(own.reshape(1), inverse, *slices)
 
 
@@ -349,7 +353,7 @@
         out_shape=(row, row),
         in_specs=[pl.BlockSpec(memory_space=pltpu.SMEM)],
         compiler_params=GRANT,
-        name="ends",
+        cost_estimate=cost(0.5), name="ends",
     )(bounds)
 
 

time: 195 us -> 195 us (level)
  no operation moved by 1% of the time
where the time goes in v8:
time: 195 us; the launch traced here: 194 us
  blocking collectives  71.6 us (37%)
  starting transfers between devices  61.3 us (31%)
  waiting for transfers between devices  33.1 us (17%)
  Pallas kernels  23.1 us (12%)
  local copies, waits for them, and re-layouts  3.57 us (2%)
    all_to_all x6, blocking collectives, exchange(): return lax.all_to_all(x, names, 0, 0, tiled=True)  71.6 us
    ppermute x23, starting transfers between devices, swap(): return lax.ppermute(x, name, [(0, 1), (1, 0)])  30.8 us
    ppermute x8, starting transfers between devices, three(): lax.ppermute(x, names, [(i, i ^ 3) for i in range(4)])  23.5 us
    ppermute x23, waiting for transfers between devices, swap(): return lax.ppermute(x, name, [(0, 1), (1, 0)])  19.2 us
    pallas_call x7, Pallas kernels, product(): pl.pallas_call(functools.partial(product_kernel, len(vs), begun is not No...  9.61 us
    ppermute x8, waiting for transfers between devices, three(): lax.ppermute(x, names, [(i, i ^ 3) for i in range(4)])  8.56 us
    all_to_all x2, starting transfers between devices, exchange(): return lax.all_to_all(x, names, 0, 0, tiled=True)  7 us
    all_to_all x2, waiting for transfers between devices, exchange(): return lax.all_to_all(x, names, 0, 0, tiled=True)  5.29 us
  transfers between devices with their start and end apart: 33, of which 17 were waited for; matrix products, arithmetic and copies ran while one was open for 1% of the time, Pallas kernels for 4%

profile of v8, /device:TPU:1, one launch (start us, length us, event | category | flops | bytes accessed | tf_op | source)
XLA Modules:
  0.0 194.0 jit_solution(17701645761578444518)
XLA Ops:
  2.3 3.7 %collective-permute-start.1 = (f32[1024,128]{1,0:T(8,128)S(1)}, f32[1024,128]{1,0:T(8,128)S(1)}, u32[]{:S(2)}, u32[]{:S(2)}) collective-permute-start(f32[1024,128]{1,0:T(8,128)S(1)} %get-tuple-element.22), channel_id=1, source_target_pairs={{0,1},{1,0},{2,3},{3,2},{4,5},{5,4},{6,7},{7,6},{8,9},{9,8},{10,11... | collective-permute-start | bytes 1572872 | tf_op jit(solution)/shard_map/ppermute | solution.py:37
  6.1 2.8 %collective-permute-start.3 = (f32[1024,128]{1,0:T(8,128)}, f32[1024,128]{1,0:T(8,128)}, u32[]{:S(2)}, u32[]{:S(2)}) collective-permute-start(f32[1024,128]{1,0:T(8,128)} %get-tuple-element.23), channel_id=1, source_target_pairs={{0,4},{4,0},{1,5},{5,1},{2,6},{6,2},{3,7},{7,3},{8,12},{12,8},{9,1... | collective-permute-start | bytes 1572872 | tf_op jit(solution)/shard_map/ppermute | solution.py:37
  10.9 3.5 %all-to-all-start = ((f32[8,40,128]{2,1,0:T(8,128)}), f32[8,40,128]{2,1,0:T(8,128)S(1)}, u32[]{:S(2)}, u32[]{:S(2)}) async-start(f32[8,40,128]{2,1,0:T(8,128)} %maximum_maximum_fusion), calls=%async_computation | async-start | bytes 327680 | tf_op jit(solution)/shard_map/all_to_all | solution.py:47
  14.4 2.9 %collective-permute-start.5 = (f32[1024,128]{1,0:T(8,128)S(1)}, f32[1024,128]{1,0:T(8,128)S(1)}, u32[]{:S(2)}, u32[]{:S(2)}) collective-permute-start(f32[1024,128]{1,0:T(8,128)S(1)} %get-tuple-element.22), channel_id=1, source_target_pairs={{0,4},{4,0},{1,5},{5,1},{2,6},{6,2},{3,7},{7,3},{8,12},{12,8},{9,1... | collective-permute-start | bytes 1572872 | tf_op jit(solution)/shard_map/ppermute | solution.py:37
  17.3 2.7 %collective-permute-start.6 = (f32[1024,128]{1,0:T(8,128)}, f32[1024,128]{1,0:T(8,128)}, u32[]{:S(2)}, u32[]{:S(2)}) collective-permute-start(f32[1024,128]{1,0:T(8,128)} %get-tuple-element.23), channel_id=1, source_target_pairs={{0,1},{1,0},{2,3},{3,2},{4,5},{5,4},{6,7},{7,6},{8,9},{9,8},{10,11... | collective-permute-start | bytes 1572872 | tf_op jit(solution)/shard_map/ppermute | solution.py:37
  20.1 2.6 %all-to-all-done.refs_0_ = f32[8,40,128]{2,1,0:T(8,128)S(1)} async-done(((f32[8,40,128]{2,1,0:T(8,128)}), f32[8,40,128]{2,1,0:T(8,128)S(1)}, u32[]{:S(2)}, u32[]{:S(2)}) %all-to-all-start) | async-done | bytes 163872 | tf_op jit(solution)/shard_map/all_to_all | solution.py:47
  22.7 2.4 %collective-permute-start.2 = (f32[1024,128]{1,0:T(8,128)S(1)}, f32[1024,128]{1,0:T(8,128)S(1)}, u32[]{:S(2)}, u32[]{:S(2)}) collective-permute-start(f32[1024,128]{1,0:T(8,128)S(1)} %collective-permute-done.1.refs_0_), channel_id=1, source_target_pairs={{0,4},{4,0},{1,5},{5,1},{2,6},{6,2},{3,7},{7,3},{8,12},{12,8},{9,1... | collective-permute-start | bytes 1572872 | tf_op jit(solution)/shard_map/ppermute | solution.py:37
  27.2 3.8 %collective-permute-start = (f32[8,40,128]{2,1,0:T(8,128)S(1)}, f32[8,40,128]{2,1,0:T(8,128)S(1)}, u32[]{:S(2)}, u32[]{:S(2)}) collective-permute-start(f32[8,40,128]{2,1,0:T(8,128)S(1)} %all-to-all-done.refs_0_), channel_id=1, source_target_pairs={{0,32},{32,0},{1,33},{33,1},{2,34},{34,2},{3,35},{35,3},{4,36},{36... | collective-permute-start | bytes 491528 | tf_op jit(solution)/shard_map/ppermute | solution.py:37
  31.1 2.3 %collective-permute-done.5.refs_2_ = f32[1024,128]{1,0:T(8,128)S(1)} collective-permute-done((f32[1024,128]{1,0:T(8,128)S(1)}, f32[1024,128]{1,0:T(8,128)S(1)}, u32[]{:S(2)}, u32[]{:S(2)}) %collective-permute-start.5) | collective-permute-done | bytes 524320 | tf_op jit(solution)/shard_map/ppermute | solution.py:37
  37.7 6.8 %collective-permute-done.2.refs_0_ = f32[1024,128]{1,0:T(8,128)S(1)} collective-permute-done((f32[1024,128]{1,0:T(8,128)S(1)}, f32[1024,128]{1,0:T(8,128)S(1)}, u32[]{:S(2)}, u32[]{:S(2)}) %collective-permute-start.2) | collective-permute-done | bytes 524320 | tf_op jit(solution)/shard_map/ppermute | solution.py:37
  45.5 13.3 %all_to_all.40 = f32[8,128,128]{2,1,0:T(8,128)S(1)} all-to-all(f32[8,128,128]{2,1,0:T(8,128)S(1)} %product.8), channel_id=1, replica_groups=mesh['ylo'=2,'core'=2,'zhi'=2,'zlo'=2,'xhi'=2,'xlo'=2,'yhi'=2] {'xlo','z..., dimensions={0} | all-to-all | bytes 1048576 | tf_op jit(solution)/shard_map/all_to_all | solution.py:47
  58.8 3.6 %collective-permute-start.7 = (f32[128,128]{1,0:T(8,128)S(1)}, f32[128,128]{1,0:T(8,128)S(1)}, u32[]{:S(2)}, u32[]{:S(2)}) collective-permute-start(f32[128,128]{1,0:T(8,128)S(1)} %subtract_divide_fusion.1.refs_0_), channel_id=1, source_target_pairs={{0,96},{32,64},{64,32},{96,0},{1,97},{33,65},{65,33},{97,1},{2,98}... | collective-permute-start | bytes 196616 | tf_op jit(solution)/shard_map/ppermute | solution.py:41
  64.3 2.4 %collective-permute-done.8.refs_2_ = f32[128,128]{1,0:T(8,128)S(1)} collective-permute-done((f32[128,128]{1,0:T(8,128)S(1)}, f32[128,128]{1,0:T(8,128)S(1)}, u32[]{:S(2)}, u32[]{:S(2)}) %collective-permute-start.8) | collective-permute-done | bytes 65568 | tf_op jit(solution)/shard_map/ppermute | solution.py:37
  68.1 11.4 %all_to_all.41 = f32[8,128,128]{2,1,0:T(8,128)S(1)} all-to-all(f32[8,128,128]{2,1,0:T(8,128)S(1)} %product.9), channel_id=1, replica_groups=mesh['ylo'=2,'core'=2,'zhi'=2,'zlo'=2,'xhi'=2,'xlo'=2,'yhi'=2] {'xlo','z..., dimensions={0} | all-to-all | bytes 1048576 | tf_op jit(solution)/shard_map/all_to_all | solution.py:47
  79.5 2.8 %collective-permute-start.10 = (f32[128,128]{1,0:T(8,128)S(1)}, f32[128,128]{1,0:T(8,128)S(1)}, u32[]{:S(2)}, u32[]{:S(2)}) collective-permute-start(f32[128,128]{1,0:T(8,128)S(1)} %divide_subtract_fusion.2.refs_0_), channel_id=1, source_target_pairs={{0,96},{32,64},{64,32},{96,0},{1,97},{33,65},{65,33},{97,1},{2,98}... | collective-permute-start | bytes 196616 | tf_op jit(solution)/shard_map/ppermute | solution.py:41
  82.9 2.3 %collective-permute-done.10.refs_1_ = f32[128,128]{1,0:T(8,128)S(1)} collective-permute-done((f32[128,128]{1,0:T(8,128)S(1)}, f32[128,128]{1,0:T(8,128)S(1)}, u32[]{:S(2)}, u32[]{:S(2)}) %collective-permute-start.10) | collective-permute-done | bytes 65568 | tf_op jit(solution)/shard_map/ppermute | solution.py:41
  87.9 11.4 %all_to_all.42 = f32[8,128,128]{2,1,0:T(8,128)S(1)} all-to-all(f32[8,128,128]{2,1,0:T(8,128)S(1)} %product.10), channel_id=1, replica_groups=mesh['ylo'=2,'core'=2,'zhi'=2,'zlo'=2,'xhi'=2,'xlo'=2,'yhi'=2] {'xlo','z..., dimensions={0} | all-to-all | bytes 1048576 | tf_op jit(solution)/shard_map/all_to_all | solution.py:47
  99.3 2.6 %collective-permute-start.13 = (f32[128,128]{1,0:T(8,128)S(1)}, f32[128,128]{1,0:T(8,128)S(1)}, u32[]{:S(2)}, u32[]{:S(2)}) collective-permute-start(f32[128,128]{1,0:T(8,128)S(1)} %divide_subtract_fusion.1.refs_0_), channel_id=1, source_target_pairs={{0,96},{32,64},{64,32},{96,0},{1,97},{33,65},{65,33},{97,1},{2,98}... | collective-permute-start | bytes 196616 | tf_op jit(solution)/shard_map/ppermute | solution.py:41
  106.0 2.2 %product.11 = f32[8,128,128]{2,1,0:T(8,128)} custom-call(s32[1]{0:T(128)} %bitcast.own_ref, s32[64]{0:T(128)S(1)} %get-tuple-element.35.place_ref, s32[64]{0:T(128)S(1)} %get-tuple-element.34.source_ref, f32[128,128]{1,0:T(8,128)S(1)} %divide_subtract_fusion.1.refs_0_, f32[128,128]{1,0:T(8,128)S(1)} %collective-permute-done.13.refs_1_, ...), custom_call_target="tpu_custom_call" | custom-call | bytes 1680000 | tf_op jit(solution)/shard_map/product/pallas_call | solution.py:175
  108.2 3.5 %all-to-all-start.4 = ((f32[8,128,128]{2,1,0:T(8,128)}), f32[8,128,128]{2,1,0:T(8,128)S(1)}, u32[]{:S(2)}, u32[]{:S(2)}) async-start(f32[8,128,128]{2,1,0:T(8,128)} %product.11), calls=%async_computation.4 | async-start | bytes 1048576 | tf_op jit(solution)/shard_map/all_to_all | solution.py:47
  111.7 3.2 %collective-permute-start.19 = (f32[128,128]{1,0:T(8,128)S(1)}, f32[128,128]{1,0:T(8,128)S(1)}, u32[]{:S(2)}, u32[]{:S(2)}) collective-permute-start(f32[128,128]{1,0:T(8,128)S(1)} %divide_subtract_fusion.1.refs_0_), channel_id=1, source_target_pairs={{0,5},{1,4},{4,1},{5,0},{2,7},{3,6},{6,3},{7,2},{8,13},{9,12},{12,... | collective-permute-start | bytes 196616 | tf_op jit(solution)/shard_map/ppermute | solution.py:41
  117.4 2.7 %all-to-all-done.4 = f32[8,128,128]{2,1,0:T(8,128)S(1)} async-done(((f32[8,128,128]{2,1,0:T(8,128)}), f32[8,128,128]{2,1,0:T(8,128)S(1)}, u32[]{:S(2)}, u32[]{:S(2)}) %all-to-all-start.4) | async-done | bytes 524320 | tf_op jit(solution)/shard_map/all_to_all | solution.py:47
  120.2 2.6 %collective-permute-start.16 = (f32[128,128]{1,0:T(8,128)S(1)}, f32[128,128]{1,0:T(8,128)S(1)}, u32[]{:S(2)}, u32[]{:S(2)}) collective-permute-start(f32[128,128]{1,0:T(8,128)S(1)} %subtract_divide_fusion.refs_0_), channel_id=1, source_target_pairs={{0,96},{32,64},{64,32},{96,0},{1,97},{33,65},{65,33},{97,1},{2,98}... | collective-permute-start | bytes 196616 | tf_op jit(solution)/shard_map/ppermute | solution.py:41
  128.2 13.8 %all_to_all.43 = f32[8,144,128]{2,1,0:T(8,128)S(1)} all-to-all(f32[8,144,128]{2,1,0:T(8,128)S(1)} %product.12), channel_id=1, replica_groups=mesh['ylo'=2,'core'=2,'zhi'=2,'zlo'=2,'xhi'=2,'xlo'=2,'yhi'=2] {'xlo','z..., dimensions={0} | all-to-all | bytes 1179648 | tf_op jit(solution)/shard_map/all_to_all | solution.py:47
  142.1 2.5 %collective-permute-start.22 = (f32[144,128]{1,0:T(8,128)S(1)}, f32[144,128]{1,0:T(8,128)S(1)}, u32[]{:S(2)}, u32[]{:S(2)}) collective-permute-start(f32[144,128]{1,0:T(8,128)S(1)} %pad_maximum_fusion.refs_0_), channel_id=1, source_target_pairs={{0,96},{32,64},{64,32},{96,0},{1,97},{33,65},{65,33},{97,1},{2,98}... | collective-permute-start | bytes 221192 | tf_op jit(solution)/shard_map/ppermute | solution.py:41
  145.3 2.1 %collective-permute-done.22.refs_1_ = f32[144,128]{1,0:T(8,128)S(1)} collective-permute-done((f32[144,128]{1,0:T(8,128)S(1)}, f32[144,128]{1,0:T(8,128)S(1)}, u32[]{:S(2)}, u32[]{:S(2)}) %collective-permute-start.22) | collective-permute-done | bytes 73760 | tf_op jit(solution)/shard_map/ppermute | solution.py:41
  150.4 12.3 %all_to_all.44.got_ref = f32[8,144,128]{2,1,0:T(8,128)S(1)} all-to-all(f32[8,144,128]{2,1,0:T(8,128)S(1)} %product.13), channel_id=1, replica_groups=mesh['ylo'=2,'core'=2,'zhi'=2,'zlo'=2,'xhi'=2,'xlo'=2,'yhi'=2] {'xlo','z..., dimensions={0} | all-to-all | bytes 1179648 | tf_op jit(solution)/shard_map/all_to_all | solution.py:47
  162.8 3.0 %collective-permute-start.25 = (f32[128,128]{1,0:T(8,128)S(1)}, f32[128,128]{1,0:T(8,128)S(1)}, u32[]{:S(2)}, u32[]{:S(2)}) collective-permute-start(f32[128,128]{1,0:T(8,128)S(1)} %divide_subtract_fusion.refs_0_), channel_id=1, source_target_pairs={{0,5},{1,4},{4,1},{5,0},{2,7},{3,6},{6,3},{7,2},{8,13},{9,12},{12,... | collective-permute-start | bytes 196616 | tf_op jit(solution)/shard_map/ppermute | solution.py:41
  168.5 3.8 %factor.1.inverse_ref = f32[128,128]{1,0:T(8,128)S(1)} custom-call(f32[8,144,128]{2,1,0:T(8,128)S(1)} %all_to_all.44.got_ref), custom_call_target="tpu_custom_call" | custom-call | bytes 4680000 | tf_op jit(solution)/shard_map/factor/pallas_call | solution.py:229
  173.6 3.1 %collective-permute-start.28 = (f32[72,128]{1,0:T(8,128)S(1)}, f32[72,128]{1,0:T(8,128)S(1)}, u32[]{:S(2)}, u32[]{:S(2)}) collective-permute-start(f32[72,128]{1,0:T(8,128)S(1)} %get-tuple-element.31), channel_id=1, source_target_pairs={{0,96},{32,64},{64,32},{96,0},{1,97},{33,65},{65,33},{97,1},{2,98}... | collective-permute-start | bytes 110600 | tf_op jit(solution)/shard_map/ppermute | solution.py:41
  180.0 9.3 %all_to_all.45.folded_ref = f32[8,72,128]{2,1,0:T(8,128)S(1)} all-to-all(f32[8,72,128]{2,1,0:T(8,128)S(1)} %broadcast_in_dim.15), channel_id=1, replica_groups=mesh['ylo'=2,'core'=2,'zhi'=2,'zlo'=2,'xhi'=2,'xlo'=2,'yhi'=2] {'xlo','z..., dimensions={0} | all-to-all | bytes 589824 | tf_op jit(solution)/shard_map/all_to_all | solution.py:47
  189.4 4.7 %finish.1 = f32[128,128]{1,0:T(8,128)} custom-call(f32[8,72,128]{2,1,0:T(8,128)S(1)} %all_to_all.45.folded_ref, f32[128,128]{1,0:T(8,128)S(1)} %get-tuple-element.32.x_ref), custom_call_target="tpu_custom_call" | custom-call | bytes 5640000 | tf_op jit(solution)/shard_map/finish/pallas_call | solution.py:272
  (106 shorter events, 41.6 us)
Async XLA Ops:
  2.3 20.3 %collective-permute-start.1 = (f32[1024,128]{1,0:T(8,128)S(1)}, f32[1024,128]{1,0:T(8,128)S(1)}, u32[]{:S(2)}, u32[]{:S(2)}) collective-permute-start(f32[1024,128]{1,0:T(8,128)S(1)} %get-tuple-element.22), channel_id=1, source_target_pairs={{0,1},{1,0},{2,3},{3,2},{4,5},{5,4},{6,7},{7,6},{8,9},{9,8},{10,11... | collective-permute-start | bytes 1572872 | tf_op jit(solution)/shard_map/ppermute | solution.py:37
  6.1 18.9 %collective-permute-start.3 = (f32[1024,128]{1,0:T(8,128)}, f32[1024,128]{1,0:T(8,128)}, u32[]{:S(2)}, u32[]{:S(2)}) collective-permute-start(f32[1024,128]{1,0:T(8,128)} %get-tuple-element.23), channel_id=1, source_target_pairs={{0,4},{4,0},{1,5},{5,1},{2,6},{6,2},{3,7},{7,3},{8,12},{12,8},{9,1... | collective-permute-start | bytes 1572872 | tf_op jit(solution)/shard_map/ppermute | solution.py:37
  10.9 11.7 %all-to-all-start = ((f32[8,40,128]{2,1,0:T(8,128)}), f32[8,40,128]{2,1,0:T(8,128)S(1)}, u32[]{:S(2)}, u32[]{:S(2)}) async-start(f32[8,40,128]{2,1,0:T(8,128)} %maximum_maximum_fusion), calls=%async_computation | async-start | bytes 327680 | tf_op jit(solution)/shard_map/all_to_all | solution.py:47
  14.4 19.0 %collective-permute-start.5 = (f32[1024,128]{1,0:T(8,128)S(1)}, f32[1024,128]{1,0:T(8,128)S(1)}, u32[]{:S(2)}, u32[]{:S(2)}) collective-permute-start(f32[1024,128]{1,0:T(8,128)S(1)} %get-tuple-element.22), channel_id=1, source_target_pairs={{0,4},{4,0},{1,5},{5,1},{2,6},{6,2},{3,7},{7,3},{8,12},{12,8},{9,1... | collective-permute-start | bytes 1572872 | tf_op jit(solution)/shard_map/ppermute | solution.py:37
  17.3 16.9 %collective-permute-start.6 = (f32[1024,128]{1,0:T(8,128)}, f32[1024,128]{1,0:T(8,128)}, u32[]{:S(2)}, u32[]{:S(2)}) collective-permute-start(f32[1024,128]{1,0:T(8,128)} %get-tuple-element.23), channel_id=1, source_target_pairs={{0,1},{1,0},{2,3},{3,2},{4,5},{5,4},{6,7},{7,6},{8,9},{9,8},{10,11... | collective-permute-start | bytes 1572872 | tf_op jit(solution)/shard_map/ppermute | solution.py:37
  22.7 21.8 %collective-permute-start.2 = (f32[1024,128]{1,0:T(8,128)S(1)}, f32[1024,128]{1,0:T(8,128)S(1)}, u32[]{:S(2)}, u32[]{:S(2)}) collective-permute-start(f32[1024,128]{1,0:T(8,128)S(1)} %collective-permute-done.1.refs_0_), channel_id=1, source_target_pairs={{0,4},{4,0},{1,5},{5,1},{2,6},{6,2},{3,7},{7,3},{8,12},{12,8},{9,1... | collective-permute-start | bytes 1572872 | tf_op jit(solution)/shard_map/ppermute | solution.py:37
  25.0 19.5 %collective-permute-start.4 = (f32[1024,128]{1,0:T(8,128)}, f32[1024,128]{1,0:T(8,128)S(1)}, u32[]{:S(2)}, u32[]{:S(2)}) collective-permute-start(f32[1024,128]{1,0:T(8,128)} %collective-permute-done.3.refs_3_), channel_id=1, source_target_pairs={{0,1},{1,0},{2,3},{3,2},{4,5},{5,4},{6,7},{7,6},{8,9},{9,8},{10,11... | collective-permute-start | bytes 1572872 | tf_op jit(solution)/shard_map/ppermute | solution.py:37
  27.2 9.3 %collective-permute-start = (f32[8,40,128]{2,1,0:T(8,128)S(1)}, f32[8,40,128]{2,1,0:T(8,128)S(1)}, u32[]{:S(2)}, u32[]{:S(2)}) collective-permute-start(f32[8,40,128]{2,1,0:T(8,128)S(1)} %all-to-all-done.refs_0_), channel_id=1, source_target_pairs={{0,32},{32,0},{1,33},{33,1},{2,34},{34,2},{3,35},{35,3},{4,36},{36... | collective-permute-start | bytes 491528 | tf_op jit(solution)/shard_map/ppermute | solution.py:37
  58.8 5.5 %collective-permute-start.7 = (f32[128,128]{1,0:T(8,128)S(1)}, f32[128,128]{1,0:T(8,128)S(1)}, u32[]{:S(2)}, u32[]{:S(2)}) collective-permute-start(f32[128,128]{1,0:T(8,128)S(1)} %subtract_divide_fusion.1.refs_0_), channel_id=1, source_target_pairs={{0,96},{32,64},{64,32},{96,0},{1,97},{33,65},{65,33},{97,1},{2,98}... | collective-permute-start | bytes 196616 | tf_op jit(solution)/shard_map/ppermute | solution.py:41
  62.4 4.3 %collective-permute-start.8 = (f32[128,128]{1,0:T(8,128)S(1)}, f32[128,128]{1,0:T(8,128)S(1)}, u32[]{:S(2)}, u32[]{:S(2)}) collective-permute-start(f32[128,128]{1,0:T(8,128)S(1)} %subtract_divide_fusion.1.refs_0_), channel_id=1, source_target_pairs={{0,64},{64,0},{1,65},{65,1},{2,66},{66,2},{3,67},{67,3},{4,68},{68... | collective-permute-start | bytes 196616 | tf_op jit(solution)/shard_map/ppermute | solution.py:37
  63.5 3.3 %collective-permute-start.9 = (f32[128,128]{1,0:T(8,128)S(1)}, f32[128,128]{1,0:T(8,128)S(1)}, u32[]{:S(2)}, u32[]{:S(2)}) collective-permute-start(f32[128,128]{1,0:T(8,128)S(1)} %subtract_divide_fusion.1.refs_0_), channel_id=1, source_target_pairs={{0,32},{32,0},{1,33},{33,1},{2,34},{34,2},{3,35},{35,3},{4,36},{36... | collective-permute-start | bytes 196616 | tf_op jit(solution)/shard_map/ppermute | solution.py:37
  79.5 5.6 %collective-permute-start.10 = (f32[128,128]{1,0:T(8,128)S(1)}, f32[128,128]{1,0:T(8,128)S(1)}, u32[]{:S(2)}, u32[]{:S(2)}) collective-permute-start(f32[128,128]{1,0:T(8,128)S(1)} %divide_subtract_fusion.2.refs_0_), channel_id=1, source_target_pairs={{0,96},{32,64},{64,32},{96,0},{1,97},{33,65},{65,33},{97,1},{2,98}... | collective-permute-start | bytes 196616 | tf_op jit(solution)/shard_map/ppermute | solution.py:41
  82.4 4.2 %collective-permute-start.11 = (f32[128,128]{1,0:T(8,128)S(1)}, f32[128,128]{1,0:T(8,128)S(1)}, u32[]{:S(2)}, u32[]{:S(2)}) collective-permute-start(f32[128,128]{1,0:T(8,128)S(1)} %divide_subtract_fusion.2.refs_0_), channel_id=1, source_target_pairs={{0,64},{64,0},{1,65},{65,1},{2,66},{66,2},{3,67},{67,3},{4,68},{68... | collective-permute-start | bytes 196616 | tf_op jit(solution)/shard_map/ppermute | solution.py:37
  82.8 3.7 %collective-permute-start.12 = (f32[128,128]{1,0:T(8,128)S(1)}, f32[128,128]{1,0:T(8,128)S(1)}, u32[]{:S(2)}, u32[]{:S(2)}) collective-permute-start(f32[128,128]{1,0:T(8,128)S(1)} %divide_subtract_fusion.2.refs_0_), channel_id=1, source_target_pairs={{0,32},{32,0},{1,33},{33,1},{2,34},{34,2},{3,35},{35,3},{4,36},{36... | collective-permute-start | bytes 196616 | tf_op jit(solution)/shard_map/ppermute | solution.py:37
  99.3 5.2 %collective-permute-start.13 = (f32[128,128]{1,0:T(8,128)S(1)}, f32[128,128]{1,0:T(8,128)S(1)}, u32[]{:S(2)}, u32[]{:S(2)}) collective-permute-start(f32[128,128]{1,0:T(8,128)S(1)} %divide_subtract_fusion.1.refs_0_), channel_id=1, source_target_pairs={{0,96},{32,64},{64,32},{96,0},{1,97},{33,65},{65,33},{97,1},{2,98}... | collective-permute-start | bytes 196616 | tf_op jit(solution)/shard_map/ppermute | solution.py:41
  101.9 4.1 %collective-permute-start.14 = (f32[128,128]{1,0:T(8,128)S(1)}, f32[128,128]{1,0:T(8,128)S(1)}, u32[]{:S(2)}, u32[]{:S(2)}) collective-permute-start(f32[128,128]{1,0:T(8,128)S(1)} %divide_subtract_fusion.1.refs_0_), channel_id=1, source_target_pairs={{0,64},{64,0},{1,65},{65,1},{2,66},{66,2},{3,67},{67,3},{4,68},{68... | collective-permute-start | bytes 196616 | tf_op jit(solution)/shard_map/ppermute | solution.py:37
  102.7 3.3 %collective-permute-start.15 = (f32[128,128]{1,0:T(8,128)S(1)}, f32[128,128]{1,0:T(8,128)S(1)}, u32[]{:S(2)}, u32[]{:S(2)}) collective-permute-start(f32[128,128]{1,0:T(8,128)S(1)} %divide_subtract_fusion.1.refs_0_), channel_id=1, source_target_pairs={{0,32},{32,0},{1,33},{33,1},{2,34},{34,2},{3,35},{35,3},{4,36},{36... | collective-permute-start | bytes 196616 | tf_op jit(solution)/shard_map/ppermute | solution.py:37
  108.2 12.0 %all-to-all-start.4 = ((f32[8,128,128]{2,1,0:T(8,128)}), f32[8,128,128]{2,1,0:T(8,128)S(1)}, u32[]{:S(2)}, u32[]{:S(2)}) async-start(f32[8,128,128]{2,1,0:T(8,128)} %product.11), calls=%async_computation.4 | async-start | bytes 1048576 | tf_op jit(solution)/shard_map/all_to_all | solution.py:47
  111.7 11.8 %collective-permute-start.19 = (f32[128,128]{1,0:T(8,128)S(1)}, f32[128,128]{1,0:T(8,128)S(1)}, u32[]{:S(2)}, u32[]{:S(2)}) collective-permute-start(f32[128,128]{1,0:T(8,128)S(1)} %divide_subtract_fusion.1.refs_0_), channel_id=1, source_target_pairs={{0,5},{1,4},{4,1},{5,0},{2,7},{3,6},{6,3},{7,2},{8,13},{9,12},{12,... | collective-permute-start | bytes 196616 | tf_op jit(solution)/shard_map/ppermute | solution.py:41
  114.9 9.3 %collective-permute-start.20 = (f32[128,128]{1,0:T(8,128)S(1)}, f32[128,128]{1,0:T(8,128)S(1)}, u32[]{:S(2)}, u32[]{:S(2)}) collective-permute-start(f32[128,128]{1,0:T(8,128)S(1)} %divide_subtract_fusion.1.refs_0_), channel_id=1, source_target_pairs={{0,4},{4,0},{1,5},{5,1},{2,6},{6,2},{3,7},{7,3},{8,12},{12,8},{9,1... | collective-permute-start | bytes 196616 | tf_op jit(solution)/shard_map/ppermute | solution.py:37
  115.5 8.7 %collective-permute-start.21 = (f32[128,128]{1,0:T(8,128)S(1)}, f32[128,128]{1,0:T(8,128)S(1)}, u32[]{:S(2)}, u32[]{:S(2)}) collective-permute-start(f32[128,128]{1,0:T(8,128)S(1)} %divide_subtract_fusion.1.refs_0_), channel_id=1, source_target_pairs={{0,1},{1,0},{2,3},{3,2},{4,5},{5,4},{6,7},{7,6},{8,9},{9,8},{10,11... | collective-permute-start | bytes 196616 | tf_op jit(solution)/shard_map/ppermute | solution.py:37
  120.2 5.2 %collective-permute-start.16 = (f32[128,128]{1,0:T(8,128)S(1)}, f32[128,128]{1,0:T(8,128)S(1)}, u32[]{:S(2)}, u32[]{:S(2)}) collective-permute-start(f32[128,128]{1,0:T(8,128)S(1)} %subtract_divide_fusion.refs_0_), channel_id=1, source_target_pairs={{0,96},{32,64},{64,32},{96,0},{1,97},{33,65},{65,33},{97,1},{2,98}... | collective-permute-start | bytes 196616 | tf_op jit(solution)/shard_map/ppermute | solution.py:41
  122.8 4.1 %collective-permute-start.17 = (f32[128,128]{1,0:T(8,128)S(1)}, f32[128,128]{1,0:T(8,128)S(1)}, u32[]{:S(2)}, u32[]{:S(2)}) collective-permute-start(f32[128,128]{1,0:T(8,128)S(1)} %subtract_divide_fusion.refs_0_), channel_id=1, source_target_pairs={{0,64},{64,0},{1,65},{65,1},{2,66},{66,2},{3,67},{67,3},{4,68},{68... | collective-permute-start | bytes 196616 | tf_op jit(solution)/shard_map/ppermute | solution.py:37
  123.5 3.4 %collective-permute-start.18 = (f32[128,128]{1,0:T(8,128)S(1)}, f32[128,128]{1,0:T(8,128)S(1)}, u32[]{:S(2)}, u32[]{:S(2)}) collective-permute-start(f32[128,128]{1,0:T(8,128)S(1)} %subtract_divide_fusion.refs_0_), channel_id=1, source_target_pairs={{0,32},{32,0},{1,33},{33,1},{2,34},{34,2},{3,35},{35,3},{4,36},{36... | collective-permute-start | bytes 196616 | tf_op jit(solution)/shard_map/ppermute | solution.py:37
  142.1 5.3 %collective-permute-start.22 = (f32[144,128]{1,0:T(8,128)S(1)}, f32[144,128]{1,0:T(8,128)S(1)}, u32[]{:S(2)}, u32[]{:S(2)}) collective-permute-start(f32[144,128]{1,0:T(8,128)S(1)} %pad_maximum_fusion.refs_0_), channel_id=1, source_target_pairs={{0,96},{32,64},{64,32},{96,0},{1,97},{33,65},{65,33},{97,1},{2,98}... | collective-permute-start | bytes 221192 | tf_op jit(solution)/shard_map/ppermute | solution.py:41
  144.6 4.4 %collective-permute-start.23 = (f32[144,128]{1,0:T(8,128)S(1)}, f32[144,128]{1,0:T(8,128)S(1)}, u32[]{:S(2)}, u32[]{:S(2)}) collective-permute-start(f32[144,128]{1,0:T(8,128)S(1)} %pad_maximum_fusion.refs_0_), channel_id=1, source_target_pairs={{0,64},{64,0},{1,65},{65,1},{2,66},{66,2},{3,67},{67,3},{4,68},{68... | collective-permute-start | bytes 221192 | tf_op jit(solution)/shard_map/ppermute | solution.py:37
  145.3 3.7 %collective-permute-start.24 = (f32[144,128]{1,0:T(8,128)S(1)}, f32[144,128]{1,0:T(8,128)S(1)}, u32[]{:S(2)}, u32[]{:S(2)}) collective-permute-start(f32[144,128]{1,0:T(8,128)S(1)} %pad_maximum_fusion.refs_0_), channel_id=1, source_target_pairs={{0,32},{32,0},{1,33},{33,1},{2,34},{34,2},{3,35},{35,3},{4,36},{36... | collective-permute-start | bytes 221192 | tf_op jit(solution)/shard_map/ppermute | solution.py:37
  162.8 9.6 %collective-permute-start.25 = (f32[128,128]{1,0:T(8,128)S(1)}, f32[128,128]{1,0:T(8,128)S(1)}, u32[]{:S(2)}, u32[]{:S(2)}) collective-permute-start(f32[128,128]{1,0:T(8,128)S(1)} %divide_subtract_fusion.refs_0_), channel_id=1, source_target_pairs={{0,5},{1,4},{4,1},{5,0},{2,7},{3,6},{6,3},{7,2},{8,13},{9,12},{12,... | collective-permute-start | bytes 196616 | tf_op jit(solution)/shard_map/ppermute | solution.py:41
  165.9 6.6 %collective-permute-start.26 = (f32[128,128]{1,0:T(8,128)S(1)}, f32[128,128]{1,0:T(8,128)S(1)}, u32[]{:S(2)}, u32[]{:S(2)}) collective-permute-start(f32[128,128]{1,0:T(8,128)S(1)} %divide_subtract_fusion.refs_0_), channel_id=1, source_target_pairs={{0,4},{4,0},{1,5},{5,1},{2,6},{6,2},{3,7},{7,3},{8,12},{12,8},{9,1... | collective-permute-start | bytes 196616 | tf_op jit(solution)/shard_map/ppermute | solution.py:37
  167.3 5.4 %collective-permute-start.27 = (f32[128,128]{1,0:T(8,128)S(1)}, f32[128,128]{1,0:T(8,128)S(1)}, u32[]{:S(2)}, u32[]{:S(2)}) collective-permute-start(f32[128,128]{1,0:T(8,128)S(1)} %divide_subtract_fusion.refs_0_), channel_id=1, source_target_pairs={{0,1},{1,0},{2,3},{3,2},{4,5},{5,4},{6,7},{7,6},{8,9},{9,8},{10,11... | collective-permute-start | bytes 196616 | tf_op jit(solution)/shard_map/ppermute | solution.py:37
  173.6 4.8 %collective-permute-start.28 = (f32[72,128]{1,0:T(8,128)S(1)}, f32[72,128]{1,0:T(8,128)S(1)}, u32[]{:S(2)}, u32[]{:S(2)}) collective-permute-start(f32[72,128]{1,0:T(8,128)S(1)} %get-tuple-element.31), channel_id=1, source_target_pairs={{0,96},{32,64},{64,32},{96,0},{1,97},{33,65},{65,33},{97,1},{2,98}... | collective-permute-start | bytes 110600 | tf_op jit(solution)/shard_map/ppermute | solution.py:41
  176.7 3.3 %collective-permute-start.29 = (f32[72,128]{1,0:T(8,128)S(1)}, f32[72,128]{1,0:T(8,128)S(1)}, u32[]{:S(2)}, u32[]{:S(2)}) collective-permute-start(f32[72,128]{1,0:T(8,128)S(1)} %get-tuple-element.31), channel_id=1, source_target_pairs={{0,64},{64,0},{1,65},{65,1},{2,66},{66,2},{3,67},{67,3},{4,68},{68... | collective-permute-start | bytes 110600 | tf_op jit(solution)/shard_map/ppermute | solution.py:37
  (9 other events, 43.8 us)
